TPU v7x, 256 devices: a whole 4x4x8 slice. The times are simulated.
256 devices in a mesh: ctx: 256 (over x, y, z, core).
Axes of the slice: x: 4, y: 4, z: 8, core: 2. Of those that a mesh axis runs over, the one named last changes fastest.
Arguments:
- queries: bfloat16 [131072, 1024], P('ctx'), may hold values from -6 to 6
- keys: bfloat16 [131072, 1024], P('ctx'), may hold values from -6 to 6
- values: bfloat16 [131072, 1024], P('ctx'), may hold values from -6 to 6
- out_grad: bfloat16 [131072, 1024], P('ctx'), may hold values from -6 to 6
Outputs:
- attended: bfloat16 [131072, 1024], P('ctx')
- query_grad: float32 [131072, 1024], P('ctx')
- key_grad: float32 [131072, 1024], P('ctx')
- value_grad: float32 [131072, 1024], P('ctx')
All inputs are finite; a program needn't handle non-finite values.
Results may differ from a plain program's by a relative error of at most 0.011.
Values may be sent and summed in bfloat16 or wider, within the bound.
No kernel may reach another device: no remote copies, remote signals or barrier semaphores. Data moves between devices by JAX's collectives and lax.ppermute only.
A program may use at most 128 MiB of HBM per device.

v0:
```python
import math

import jax
import jax.numpy as jnp
from jax import lax
from jax.sharding import PartitionSpec as P

H = 8
HD = 128
NB = 128
LEVELS = 4


LN_TWO = math.log(2.0)


def from_partner(value, axis, stride):
    mask = 2**stride
    pairs = [(source, source ^ mask) for source in range(lax.axis_size(axis))]
    return lax.ppermute(value, axis, pairs)


def as_sent(array):
    return jax.tree.map(lambda a: a.astype(jnp.bfloat16) if a.dtype == jnp.float32 else a, array)


def extended(cells, sides, width):
    for axis, dim in sides:
        count = lax.axis_size(axis)
        ends = count - 1
        head = lax.slice_in_dim(cells, 0, width, axis=dim)
        tail = lax.slice_in_dim(cells, cells.shape[dim] - width, cells.shape[dim], axis=dim)
        cells = jnp.concatenate(
            [
                lax.ppermute(tail, axis, [(i, (i + 1) % count) for i in range(ends)]),
                cells,
                lax.ppermute(head, axis, [((i + 1) % count, i) for i in range(ends)]),
            ],
            axis=dim,
        )
    return cells


def shifted(array, axis, by):
    count = lax.axis_size(axis)
    pairs = [(i, i + by) for i in range(count) if 0 <= i + by < count]
    return lax.ppermute(array, axis, pairs)


def ordered(own_rows, partner, position, bit_no):
    upper_half = position >> bit_no & 1
    return jnp.where(
        upper_half == 0,
        jnp.concatenate([own_rows, partner], axis=1),
        jnp.concatenate([partner, own_rows], axis=1),
    )


def split_half(buffer, position, bit_no):
    half_rows = buffer.shape[1] // 2
    lower_rows = buffer[:, :half_rows]
    higher = buffer[:, half_rows:]
    upper_half = position >> bit_no & 1
    return (
        jnp.where(upper_half == 0, lower_rows, higher),
        jnp.where(upper_half == 0, higher, lower_rows),
    )


def gather_groups(buffers, position):
    buffers = list(buffers)
    partner = from_partner(buffers[0], "ctx", 0)
    buffers[0] = ordered(buffers[0], partner, position, 0)
    return buffers


def halve_groups(buffers, depths, position):
    buffers = list(buffers)
    for bit_no in reversed(range(depths[0])):
        kept_half, sent_half = split_half(buffers[0], position, bit_no)
        received = from_partner(as_sent(sent_half), "ctx", bit_no).astype(sent_half.dtype)
        buffers[0] = kept_half + received
    return buffers


def spread_rows(owned, factor):
    scaled = owned / factor
    pairs, row_count, features = scaled.shape
    widened = jnp.broadcast_to(scaled[:, :, None, :], (pairs, row_count, factor, features))
    return widened.reshape(pairs, row_count * factor, features)


def body(queries, keys, values, out_grad):
    tok_rows, features = queries.shape
    devices = lax.axis_size("ctx")
    position = lax.axis_index("ctx")
    first_tok = position * tok_rows
    seq_total = tok_rows * devices
    blocks = tok_rows // NB
    score_scale = 1.0 / math.sqrt(HD)
    keys_values = jnp.stack([keys, values])
    pooled_list = []
    for level_id in range(LEVELS):
        factor = 2**level_id
        if level_id == 0:
            pooled_list.append(keys_values)
        else:
            grouped_rows = keys_values.astype(jnp.float32).reshape(
                2, tok_rows // factor, factor, features
            )
            pooled_list.append(jnp.mean(grouped_rows, axis=2).astype(jnp.bfloat16))
    near_ids = [level_id for level_id in range(LEVELS) if NB * 2**level_id <= tok_rows]
    far_ids = [level_id for level_id in range(LEVELS) if NB * 2**level_id > tok_rows]
    groups = [NB * 2**level_id // tok_rows for level_id in far_ids]
    depths = [member.bit_length() - 1 for member in groups]
    widened = {}
    for level_id in near_ids:
        widened[level_id] = extended(pooled_list[level_id], (("ctx", 1),), NB)
    grouped = gather_groups([pooled_list[level_id] for level_id in far_ids], position)
    slot_id = 0
    left_sets = [shifted(grouped[slot_id], "ctx", groups[slot_id])]
    right_sets = [shifted(grouped[slot_id], "ctx", -groups[slot_id])]
    sources = []
    for level_id in range(LEVELS):
        if level_id in widened:
            sources.append(widened[level_id])
        else:
            slot_id = far_ids.index(level_id)
            sources.append(jnp.concatenate([left_sets[slot_id], right_sets[slot_id]], axis=1))
    bias_rows = []
    for block_id in range(blocks):
        block_first = first_tok + block_id * NB
        bias_parts = []
        for level_id in range(LEVELS):
            factor = 2**level_id
            span_tok = NB * factor
            local_rows = tok_rows // factor
            if level_id in widened:
                local_sup = block_id * NB // span_tok
                key_index = (
                    position * local_rows
                    - NB
                    + local_sup * NB
                    + jnp.arange(3 * NB, dtype=jnp.int32)
                )
            else:
                super_no = first_tok // span_tok
                key_index = jnp.concatenate(
                    [
                        (super_no - 1) * NB + jnp.arange(NB, dtype=jnp.int32),
                        (super_no + 1) * NB + jnp.arange(NB, dtype=jnp.int32),
                    ]
                )
            admitted = (key_index >= 0) & (key_index < seq_total // factor)
            if level_id > 0:
                child_block = block_first // (span_tok // 2)
                admitted = admitted & (jnp.abs(key_index // (NB // 2) - child_block) > 1)
            bias_parts.append(
                jnp.where(admitted, jnp.float32(level_id * LN_TWO), jnp.float32(-jnp.inf))
            )
        bias_rows.append(jnp.concatenate(bias_parts))
    key_bias = jnp.stack(bias_rows)
    q_blocks = queries.reshape(blocks, NB, features)
    g_blocks = out_grad.reshape(blocks, NB, features)
    grad_shapes = [(2, source.shape[1], features) for source in sources]

    def per_head(head_id, carry):
        attended, query_grad, level_grads = carry
        lane_start = head_id * HD
        head_lanes = [lax.dynamic_slice_in_dim(source, lane_start, HD, 2) for source in sources]
        block_sets = []
        for block_id in range(blocks):
            key_parts = []
            for level_id in range(LEVELS):
                if level_id in widened:
                    local_sup = block_id * NB // (NB * 2**level_id)
                    key_parts.append(
                        head_lanes[level_id][:, local_sup * NB : local_sup * NB + 3 * NB]
                    )
                else:
                    key_parts.append(head_lanes[level_id])
            block_sets.append(jnp.concatenate(key_parts, axis=1))
        key_sets = jnp.stack(block_sets, axis=1)
        head_key_rows = key_sets[0]
        head_value_rows = key_sets[1]
        head_query_rows = lax.dynamic_slice_in_dim(q_blocks, lane_start, HD, 2)
        output_head_gradient = lax.dynamic_slice_in_dim(g_blocks, lane_start, HD, 2)
        scores = (
            jnp.einsum(
                "gte,gve->gtv", head_query_rows, head_key_rows, preferred_element_type=jnp.float32
            )
            * score_scale
            + key_bias[:, None, :]
        )
        row_max = jnp.max(scores, axis=-1, keepdims=True)
        exp_terms = jnp.exp(scores - row_max)
        prob_f32 = exp_terms / jnp.sum(exp_terms, axis=-1, keepdims=True)
        attention_weight = prob_f32.astype(jnp.bfloat16)
        out_head = jnp.einsum(
            "fow,fwn->fon", attention_weight, head_value_rows, preferred_element_type=jnp.float32
        ).astype(jnp.bfloat16)
        probability_gradient = jnp.einsum(
            "gte,gve->gtv",
            output_head_gradient,
            head_value_rows,
            preferred_element_type=jnp.float32,
        )
        row_delta = jnp.sum(prob_f32 * probability_gradient, axis=-1, keepdims=True)
        logit_gradient = (prob_f32 * (probability_gradient - row_delta) * score_scale).astype(
            jnp.bfloat16
        )
        query_head_gradient = jnp.einsum(
            "fow,fwn->fon", logit_gradient, head_key_rows, preferred_element_type=jnp.float32
        )
        key_head_gradient = jnp.einsum(
            "sme,smy->sey", logit_gradient, head_query_rows, preferred_element_type=jnp.float32
        )
        value_head_gradient = jnp.einsum(
            "sme,smy->sey",
            attention_weight,
            output_head_gradient,
            preferred_element_type=jnp.float32,
        )
        key_grads = jnp.stack([key_head_gradient, value_head_gradient])
        attended = lax.dynamic_update_slice_in_dim(attended, out_head, lane_start, 2)
        query_grad = lax.dynamic_update_slice_in_dim(query_grad, query_head_gradient, lane_start, 2)
        new_grads = []
        offset = 0
        for level_id in range(LEVELS):
            if level_id in widened:
                grad_piece = jnp.zeros((2, grad_shapes[level_id][1], HD), jnp.float32)
                for block_id in range(blocks):
                    local_sup = block_id * NB // (NB * 2**level_id)
                    grad_piece = grad_piece.at[:, local_sup * NB : local_sup * NB + 3 * NB].add(
                        key_grads[:, block_id, offset : offset + 3 * NB]
                    )
                offset += 3 * NB
            else:
                grad_piece = jnp.sum(key_grads[:, :, offset : offset + 2 * NB], axis=1)
                offset += 2 * NB
            new_grads.append(
                lax.dynamic_update_slice_in_dim(level_grads[level_id], grad_piece, lane_start, 2)
            )
        return (attended, query_grad, tuple(new_grads))

    initial = (
        jnp.zeros((blocks, NB, features), jnp.bfloat16),
        jnp.zeros((blocks, NB, features), jnp.float32),
        tuple((jnp.zeros(shape_of, jnp.float32) for shape_of in grad_shapes)),
    )
    attended, query_grad, level_grads = lax.fori_loop(0, H, per_head, initial)
    token_grad = jnp.zeros((2, tok_rows, features), jnp.float32)
    far_left = []
    far_right = []
    for level_id in range(LEVELS):
        if level_id in widened:
            local_rows = tok_rows // 2**level_id
            ext_grad = level_grads[level_id]
            owned = ext_grad[:, NB : NB + local_rows]
            from_above = shifted(ext_grad[:, :NB].astype(jnp.bfloat16), "ctx", -1).astype(
                jnp.float32
            )
            from_below = shifted(
                ext_grad[:, local_rows + NB :].astype(jnp.bfloat16), "ctx", 1
            ).astype(jnp.float32)
            owned = owned.at[:, local_rows - NB :].add(from_above)
            owned = owned.at[:, :NB].add(from_below)
            token_grad = token_grad + spread_rows(owned, 2**level_id)
        else:
            far_left.append(level_grads[level_id][:, :NB])
            far_right.append(level_grads[level_id][:, NB:])
    slot_id = 0
    back_left = shifted(far_left[slot_id].astype(jnp.bfloat16), "ctx", -groups[slot_id]).astype(
        jnp.float32
    )
    back_right = shifted(far_right[slot_id].astype(jnp.bfloat16), "ctx", groups[slot_id]).astype(
        jnp.float32
    )
    incoming = [back_left + back_right]
    owned_list = halve_groups(incoming, depths, position)
    for slot_id, level_id in enumerate(far_ids):
        token_grad = token_grad + spread_rows(owned_list[slot_id], 2**level_id)
    return (
        attended.reshape(tok_rows, features),
        query_grad.reshape(tok_rows, features),
        token_grad[0],
        token_grad[1],
    )


def solution(mesh):
    placed = (P("ctx", None), P("ctx", None), P("ctx", None), P("ctx", None))
    return jax.shard_map(
        body,
        mesh=mesh,
        in_specs=placed,
        out_specs=(P("ctx", None), P("ctx", None), P("ctx", None), P("ctx", None)),
        check_vma=False,
    )
```

profile of v0, /device:TPU:6, one launch (start us, length us, event | category | flops | bytes accessed | tf_op | source)
XLA Modules:
  0.0 453.5 jit_solution(14813657674517216900)
XLA Ops:
  4.3 4.3 convert_reduce_fusion.1
  9.6 9.9 %collective-permute-start.5 = (bf16[2,128,1024]{2,1,0:T(8,128)(2,1)}, bf16[2,128,1024]{2,1,0:T(8,128)(2,1)}, u32[]{:S(2)}, u32[]{:S(2)}) collective-permute-start(bf16[2,128,1024]{2,1,0:T(8,128)(2,1)} %multiply_convert_fusion.1), channel_id=1, source_target_pairs={{1,0},{2,1},{3,2},{4,3},{5,4},{6,5},{7,6},{8,7},{9,8},{10,9},{11,1... | collective-permute-start | bytes 1572872 | tf_op jit(solution)/shard_map/ppermute | solution.py:37
  24.9 7.2 %convert_reduce_fusion.2 = f32[2,256,1024]{2,1,0:T(8,128)S(1)} fusion(bf16[1,256,2,1024]{3,2,1,0:T(2,128)(2,1)} %stack.134, bf16[1,256,2,1024]{3,2,1,0:T(2,128)(2,1)S(1)} %stack.133), kind=kLoop, calls=%fused_computation.101 | loop fusion | flops 2621440 | bytes 4194304 | tf_op jit(solution)/shard_map/reduce_sum | solution.py:111
  35.7 7.4 %collective-permute-start.3 = (bf16[2,128,1024]{2,1,0:T(8,128)(2,1)}, bf16[2,128,1024]{2,1,0:T(8,128)(2,1)}, u32[]{:S(2)}, u32[]{:S(2)}) collective-permute-start(bf16[2,128,1024]{2,1,0:T(8,128)(2,1)} %get-tuple-element.870), channel_id=1, source_target_pairs={{1,0},{2,1},{3,2},{4,3},{5,4},{6,5},{7,6},{8,7},{9,8},{10,9},{11,1... | collective-permute-start | bytes 1572872 | tf_op jit(solution)/shard_map/ppermute | solution.py:37
  46.5 7.9 %collective-permute-start.1 = (bf16[2,128,1024]{2,1,0:T(8,128)(2,1)}, bf16[2,128,1024]{2,1,0:T(8,128)(2,1)}, u32[]{:S(2)}, u32[]{:S(2)}) collective-permute-start(bf16[2,128,1024]{2,1,0:T(8,128)(2,1)} %get-tuple-element.864), channel_id=1, source_target_pairs={{1,0},{2,1},{3,2},{4,3},{5,4},{6,5},{7,6},{8,7},{9,8},{10,9},{11,1... | collective-permute-start | bytes 1572872 | tf_op jit(solution)/shard_map/ppermute | solution.py:37
  57.6 4.1 collective-permute-start.7
  72.5 5.1 %collective-permute-done.7 = bf16[2,128,1024]{2,1,0:T(8,128)(2,1)S(1)} collective-permute-done((bf16[2,128,1024]{2,1,0:T(8,128)(2,1)S(1)}, bf16[2,128,1024]{2,1,0:T(8,128)(2,1)S(1)}, u32[]{:S(2)}, u32[]{:S(2)}) %collective-permute-start.7) | collective-permute-done | bytes 524320 | tf_op jit(solution)/shard_map/ppermute | solution.py:47
  86.2 3.4 broadcast_in_dim.98
  89.6 284.9 %while.82 = (s32[]{:T(128)}, bf16[4,128,1024]{2,1,0:T(8,128)(2,1)}, f32[4,128,1024]{2,1,0:T(8,128)}, f32[2,768,1024]{2,1,0:T(8,128)}, f32[2,512,1024]{2,1,0:T(8,...) while((s32[]{:T(128)}, bf16[4,128,1024]{2,1,0:T(8,128)(2,1)}, ...), condition=%wide.region_8.9_spmd, body=%wide.region_3.8_spmd.sunk | while | flops 1139020928 | bytes 114921856 | solution.py:251
  93.1 3.1 fusion.154
  96.2 3.4 fusion.152
  102.7 7.6 %fusion.155 = f32[4,128,1024]{2,1,0:T(8,128)} fusion(f32[4,128,1024]{2,1,0:T(8,128)} %get-tuple-element.1033, s32[]{:T(128)S(6)} %select_n.242, bf16[2,4,1408,128]{3,2,1,0:T(8,128)(2,1)S(1)} %pad_maximum_fusion.26, f32[4,128,1408]{2,1,0:T(8,128)} %fusion.154, f32[4,128,1408]{2,1,0:T(8,128)} %get-tuple-element.999, f32[4,128]{1,0:T(4,128)S(1)} %get-tuple-element.1000), kind=kOutput, calls=%fused_computation.31.clone.1 | convolution fusion | flops 189597568 | bytes 13242372 | tf_op jit(solution)/shard_map/while/body/eval_jaxpr/fow,fwn->fon/dot_general | solution.py:212
  110.3 8.0 %convolution_bitcast_fusion.5 = f32[1,4,1408,128]{3,2,1,0:T(8,128)S(1)} fusion(f32[4,128,1408]{2,1,0:T(8,128)} %fusion.154, bf16[4,128,1024]{2,1,0:T(8,128)(2,1)} %get-tuple-element.1060, s32[]{:T(128)S(6)} %select_n.242, f32[4,128,1408]{2,1,0:T(8,128)} %get-tuple-element.999, f32[4,128]{1,0:T(4,128)S(1)} %get-tuple-element.1000), kind=kOutput, calls=%fused_computation.10.clone.1 | convolution fusion | flops 189597568 | bytes 14553092 | tf_op jit(solution)/shard_map/while/body/eval_jaxpr/sme,smy->sey/dot_general | solution.py:215
  128.7 3.1 fusion.154
  131.8 3.4 fusion.152
  138.3 7.6 %fusion.155 = f32[4,128,1024]{2,1,0:T(8,128)} fusion(f32[4,128,1024]{2,1,0:T(8,128)} %get-tuple-element.1033, s32[]{:T(128)S(6)} %select_n.242, bf16[2,4,1408,128]{3,2,1,0:T(8,128)(2,1)S(1)} %pad_maximum_fusion.26, f32[4,128,1408]{2,1,0:T(8,128)} %fusion.154, f32[4,128,1408]{2,1,0:T(8,128)} %get-tuple-element.999, f32[4,128]{1,0:T(4,128)S(1)} %get-tuple-element.1000), kind=kOutput, calls=%fused_computation.31.clone.1 | convolution fusion | flops 189597568 | bytes 13242372 | tf_op jit(solution)/shard_map/while/body/eval_jaxpr/fow,fwn->fon/dot_general | solution.py:212
  145.9 8.0 %convolution_bitcast_fusion.5 = f32[1,4,1408,128]{3,2,1,0:T(8,128)S(1)} fusion(f32[4,128,1408]{2,1,0:T(8,128)} %fusion.154, bf16[4,128,1024]{2,1,0:T(8,128)(2,1)} %get-tuple-element.1060, s32[]{:T(128)S(6)} %select_n.242, f32[4,128,1408]{2,1,0:T(8,128)} %get-tuple-element.999, f32[4,128]{1,0:T(4,128)S(1)} %get-tuple-element.1000), kind=kOutput, calls=%fused_computation.10.clone.1 | convolution fusion | flops 189597568 | bytes 14553092 | tf_op jit(solution)/shard_map/while/body/eval_jaxpr/sme,smy->sey/dot_general | solution.py:215
  167.4 3.4 fusion.152
  173.9 7.6 %fusion.155 = f32[4,128,1024]{2,1,0:T(8,128)} fusion(f32[4,128,1024]{2,1,0:T(8,128)} %get-tuple-element.1033, s32[]{:T(128)S(6)} %select_n.242, bf16[2,4,1408,128]{3,2,1,0:T(8,128)(2,1)S(1)} %pad_maximum_fusion.26, f32[4,128,1408]{2,1,0:T(8,128)} %fusion.154, f32[4,128,1408]{2,1,0:T(8,128)} %get-tuple-element.999, f32[4,128]{1,0:T(4,128)S(1)} %get-tuple-element.1000), kind=kOutput, calls=%fused_computation.31.clone.1 | convolution fusion | flops 189597568 | bytes 13242372 | tf_op jit(solution)/shard_map/while/body/eval_jaxpr/fow,fwn->fon/dot_general | solution.py:212
  181.5 8.0 %convolution_bitcast_fusion.5 = f32[1,4,1408,128]{3,2,1,0:T(8,128)S(1)} fusion(f32[4,128,1408]{2,1,0:T(8,128)} %fusion.154, bf16[4,128,1024]{2,1,0:T(8,128)(2,1)} %get-tuple-element.1060, s32[]{:T(128)S(6)} %select_n.242, f32[4,128,1408]{2,1,0:T(8,128)} %get-tuple-element.999, f32[4,128]{1,0:T(4,128)S(1)} %get-tuple-element.1000), kind=kOutput, calls=%fused_computation.10.clone.1 | convolution fusion | flops 189597568 | bytes 14553092 | tf_op jit(solution)/shard_map/while/body/eval_jaxpr/sme,smy->sey/dot_general | solution.py:215
  203.0 3.4 fusion.152
  209.5 7.6 %fusion.155 = f32[4,128,1024]{2,1,0:T(8,128)} fusion(f32[4,128,1024]{2,1,0:T(8,128)} %get-tuple-element.1033, s32[]{:T(128)S(6)} %select_n.242, bf16[2,4,1408,128]{3,2,1,0:T(8,128)(2,1)S(1)} %pad_maximum_fusion.26, f32[4,128,1408]{2,1,0:T(8,128)} %fusion.154, f32[4,128,1408]{2,1,0:T(8,128)} %get-tuple-element.999, f32[4,128]{1,0:T(4,128)S(1)} %get-tuple-element.1000), kind=kOutput, calls=%fused_computation.31.clone.1 | convolution fusion | flops 189597568 | bytes 13242372 | tf_op jit(solution)/shard_map/while/body/eval_jaxpr/fow,fwn->fon/dot_general | solution.py:212
  217.1 8.0 %convolution_bitcast_fusion.5 = f32[1,4,1408,128]{3,2,1,0:T(8,128)S(1)} fusion(f32[4,128,1408]{2,1,0:T(8,128)} %fusion.154, bf16[4,128,1024]{2,1,0:T(8,128)(2,1)} %get-tuple-element.1060, s32[]{:T(128)S(6)} %select_n.242, f32[4,128,1408]{2,1,0:T(8,128)} %get-tuple-element.999, f32[4,128]{1,0:T(4,128)S(1)} %get-tuple-element.1000), kind=kOutput, calls=%fused_computation.10.clone.1 | convolution fusion | flops 189597568 | bytes 14553092 | tf_op jit(solution)/shard_map/while/body/eval_jaxpr/sme,smy->sey/dot_general | solution.py:215
  235.5 3.1 fusion.154
  238.6 3.4 fusion.152
  245.1 7.6 %fusion.155 = f32[4,128,1024]{2,1,0:T(8,128)} fusion(f32[4,128,1024]{2,1,0:T(8,128)} %get-tuple-element.1033, s32[]{:T(128)S(6)} %select_n.242, bf16[2,4,1408,128]{3,2,1,0:T(8,128)(2,1)S(1)} %pad_maximum_fusion.26, f32[4,128,1408]{2,1,0:T(8,128)} %fusion.154, f32[4,128,1408]{2,1,0:T(8,128)} %get-tuple-element.999, f32[4,128]{1,0:T(4,128)S(1)} %get-tuple-element.1000), kind=kOutput, calls=%fused_computation.31.clone.1 | convolution fusion | flops 189597568 | bytes 13242372 | tf_op jit(solution)/shard_map/while/body/eval_jaxpr/fow,fwn->fon/dot_general | solution.py:212
  252.7 8.0 %convolution_bitcast_fusion.5 = f32[1,4,1408,128]{3,2,1,0:T(8,128)S(1)} fusion(f32[4,128,1408]{2,1,0:T(8,128)} %fusion.154, bf16[4,128,1024]{2,1,0:T(8,128)(2,1)} %get-tuple-element.1060, s32[]{:T(128)S(6)} %select_n.242, f32[4,128,1408]{2,1,0:T(8,128)} %get-tuple-element.999, f32[4,128]{1,0:T(4,128)S(1)} %get-tuple-element.1000), kind=kOutput, calls=%fused_computation.10.clone.1 | convolution fusion | flops 189597568 | bytes 14553092 | tf_op jit(solution)/shard_map/while/body/eval_jaxpr/sme,smy->sey/dot_general | solution.py:215
  274.2 3.4 fusion.152
  280.7 7.6 %fusion.155 = f32[4,128,1024]{2,1,0:T(8,128)} fusion(f32[4,128,1024]{2,1,0:T(8,128)} %get-tuple-element.1033, s32[]{:T(128)S(6)} %select_n.242, bf16[2,4,1408,128]{3,2,1,0:T(8,128)(2,1)S(1)} %pad_maximum_fusion.26, f32[4,128,1408]{2,1,0:T(8,128)} %fusion.154, f32[4,128,1408]{2,1,0:T(8,128)} %get-tuple-element.999, f32[4,128]{1,0:T(4,128)S(1)} %get-tuple-element.1000), kind=kOutput, calls=%fused_computation.31.clone.1 | convolution fusion | flops 189597568 | bytes 13242372 | tf_op jit(solution)/shard_map/while/body/eval_jaxpr/fow,fwn->fon/dot_general | solution.py:212
  288.3 8.0 %convolution_bitcast_fusion.5 = f32[1,4,1408,128]{3,2,1,0:T(8,128)S(1)} fusion(f32[4,128,1408]{2,1,0:T(8,128)} %fusion.154, bf16[4,128,1024]{2,1,0:T(8,128)(2,1)} %get-tuple-element.1060, s32[]{:T(128)S(6)} %select_n.242, f32[4,128,1408]{2,1,0:T(8,128)} %get-tuple-element.999, f32[4,128]{1,0:T(4,128)S(1)} %get-tuple-element.1000), kind=kOutput, calls=%fused_computation.10.clone.1 | convolution fusion | flops 189597568 | bytes 14553092 | tf_op jit(solution)/shard_map/while/body/eval_jaxpr/sme,smy->sey/dot_general | solution.py:215
  306.7 3.1 fusion.154
  309.8 3.4 fusion.152
  316.3 7.6 %fusion.155 = f32[4,128,1024]{2,1,0:T(8,128)} fusion(f32[4,128,1024]{2,1,0:T(8,128)} %get-tuple-element.1033, s32[]{:T(128)S(6)} %select_n.242, bf16[2,4,1408,128]{3,2,1,0:T(8,128)(2,1)S(1)} %pad_maximum_fusion.26, f32[4,128,1408]{2,1,0:T(8,128)} %fusion.154, f32[4,128,1408]{2,1,0:T(8,128)} %get-tuple-element.999, f32[4,128]{1,0:T(4,128)S(1)} %get-tuple-element.1000), kind=kOutput, calls=%fused_computation.31.clone.1 | convolution fusion | flops 189597568 | bytes 13242372 | tf_op jit(solution)/shard_map/while/body/eval_jaxpr/fow,fwn->fon/dot_general | solution.py:212
  323.9 8.0 %convolution_bitcast_fusion.5 = f32[1,4,1408,128]{3,2,1,0:T(8,128)S(1)} fusion(f32[4,128,1408]{2,1,0:T(8,128)} %fusion.154, bf16[4,128,1024]{2,1,0:T(8,128)(2,1)} %get-tuple-element.1060, s32[]{:T(128)S(6)} %select_n.242, f32[4,128,1408]{2,1,0:T(8,128)} %get-tuple-element.999, f32[4,128]{1,0:T(4,128)S(1)} %get-tuple-element.1000), kind=kOutput, calls=%fused_computation.10.clone.1 | convolution fusion | flops 189597568 | bytes 14553092 | tf_op jit(solution)/shard_map/while/body/eval_jaxpr/sme,smy->sey/dot_general | solution.py:215
  342.4 3.1 fusion.154
  345.5 3.4 fusion.152
  351.9 7.6 %fusion.155 = f32[4,128,1024]{2,1,0:T(8,128)} fusion(f32[4,128,1024]{2,1,0:T(8,128)} %get-tuple-element.1033, s32[]{:T(128)S(6)} %select_n.242, bf16[2,4,1408,128]{3,2,1,0:T(8,128)(2,1)S(1)} %pad_maximum_fusion.26, f32[4,128,1408]{2,1,0:T(8,128)} %fusion.154, f32[4,128,1408]{2,1,0:T(8,128)} %get-tuple-element.999, f32[4,128]{1,0:T(4,128)S(1)} %get-tuple-element.1000), kind=kOutput, calls=%fused_computation.31.clone.1 | convolution fusion | flops 189597568 | bytes 13242372 | tf_op jit(solution)/shard_map/while/body/eval_jaxpr/fow,fwn->fon/dot_general | solution.py:212
  359.6 8.0 %convolution_bitcast_fusion.5 = f32[1,4,1408,128]{3,2,1,0:T(8,128)S(1)} fusion(f32[4,128,1408]{2,1,0:T(8,128)} %fusion.154, bf16[4,128,1024]{2,1,0:T(8,128)(2,1)} %get-tuple-element.1060, s32[]{:T(128)S(6)} %select_n.242, f32[4,128,1408]{2,1,0:T(8,128)} %get-tuple-element.999, f32[4,128]{1,0:T(4,128)S(1)} %get-tuple-element.1000), kind=kOutput, calls=%fused_computation.10.clone.1 | convolution fusion | flops 189597568 | bytes 14553092 | tf_op jit(solution)/shard_map/while/body/eval_jaxpr/sme,smy->sey/dot_general | solution.py:215
  377.8 3.7 collective-permute-start.15
  385.2 4.9 %collective-permute-start.13 = (bf16[2,128,1024]{2,1,0:T(8,128)(2,1)}, bf16[2,128,1024]{2,1,0:T(8,128)(2,1)}, u32[]{:S(2)}, u32[]{:S(2)}) collective-permute-start(bf16[2,128,1024]{2,1,0:T(8,128)(2,1)} %get-tuple-element.865), channel_id=1, source_target_pairs={{1,0},{2,1},{3,2},{4,3},{5,4},{6,5},{7,6},{8,7},{9,8},{10,9},{11,1... | collective-permute-start | bytes 1572872 | tf_op jit(solution)/shard_map/ppermute | solution.py:47
  390.2 4.8 %collective-permute-start.11 = (bf16[2,128,1024]{2,1,0:T(8,128)(2,1)S(1)}, bf16[2,128,1024]{2,1,0:T(8,128)(2,1)S(1)}, u32[]{:S(2)}, u32[]{:S(2)}) collective-permute-start(bf16[2,128,1024]{2,1,0:T(8,128)(2,1)S(1)} %get-tuple-element.862), channel_id=1, source_target_pairs={{1,0},{2,1},{3,2},{4,3},{5,4},{6,5},{7,6},{8,7},{9,8},{10,9},{11,1... | collective-permute-start | bytes 1572872 | tf_op jit(solution)/shard_map/ppermute | solution.py:47
  405.3 7.9 %collective-permute-start.9 = (bf16[2,128,1024]{2,1,0:T(8,128)(2,1)}, bf16[2,128,1024]{2,1,0:T(8,128)(2,1)}, u32[]{:S(2)}, u32[]{:S(2)}) collective-permute-start(bf16[2,128,1024]{2,1,0:T(8,128)(2,1)} %get-tuple-element.860), channel_id=1, source_target_pairs={{1,0},{2,1},{3,2},{4,3},{5,4},{6,5},{7,6},{8,7},{9,8},{10,9},{11,1... | collective-permute-start | bytes 1572872 | tf_op jit(solution)/shard_map/ppermute | solution.py:47
  413.3 6.2 %collective-permute-done.12 = bf16[2,128,1024]{2,1,0:T(8,128)(2,1)S(1)} collective-permute-done((bf16[2,128,1024]{2,1,0:T(8,128)(2,1)S(1)}, bf16[2,128,1024]{2,1,0:T(8,128)(2,1)S(1)}, u32[]{:S(2)}, u32[]{:S(2)}) %collective-permute-start.12) | collective-permute-done | bytes 524320 | tf_op jit(solution)/shard_map/ppermute | solution.py:47
  420.0 3.4 broadcast_in_dim.108
  423.5 6.1 %reshape.883 = f32[2,512,1024]{2,1,0:T(8,128)} reshape(f32[2,256,2,1024]{3,2,1,0:T(2,128)} %broadcast_in_dim.108) | data formatting | bytes 8388608 | tf_op jit(solution)/shard_map/reshape | solution.py:90
  431.0 3.2 broadcast_in_dim.109
  434.2 5.3 %reshape.884 = f32[2,512,1024]{2,1,0:T(8,128)} reshape(f32[2,128,4,1024]{3,2,1,0:T(4,128)} %broadcast_in_dim.109) | data formatting | bytes 8388608 | tf_op jit(solution)/shard_map/reshape | solution.py:90
  446.0 5.2 %bitcast_add_fusion = f32[2,512,1024]{2,1,0:T(8,128)S(1)} fusion(f32[2,512,1024]{2,1,0:T(8,128)} %reshape.884, f32[2,512,1024]{2,1,0:T(8,128)} %fusion.66, f32[2,512,1024]{2,1,0:T(8,128)S(1)} %copy-done.4, f32[2,64,1024]{2,1,0:T(8,128)S(1)} %add_multiply_fusion.1), kind=kLoop, calls=%fused_computation.98 | loop fusion | flops 3145728 | bytes 17301504 | tf_op jit(solution)/shard_map/add | solution.py:282
  (293 shorter events, 183.7 us)
Async XLA Ops:
  4.3 17.1 %copy-start.1 = (bf16[512,1024]{1,0:T(8,128)(2,1)S(1)}, bf16[512,1024]{1,0:T(8,128)(2,1)}, u32[]{:S(2)}) copy-start(bf16[512,1024]{1,0:T(8,128)(2,1)} %param.56) | copy-start | bytes 3145732
  4.3 17.1 %copy-start.2 = (bf16[512,1024]{1,0:T(8,128)(2,1)S(1)}, bf16[512,1024]{1,0:T(8,128)(2,1)}, u32[]{:S(2)}) copy-start(bf16[512,1024]{1,0:T(8,128)(2,1)} %param.55) | copy-start | bytes 3145732
  9.6 37.0 %collective-permute-start.5 = (bf16[2,128,1024]{2,1,0:T(8,128)(2,1)}, bf16[2,128,1024]{2,1,0:T(8,128)(2,1)}, u32[]{:S(2)}, u32[]{:S(2)}) collective-permute-start(bf16[2,128,1024]{2,1,0:T(8,128)(2,1)} %multiply_convert_fusion.1), channel_id=1, source_target_pairs={{1,0},{2,1},{3,2},{4,3},{5,4},{6,5},{7,6},{8,7},{9,8},{10,9},{11,1... | collective-permute-start | bytes 1572872 | tf_op jit(solution)/shard_map/ppermute | solution.py:37
  19.5 36.2 %collective-permute-start.4 = (bf16[2,128,1024]{2,1,0:T(8,128)(2,1)}, bf16[2,128,1024]{2,1,0:T(8,128)(2,1)}, u32[]{:S(2)}, u32[]{:S(2)}) collective-permute-start(bf16[2,128,1024]{2,1,0:T(8,128)(2,1)} %multiply_convert_fusion.1), channel_id=1, source_target_pairs={{0,1},{1,2},{2,3},{3,4},{4,5},{5,6},{6,7},{7,8},{8,9},{9,10},{10,1... | collective-permute-start | bytes 1572872 | tf_op jit(solution)/shard_map/ppermute | solution.py:35
  22.9 21.7 %collective-permute-start.6 = (bf16[2,64,1024]{2,1,0:T(8,128)(2,1)S(1)}, bf16[2,64,1024]{2,1,0:T(8,128)(2,1)}, u32[]{:S(2)}, u32[]{:S(2)}) collective-permute-start(bf16[2,64,1024]{2,1,0:T(8,128)(2,1)S(1)} %multiply_convert_fusion.2), channel_id=1, source_target_pairs={{0,1},{1,0},{2,3},{3,2},{4,5},{5,4},{6,7},{7,6},{8,9},{9,8},{10,11... | collective-permute-start | bytes 786440 | tf_op jit(solution)/shard_map/ppermute | solution.py:20
  33.4 24.3 %collective-permute-start.2 = (bf16[2,128,1024]{2,1,0:T(8,128)(2,1)}, bf16[2,128,1024]{2,1,0:T(8,128)(2,1)}, u32[]{:S(2)}, u32[]{:S(2)}) collective-permute-start(bf16[2,128,1024]{2,1,0:T(8,128)(2,1)} %get-tuple-element.869), channel_id=1, source_target_pairs={{0,1},{1,2},{2,3},{3,4},{4,5},{5,6},{6,7},{7,8},{8,9},{9,10},{10,1... | collective-permute-start | bytes 1572872 | tf_op jit(solution)/shard_map/ppermute | solution.py:35
  35.7 28.7 %collective-permute-start.3 = (bf16[2,128,1024]{2,1,0:T(8,128)(2,1)}, bf16[2,128,1024]{2,1,0:T(8,128)(2,1)}, u32[]{:S(2)}, u32[]{:S(2)}) collective-permute-start(bf16[2,128,1024]{2,1,0:T(8,128)(2,1)} %get-tuple-element.870), channel_id=1, source_target_pairs={{1,0},{2,1},{3,2},{4,3},{5,4},{6,5},{7,6},{8,7},{9,8},{10,9},{11,1... | collective-permute-start | bytes 1572872 | tf_op jit(solution)/shard_map/ppermute | solution.py:37
  44.6 22.5 %collective-permute-start = (bf16[2,128,1024]{2,1,0:T(8,128)(2,1)}, bf16[2,128,1024]{2,1,0:T(8,128)(2,1)}, u32[]{:S(2)}, u32[]{:S(2)}) collective-permute-start(bf16[2,128,1024]{2,1,0:T(8,128)(2,1)} %get-tuple-element.863), channel_id=1, source_target_pairs={{0,1},{1,2},{2,3},{3,4},{4,5},{5,6},{6,7},{7,8},{8,9},{9,10},{10,1... | collective-permute-start | bytes 1572872 | tf_op jit(solution)/shard_map/ppermute | solution.py:35
  46.5 20.6 %collective-permute-start.1 = (bf16[2,128,1024]{2,1,0:T(8,128)(2,1)}, bf16[2,128,1024]{2,1,0:T(8,128)(2,1)}, u32[]{:S(2)}, u32[]{:S(2)}) collective-permute-start(bf16[2,128,1024]{2,1,0:T(8,128)(2,1)} %get-tuple-element.864), channel_id=1, source_target_pairs={{1,0},{2,1},{3,2},{4,3},{5,4},{6,5},{7,6},{8,7},{9,8},{10,9},{11,1... | collective-permute-start | bytes 1572872 | tf_op jit(solution)/shard_map/ppermute | solution.py:37
  55.7 16.9 %collective-permute-start.8 = (bf16[2,128,1024]{2,1,0:T(8,128)(2,1)S(1)}, bf16[2,128,1024]{2,1,0:T(8,128)(2,1)S(1)}, u32[]{:S(2)}, u32[]{:S(2)}) collective-permute-start(bf16[2,128,1024]{2,1,0:T(8,128)(2,1)S(1)} %maximum_select_fusion), channel_id=1, source_target_pairs={{2,0},{3,1},{4,2},{5,3},{6,4},{7,5},{8,6},{9,7},{10,8},{11,9},{12,... | collective-permute-start | bytes 1572872 | tf_op jit(solution)/shard_map/ppermute | solution.py:47
  57.6 20.1 %collective-permute-start.7 = (bf16[2,128,1024]{2,1,0:T(8,128)(2,1)S(1)}, bf16[2,128,1024]{2,1,0:T(8,128)(2,1)S(1)}, u32[]{:S(2)}, u32[]{:S(2)}) collective-permute-start(bf16[2,128,1024]{2,1,0:T(8,128)(2,1)S(1)} %maximum_select_fusion), channel_id=1, source_target_pairs={{0,2},{1,3},{2,4},{3,5},{4,6},{5,7},{6,8},{7,9},{8,10},{9,11},{10,... | collective-permute-start | bytes 1572872 | tf_op jit(solution)/shard_map/ppermute | solution.py:47
  89.6 3.1 copy-start.8
  122.6 2.6 copy-start.9
  125.2 3.1 copy-start.8
  158.2 2.6 copy-start.9
  160.8 3.1 copy-start.8
  193.8 2.6 copy-start.9
  196.4 3.1 copy-start.8
  229.5 2.5 copy-start.9
  232.0 3.1 copy-start.8
  265.0 2.6 copy-start.9
  267.6 3.1 copy-start.8
  300.6 2.6 copy-start.9
  303.2 3.1 copy-start.8
  336.3 2.5 copy-start.9
  338.8 3.1 copy-start.8
  371.9 2.6 copy-start.9
  374.5 2.8 copy-start
  374.5 3.1 copy-start.7
  377.3 6.5 %copy-start.3 = (f32[2,384,1024]{2,1,0:T(8,128)S(1)}, f32[2,384,1024]{2,1,0:T(8,128)}, u32[]{:S(2)}) copy-start(f32[2,384,1024]{2,1,0:T(8,128)} %get-tuple-element.799) | copy-start | bytes 9437188
  377.3 17.7 %slice-start = ((s8[6291456]{0:T(1024)(128)(4,1)}), s8[4194304]{0:T(1024)(128)(4,1)S(1)}, s32[]{:S(2)}) async-start(s8[6291456]{0:T(1024)(128)(4,1)} %bitcast.138), calls=%async_computation | async-start | bytes 8388608
  377.8 23.1 %collective-permute-start.15 = (bf16[2,128,1024]{2,1,0:T(8,128)(2,1)S(1)}, bf16[2,128,1024]{2,1,0:T(8,128)(2,1)S(1)}, u32[]{:S(2)}, u32[]{:S(2)}) collective-permute-start(bf16[2,128,1024]{2,1,0:T(8,128)(2,1)S(1)} %get-tuple-element.867), channel_id=1, source_target_pairs={{2,0},{3,1},{4,2},{5,3},{6,4},{7,5},{8,6},{9,7},{10,8},{11,9},{12,... | collective-permute-start | bytes 1572872 | tf_op jit(solution)/shard_map/ppermute | solution.py:47
  381.5 21.3 %collective-permute-start.16 = (bf16[2,128,1024]{2,1,0:T(8,128)(2,1)S(1)}, bf16[2,128,1024]{2,1,0:T(8,128)(2,1)S(1)}, u32[]{:S(2)}, u32[]{:S(2)}) collective-permute-start(bf16[2,128,1024]{2,1,0:T(8,128)(2,1)S(1)} %get-tuple-element.868), channel_id=1, source_target_pairs={{0,2},{1,3},{2,4},{3,5},{4,6},{5,7},{6,8},{7,9},{8,10},{9,11},{10,... | collective-permute-start | bytes 1572872 | tf_op jit(solution)/shard_map/ppermute | solution.py:47
  383.9 11.1 %slice-start.1 = ((s8[6291456]{0:T(1024)(128)(4,1)}), s8[2097152]{0:T(1024)(128)(4,1)S(1)}, s32[]{:S(2)}) async-start(s8[6291456]{0:T(1024)(128)(4,1)} %bitcast.138), calls=%async_computation.1 | async-start | bytes 4194304
  385.2 44.3 %collective-permute-start.13 = (bf16[2,128,1024]{2,1,0:T(8,128)(2,1)}, bf16[2,128,1024]{2,1,0:T(8,128)(2,1)}, u32[]{:S(2)}, u32[]{:S(2)}) collective-permute-start(bf16[2,128,1024]{2,1,0:T(8,128)(2,1)} %get-tuple-element.865), channel_id=1, source_target_pairs={{1,0},{2,1},{3,2},{4,3},{5,4},{6,5},{7,6},{8,7},{9,8},{10,9},{11,1... | collective-permute-start | bytes 1572872 | tf_op jit(solution)/shard_map/ppermute | solution.py:47
  390.2 15.1 %collective-permute-start.11 = (bf16[2,128,1024]{2,1,0:T(8,128)(2,1)S(1)}, bf16[2,128,1024]{2,1,0:T(8,128)(2,1)S(1)}, u32[]{:S(2)}, u32[]{:S(2)}) collective-permute-start(bf16[2,128,1024]{2,1,0:T(8,128)(2,1)S(1)} %get-tuple-element.862), channel_id=1, source_target_pairs={{1,0},{2,1},{3,2},{4,3},{5,4},{6,5},{7,6},{8,7},{9,8},{10,9},{11,1... | collective-permute-start | bytes 1572872 | tf_op jit(solution)/shard_map/ppermute | solution.py:47
  398.9 30.6 %collective-permute-start.14 = (bf16[2,128,1024]{2,1,0:T(8,128)(2,1)}, bf16[2,128,1024]{2,1,0:T(8,128)(2,1)}, u32[]{:S(2)}, u32[]{:S(2)}) collective-permute-start(bf16[2,128,1024]{2,1,0:T(8,128)(2,1)} %get-tuple-element.866), channel_id=1, source_target_pairs={{0,1},{1,2},{2,3},{3,4},{4,5},{5,6},{6,7},{7,8},{8,9},{9,10},{10,1... | collective-permute-start | bytes 1572872 | tf_op jit(solution)/shard_map/ppermute | solution.py:47
  400.9 18.6 %collective-permute-start.12 = (bf16[2,128,1024]{2,1,0:T(8,128)(2,1)S(1)}, bf16[2,128,1024]{2,1,0:T(8,128)(2,1)S(1)}, u32[]{:S(2)}, u32[]{:S(2)}) collective-permute-start(bf16[2,128,1024]{2,1,0:T(8,128)(2,1)S(1)} %get-tuple-element.861), channel_id=1, source_target_pairs={{0,1},{1,2},{2,3},{3,4},{4,5},{5,6},{6,7},{7,8},{8,9},{9,10},{10,1... | collective-permute-start | bytes 1572872 | tf_op jit(solution)/shard_map/ppermute | solution.py:47
  402.8 39.3 %collective-permute-start.10 = (bf16[2,128,1024]{2,1,0:T(8,128)(2,1)}, bf16[2,128,1024]{2,1,0:T(8,128)(2,1)}, u32[]{:S(2)}, u32[]{:S(2)}) collective-permute-start(bf16[2,128,1024]{2,1,0:T(8,128)(2,1)} %get-tuple-element.859), channel_id=1, source_target_pairs={{0,1},{1,2},{2,3},{3,4},{4,5},{5,6},{6,7},{7,8},{8,9},{9,10},{10,1... | collective-permute-start | bytes 1572872 | tf_op jit(solution)/shard_map/ppermute | solution.py:47
  405.2 14.6 %copy-start.5 = (f32[2,128,1024]{2,1,0:T(8,128)}, f32[2,128,1024]{2,1,0:T(8,128)S(1)}, u32[]{:S(2)}) copy-start(f32[2,128,1024]{2,1,0:T(8,128)S(1)} %convert_add_fusion) | copy-start | bytes 3145732
  405.3 34.2 %collective-permute-start.9 = (bf16[2,128,1024]{2,1,0:T(8,128)(2,1)}, bf16[2,128,1024]{2,1,0:T(8,128)(2,1)}, u32[]{:S(2)}, u32[]{:S(2)}) collective-permute-start(bf16[2,128,1024]{2,1,0:T(8,128)(2,1)} %get-tuple-element.860), channel_id=1, source_target_pairs={{1,0},{2,1},{3,2},{4,3},{5,4},{6,5},{7,6},{8,7},{9,8},{10,9},{11,1... | collective-permute-start | bytes 1572872 | tf_op jit(solution)/shard_map/ppermute | solution.py:47
  419.5 25.4 %collective-permute-start.17 = (bf16[2,64,1024]{2,1,0:T(8,128)(2,1)S(1)}, bf16[2,64,1024]{2,1,0:T(8,128)(2,1)}, u32[]{:S(2)}, u32[]{:S(2)}) collective-permute-start(bf16[2,64,1024]{2,1,0:T(8,128)(2,1)S(1)} %select_convert_fusion), channel_id=1, source_target_pairs={{0,1},{1,0},{2,3},{3,2},{4,5},{5,4},{6,7},{7,6},{8,9},{9,8},{10,11... | collective-permute-start | bytes 786440 | tf_op jit(solution)/shard_map/ppermute | solution.py:20
  439.5 5.4 %copy-start.6 = (f32[2,128,1024]{2,1,0:T(8,128)S(1)}, f32[2,128,1024]{2,1,0:T(8,128)}, u32[]{:S(2)}) copy-start(f32[2,128,1024]{2,1,0:T(8,128)} %copy-done.5) | copy-start | bytes 3145732
  442.2 3.8 copy-start.4
where the time goes:
time: 456 us; the launch traced here: 453 us
  matrix products  222 us (49%)
  local copies, waits for them, and re-layouts  89.5 us (20%)
  starting transfers between devices  67.4 us (15%)
  other arithmetic  58.3 us (13%)
  waiting for transfers between devices  13.8 us (3%)
    dot_general x8, matrix products, per_head(): jnp.einsum('sme,smy->sey', logit_gradient, head_query_rows, preferred_ele...  64 us
    dot_general x8, matrix products, per_head(): jnp.einsum('fow,fwn->fon', logit_gradient, head_key_rows, preferred_eleme...  60.9 us
    ppermute x10, starting transfers between devices, shifted(): return lax.ppermute(array, axis, pairs)  35.7 us
    sub x8, matrix products, per_head(): exp_terms = jnp.exp(scores - row_max)  27.2 us
    ppermute x3, starting transfers between devices, extended(): lax.ppermute(head, axis, [((i + 1) % count, i) for i in range(ends)])  25.2 us
    dot_general x8, matrix products, per_head(): jnp.einsum('gte,gve->gtv', output_head_gradient, head_value_rows, preferr...  24.8 us
    dot_general x8, matrix products, per_head(): jnp.einsum('fow,fwn->fon', attention_weight, head_value_rows, preferred_e...  24.6 us
    dot_general x8, matrix products, per_head(): jnp.einsum('sme,smy->sey', attention_weight, output_head_gradient, prefer...  20.8 us
  transfers between devices with their start and end apart: 18, of which 3 were waited for; matrix products, arithmetic and copies ran while one was open for 12% of the time, Pallas kernels for 0%

commit v1 on v0

v1 whole, which is shorter than its diff:
```python
import functools
import math

import jax
import jax.numpy as jnp
import numpy as np
from jax import lax
from jax.experimental import pallas as pl
from jax.experimental.pallas import tpu as pltpu
from jax.sharding import PartitionSpec as P

H = 8
HD = 128
NB = 128
HB = NB // 2
TOK = 4 * NB
EDGE = 2 * NB
ROWS = 9 * NB
SCALE = 1.0 / math.sqrt(HD)
SCALE_LOG2 = SCALE * math.log2(math.e)
PENALTY = 1e30
BF = jnp.bfloat16
F32 = jnp.float32


def pool_matrix(rows, source_rows, pieces):
    matrix = np.zeros((rows, source_rows), np.float32)
    for first, count, source, factor in pieces:
        for row in range(count):
            start = source + row * factor
            matrix[first + row, start : start + factor] = 1.0 / factor
    return matrix


BLOCK_POOL = pool_matrix(128, 128, [(0, 64, 0, 2), (64, 32, 0, 4), (96, 16, 0, 8)])
NEAR_POOL = pool_matrix(128, 256, [(0, 64, 0, 2), (64, 32, 0, 4), (96, 32, 128, 2)])
FAR_POOL = pool_matrix(64, 256, [(0, 16, 0, 8), (16, 16, 128, 4), (32, 32, 192, 2)])
SPREAD = pool_matrix(
    576,
    512,
    [
        (0, 128, 0, 1),
        (128, 64, 128, 2),
        (192, 64, 256, 4),
        (256, 128, 384, 1),
        (384, 64, 256, 2),
        (448, 64, 0, 4),
        (512, 64, 0, 8),
    ],
).T
BLOCK_SPREAD = np.concatenate([BLOCK_POOL[:64].T, BLOCK_POOL[:64].T], axis=1)


def mm(a, b):
    return jnp.dot(a, b, preferred_element_type=F32)


def mm_nt(a, b):
    return lax.dot_general(a, b, (((1,), (1,)), ((), ())), preferred_element_type=F32)


def is_even():
    return lax.rem(lax.axis_index("ctx"), 2) == 0


def pool_kernel(pool_ref, k_ref, v_ref, cross_ref, inner_ref, far_ref):
    even = is_even()
    for which, ref in enumerate((k_ref, v_ref)):
        pooled = [
            mm(pool_ref[...], ref[b * NB : (b + 1) * NB, :]).astype(BF) for b in range(4)
        ]

        def left(out):
            out[which, :NB] = ref[:NB, :]
            out[which, NB : NB + 64] = pooled[1][:64]
            out[which, NB + 64 : NB + 96] = pooled[2][64:96]
            out[which, NB + 96 :] = pooled[3][64:96]

        def right(out):
            out[which, :NB] = ref[3 * NB :, :]
            out[which, NB : NB + 64] = pooled[2][:64]
            out[which, NB + 64 : NB + 96] = pooled[0][64:96]
            out[which, NB + 96 :] = pooled[1][64:96]

        @pl.when(even)
        def _():
            left(cross_ref)
            right(inner_ref)

        @pl.when(jnp.logical_not(even))
        def _():
            right(cross_ref)
            left(inner_ref)

        for b in range(4):
            far_ref[which, b * 16 : (b + 1) * 16] = pooled[b][96:112]


def far_kernel(pool_ref, cross_ref, far_ref, out_ref):
    for which in range(2):
        out_ref[which, :64] = far_ref[which]
        out_ref[which, 64:] = mm(pool_ref[...], cross_ref[which]).astype(BF)


def fold_kernel(pool_ref, cross_ref, far_ref, got_ref, cross_out, far_out):
    for which in range(2):
        spread = mm(pool_ref[...], got_ref[which, 64:])
        cross_out[which] = (cross_ref[which].astype(F32) + spread).astype(BF)
        far_out[which] = (far_ref[which].astype(F32) + got_ref[which, :64].astype(F32)).astype(BF)


def final_kernel(spread_ref, cross_ref, inner_ref, far_ref, kg_ref, vg_ref, kg_out, vg_out):
    even = is_even()
    for which, (ref, out) in enumerate(((kg_ref, kg_out), (vg_ref, vg_out))):
        cross = cross_ref[which]
        inner = inner_ref[which]
        left = jnp.where(even, cross, inner)
        right = jnp.where(even, inner, cross)
        rows = jnp.concatenate([left, right, far_ref[which]], axis=0)
        out[...] = ref[...] + mm(spread_ref[...], rows)


PAIR_ROWS = (
    ((0, 384), (512, 704), (768, 1152)),
    ((128, 512), (576, 768), (768, 1152)),
)
PAIR_ZEROS = (((384, 512), (704, 768)), ((0, 128), (512, 576)))
CHUNKS = (
    (
        (0, 128, 0, "left"),
        (128, 512, 0, "own"),
        (512, 576, 1, "own"),
        (576, 640, 1, "left"),
        (640, 704, 1, "own"),
        (704, 768, 1, "left"),
        (768, 832, 2, "left"),
        (832, 960, 2, "right"),
        (960, 1024, 3, "far0"),
        (1024, 1088, 3, "far1"),
        (1088, 1152, 3, "far2"),
    ),
    (
        (0, 384, 0, "own"),
        (384, 512, 0, "right"),
        (512, 576, 1, "right"),
        (576, 640, 1, "own"),
        (640, 704, 1, "right"),
        (704, 768, 1, "own"),
        (768, 896, 2, "left"),
        (896, 960, 2, "right"),
        (960, 1024, 3, "far0"),
        (1024, 1088, 3, "far1"),
        (1088, 1152, 3, "far2"),
    ),
)


def overlap(chunk, ranges):
    for low, high in ranges:
        first, end = max(chunk[0], low), min(chunk[1], high)
        if first < end:
            return first, end
    return None


def fold_rows(x, op):
    return op(x.reshape(x.shape[0] // 8, 8, x.shape[1]), axis=0)


def core_kernel(
    devices,
    pool_ref,
    near_ref,
    near_t_ref,
    spread_ref,
    q_ref,
    k_ref,
    v_ref,
    g_ref,
    cross_ref,
    inner_ref,
    far_ref,
    swap_ref,
    att_ref,
    dq_ref,
    kg_ref,
    vg_ref,
    crossg_ref,
    innerg_ref,
    farg_ref,
    swapg_ref,
    rows_ref,
    cols_ref,
    s_ref,
    p_ref,
    ds_ref,
):
    d = lax.axis_index("ctx")
    even = is_even()

    def penalty(valid):
        return jnp.where(valid, 0.0, PENALTY).astype(F32)

    step = jnp.where(even, 1, -1)
    far_ids = (d - 2 * step, d + 3 * step, d + 2 * step)
    penalties = {"own": 0.0, "left": penalty(d > 0), "right": penalty(d < devices - 1)}
    for i, far_id in enumerate(far_ids):
        penalties["far%d" % i] = penalty((far_id >= 0) & (far_id < devices))

    @pl.when(pl.program_id(0) == 0)
    def _():
        for pair in range(2):
            for blk in range(2):
                for low, high in PAIR_ZEROS[blk]:
                    zeros = jnp.zeros((high - low, NB), BF)
                    p_ref[pair, low:high, blk * NB : (blk + 1) * NB] = zeros
                    ds_ref[pair, low:high, blk * NB : (blk + 1) * NB] = zeros

    for which, own in enumerate((k_ref, v_ref)):
        cross = cross_ref[which]
        inner = inner_ref[which]
        left = jnp.where(even, cross, inner)
        right = jnp.where(even, inner, cross)
        near_l = mm(near_ref[...], left).astype(BF)
        near_r = mm(near_ref[...], right).astype(BF)
        halves = [
            mm(pool_ref[:64], own[b * NB : (b + 1) * NB, :]).astype(BF) for b in range(4)
        ]
        a = rows_ref.at[0, which]
        b = rows_ref.at[1, which]
        a[:128] = left[:128]
        a[128:512] = own[: 3 * NB, :]
        a[512:576] = halves[2]
        a[576:640] = left[128:192]
        a[640:704] = halves[3]
        a[704:768] = near_l[:64]
        a[768:832] = left[192:256]
        a[832:896] = near_r[64:]
        a[896:960] = right[192:256]
        b[:384] = own[NB:, :]
        b[384:512] = right[:128]
        b[512:576] = near_r[:64]
        b[576:640] = halves[0]
        b[640:704] = right[128:192]
        b[704:768] = halves[1]
        b[768:832] = left[192:256]
        b[832:896] = near_l[64:]
        b[896:960] = right[192:256]
        for pair in (a, b):
            pair[960:1024] = far_ref[which]
            pair[1024:1152] = swap_ref[which]
        for pair in range(2):
            cols_ref[pair, which] = rows_ref[pair, which].T

    grads = []
    for pair in range(2):
        first = pair * 2 * NB
        q = q_ref[first : first + 2 * NB, :]
        g = g_ref[first : first + 2 * NB, :]
        g_t = g.T
        best = [None, None]
        for chunk in CHUNKS[pair]:
            low, high, level, side = chunk
            s = mm_nt(rows_ref[pair, 0, low:high], q)
            s_ref[pair, low:high] = s
            for blk in range(2):
                part = overlap(chunk, PAIR_ROWS[blk])
                if part is None:
                    continue
                piece = s[part[0] - low : part[1] - low, blk * NB : (blk + 1) * NB]
                top = fold_rows(piece, jnp.max) * SCALE_LOG2 + (level - penalties[side])
                best[blk] = top if best[blk] is None else jnp.maximum(best[blk], top)
        best = [jnp.max(b, axis=0, keepdims=True) for b in best]
        totals = []
        for blk in range(2):
            lanes = slice(blk * NB, (blk + 1) * NB)
            total = jnp.zeros((8, NB), F32)
            for chunk in CHUNKS[pair]:
                low, high, level, side = chunk
                part = overlap(chunk, PAIR_ROWS[blk])
                if part is None:
                    continue
                shift = best[blk] - (level - penalties[side])
                prob = jnp.exp2(s_ref[pair, part[0] : part[1], lanes] * SCALE_LOG2 - shift)
                total = total + fold_rows(prob, jnp.sum)
                p_ref[pair, part[0] : part[1], lanes] = prob.astype(BF)
            totals.append(jnp.sum(total, axis=0, keepdims=True))
        inverse = 1.0 / jnp.concatenate(totals, axis=1)
        out_t = mm(cols_ref[pair, 1], p_ref[pair]) * inverse
        att_ref[first : first + 2 * NB, :] = out_t.T.astype(BF)
        delta = jnp.sum(out_t * g_t.astype(F32), axis=0, keepdims=True)
        for chunk in CHUNKS[pair]:
            low, high, level, side = chunk
            dp = mm(rows_ref[pair, 1, low:high], g_t)
            for blk in range(2):
                lanes = slice(blk * NB, (blk + 1) * NB)
                part = overlap(chunk, PAIR_ROWS[blk])
                if part is None:
                    continue
                piece = dp[part[0] - low : part[1] - low, lanes]
                prob = p_ref[pair, part[0] : part[1], lanes].astype(F32) * inverse[:, lanes]
                p_ref[pair, part[0] : part[1], lanes] = prob.astype(BF)
                ds_ref[pair, part[0] : part[1], lanes] = (
                    prob * (piece - delta[:, lanes])
                ).astype(BF)
        dq_t = mm(cols_ref[pair, 0], ds_ref[pair]) * SCALE
        dq_ref[first : first + 2 * NB, :] = dq_t.T
        grads.append((mm(ds_ref[pair], q) * SCALE, mm(p_ref[pair], g)))

    for which, out in enumerate((kg_ref, vg_ref)):
        a = grads[0][which]
        b = grads[1][which]
        tokens = (
            a[128:256],
            a[256:384] + b[:128],
            a[384:512] + b[128:256],
            b[256:384],
        )
        halves = (b[576:640], b[704:768], a[512:576], a[640:704])
        for blk in range(4):
            high = halves[blk].astype(BF)
            low = (halves[blk] - high.astype(F32)).astype(BF)
            spread = mm(spread_ref[...], jnp.concatenate([high, low], axis=0))
            out[blk * NB : (blk + 1) * NB, :] = tokens[blk] + spread
        near_l = jnp.concatenate([a[704:768], b[832:896]], axis=0).astype(BF)
        near_r = jnp.concatenate([b[512:576], a[832:896]], axis=0).astype(BF)
        left = jnp.concatenate([a[:128], a[576:640], a[768:832] + b[768:832]], axis=0)
        right = jnp.concatenate([b[384:512], b[640:704], a[896:960] + b[896:960]], axis=0)
        left = (left + mm(near_t_ref[...], near_l)).astype(BF)
        right = (right + mm(near_t_ref[...], near_r)).astype(BF)
        crossg_ref[which] = jnp.where(even, left, right)
        innerg_ref[which] = jnp.where(even, right, left)
        far = (a[960:] + b[960:]).astype(BF)
        farg_ref[which] = far[:64]
        swapg_ref[which] = far[64:]


VMEM_LIMIT = 56 * 2**20


def params():
    return pltpu.CompilerParams(vmem_limit_bytes=VMEM_LIMIT)


def whole(shape):
    return pl.BlockSpec(shape, lambda i: (0,) * len(shape))


def lanes(rows, width, pair=True):
    if pair:
        return pl.BlockSpec((2, rows, width), lambda i: (0, 0, i))
    return pl.BlockSpec((rows, width), lambda i: (0, i))


def constant(matrix):
    return jnp.asarray(matrix, BF)


def shaped(*shape, dtype=BF):
    return jax.ShapeDtypeStruct(shape, dtype)


def swap_pairs(n):
    return [(i, i ^ 1) for i in range(n)]


def in_range(pairs, n):
    return [(i, j) for i, j in pairs if 0 <= j < n]


def cross_pairs(n):
    return in_range([(i, i + 1 if i % 2 else i - 1) for i in range(n)], n)


def far_pairs(n):
    return in_range([(i, i - 2 if i % 2 else i + 2) for i in range(n)], n)


def back_pairs(n):
    return in_range([(i, i + 2 if i % 2 else i - 2) for i in range(n)], n)


def body(queries, keys, values, out_grad):
    tok, feat = queries.shape
    n = lax.axis_size("ctx")
    width = 256
    cross, inner, far = pl.pallas_call(
        pool_kernel,
        grid=(feat // width,),
        in_specs=[whole((128, 128)), lanes(tok, width, False), lanes(tok, width, False)],
        out_specs=[lanes(EDGE, width), lanes(EDGE, width), lanes(64, width)],
        out_shape=[shaped(2, EDGE, feat), shaped(2, EDGE, feat), shaped(2, 64, feat)],
        compiler_params=params(),
        name="pool",
    )(constant(BLOCK_POOL), keys, values)
    cross_in = lax.ppermute(cross, "ctx", cross_pairs(n))
    far_in = lax.ppermute(far, "ctx", far_pairs(n))
    inner_in = lax.ppermute(inner, "ctx", swap_pairs(n))
    far_send = pl.pallas_call(
        far_kernel,
        grid=(feat // width,),
        in_specs=[whole((64, 256)), lanes(EDGE, width), lanes(64, width)],
        out_specs=lanes(128, width),
        out_shape=shaped(2, 128, feat),
        compiler_params=params(),
        name="far",
    )(constant(FAR_POOL), cross_in, far_in)
    swap_in = lax.ppermute(far_send, "ctx", swap_pairs(n))

    att, dq, kg, vg, cross_g, inner_g, far_g, swap_g = pl.pallas_call(
        functools.partial(core_kernel, n),
        grid=(feat // HD,),
        in_specs=[
            whole((128, 128)),
            whole((128, 256)),
            whole((256, 128)),
            whole((128, 128)),
            lanes(tok, HD, False),
            lanes(tok, HD, False),
            lanes(tok, HD, False),
            lanes(tok, HD, False),
            lanes(EDGE, HD),
            lanes(EDGE, HD),
            lanes(64, HD),
            lanes(128, HD),
        ],
        out_specs=[
            lanes(tok, HD, False),
            lanes(tok, HD, False),
            lanes(tok, HD, False),
            lanes(tok, HD, False),
            lanes(EDGE, HD),
            lanes(EDGE, HD),
            lanes(64, HD),
            lanes(128, HD),
        ],
        out_shape=[
            shaped(tok, feat),
            shaped(tok, feat, dtype=F32),
            shaped(tok, feat, dtype=F32),
            shaped(tok, feat, dtype=F32),
            shaped(2, EDGE, feat),
            shaped(2, EDGE, feat),
            shaped(2, 64, feat),
            shaped(2, 128, feat),
        ],
        scratch_shapes=[
            pltpu.VMEM((2, 2, ROWS, HD), BF),
            pltpu.VMEM((2, 2, HD, ROWS), BF),
            pltpu.VMEM((2, ROWS, 2 * NB), F32),
            pltpu.VMEM((2, ROWS, 2 * NB), BF),
            pltpu.VMEM((2, ROWS, 2 * NB), BF),
        ],
        compiler_params=params(),
        name="core",
    )(
        constant(BLOCK_POOL),
        constant(NEAR_POOL),
        constant(NEAR_POOL.T),
        constant(BLOCK_SPREAD),
        queries,
        keys,
        values,
        out_grad,
        cross_in,
        inner_in,
        far_in,
        swap_in,
    )

    swap_back = lax.ppermute(swap_g, "ctx", swap_pairs(n))
    cross_g, far_g = pl.pallas_call(
        fold_kernel,
        grid=(feat // width,),
        in_specs=[whole((256, 64)), lanes(EDGE, width), lanes(64, width), lanes(128, width)],
        out_specs=[lanes(EDGE, width), lanes(64, width)],
        out_shape=[shaped(2, EDGE, feat), shaped(2, 64, feat)],
        compiler_params=params(),
        name="fold",
    )(constant(FAR_POOL.T), cross_g, far_g, swap_back)
    cross_back = lax.ppermute(cross_g, "ctx", cross_pairs(n))
    far_back = lax.ppermute(far_g, "ctx", back_pairs(n))
    inner_back = lax.ppermute(inner_g, "ctx", swap_pairs(n))
    kg, vg = pl.pallas_call(
        final_kernel,
        grid=(feat // width,),
        in_specs=[
            whole((512, 576)),
            lanes(EDGE, width),
            lanes(EDGE, width),
            lanes(64, width),
            lanes(tok, width, False),
            lanes(tok, width, False),
        ],
        out_specs=[lanes(tok, width, False), lanes(tok, width, False)],
        out_shape=[shaped(tok, feat, dtype=F32), shaped(tok, feat, dtype=F32)],
        input_output_aliases={4: 0, 5: 1},
        compiler_params=params(),
        name="final",
    )(constant(SPREAD), cross_back, inner_back, far_back, kg, vg)
    return att, dq, kg, vg


def solution(mesh):
    spec = P("ctx", None)
    return jax.shard_map(
        body,
        mesh=mesh,
        in_specs=(spec, spec, spec, spec),
        out_specs=(spec, spec, spec, spec),
        check_vma=False,
    )
```

time: 456 us -> 110 us (0.24)
  matrix products: 222 us -> 0 us
  local copies, waits for them, and re-layouts: 89.5 us -> 4.66 us
  other arithmetic: 58.3 us -> 0 us
  Pallas kernels: 0 us -> 50.8 us
  starting transfers between devices: 67.4 us -> 21.6 us
  waiting for transfers between devices: 13.8 us -> 30.7 us
    dot_general x40 -> x0, matrix products: 195 us -> none  [the longest x8 64 us: per_head(): jnp.einsum('sme,smy->sey', logit_gradient, head_query_rows, preferred_ele...]
    pallas_call x0 -> x5, Pallas kernels: none -> 50.8 us  [the longest x1 31.7 us: body(): pl.pallas_call(functools.partial(core_kernel, n), grid=(feat // HD,), in_...]
    ppermute x18 -> x8, starting transfers between devices: 67.4 us -> 21.6 us  [the longest x1 9.92 us: body(): cross_in = lax.ppermute(cross, 'ctx', cross_pairs(n))]
    sub x8 -> x0, matrix products: 27.2 us -> none  [per_head(): exp_terms = jnp.exp(scores - row_max)]
    dynamic_update_slice x24 -> x0, local copies, waits for them, and re-layouts: 20.6 us -> none  [per_head(): lax.dynamic_update_slice_in_dim(level_grads[level_id], grad_piece, lane_s...]
    slice x15 -> x0, local copies, waits for them, and re-layouts: 19.5 us -> none  [the longest x8 11.9 us: per_head(): head_lanes[level_id][:, local_sup * NB:local_sup * NB + 3 * NB]]
    broadcast_in_dim x8 -> x0, local copies, waits for them, and re-layouts: 18.5 us -> none  [the longest x4 9.15 us: body(): jnp.zeros(shape_of, jnp.float32)]
    ppermute x18 -> x8, waiting for transfers between devices: 13.8 us -> 30.7 us  [the longest x1 13.5 us: body(): far_back = lax.ppermute(far_g, 'ctx', back_pairs(n))]
  transfers between devices with their start and end apart: 18 -> 8, of which waited for: 3 -> 4; matrix products, arithmetic and copies ran while one was open for 12% -> 0% of each run, Pallas kernels for 0% -> 7%
where the time goes in v1:
time: 110 us; the launch traced here: 108 us
  Pallas kernels  50.8 us (46%)
  waiting for transfers between devices  30.7 us (28%)
  starting transfers between devices  21.6 us (20%)
  local copies, waits for them, and re-layouts  4.66 us (4%)
    pallas_call x1, Pallas kernels, body(): pl.pallas_call(functools.partial(core_kernel, n), grid=(feat // HD,), in_...  31.7 us
    ppermute x1, waiting for transfers between devices, body(): far_back = lax.ppermute(far_g, 'ctx', back_pairs(n))  13.5 us
    ppermute x1, waiting for transfers between devices, body(): far_in = lax.ppermute(far, 'ctx', far_pairs(n))  13.5 us
    ppermute x1, starting transfers between devices, body(): cross_in = lax.ppermute(cross, 'ctx', cross_pairs(n))  9.92 us
    ppermute x1, starting transfers between devices, body(): cross_back = lax.ppermute(cross_g, 'ctx', cross_pairs(n))  7.14 us
    pallas_call x1, Pallas kernels, body(): pl.pallas_call(final_kernel, grid=(feat // width,), in_specs=[whole((512,...  6.81 us
    unnamed x16, local copies, waits for them, and re-layouts  4.66 us
    pallas_call x1, Pallas kernels, body(): pl.pallas_call(pool_kernel, grid=(feat // width,), in_specs=[whole((128,...  4.65 us
  transfers between devices with their start and end apart: 8, of which 4 were waited for; matrix products, arithmetic and copies ran while one was open for 0% of the time, Pallas kernels for 7%

profile of v1, /device:TPU:6, one launch (start us, length us, event | category | flops | bytes accessed | tf_op | source)
XLA Modules:
  0.0 108.4 jit_solution(13698366929309176018)
XLA Ops:
  0.6 4.7 %pool.1 = (bf16[2,256,1024]{2,1,0:T(8,128)(2,1)}, bf16[2,256,1024]{2,1,0:T(8,128)(2,1)}, bf16[2,64,1024]{2,1,0:T(8,128)(2,1)}) custom-call(bf16[128,128]{1,0:T(8,128)(2,1)} %constant.14.clone.pool_ref, bf16[512,1024]{1,0:T(8,128)(2,1)} %k_ref.3, bf16[512,1024]{1,0:T(8,128)(2,1)} %v_ref.3), custom_call_target="tpu_custom_call" | custom-call | tf_op jit(solution)/shard_map/pool/pallas_call | solution.py:387
  5.3 9.9 %collective-permute-start = (bf16[2,256,1024]{2,1,0:T(8,128)(2,1)}, bf16[2,256,1024]{2,1,0:T(8,128)(2,1)S(1)}, u32[]{:S(2)}, u32[]{:S(2)}) collective-permute-start(bf16[2,256,1024]{2,1,0:T(8,128)(2,1)} %get-tuple-element.19), channel_id=1, source_target_pairs={{1,2},{2,1},{3,4},{4,3},{5,6},{6,5},{7,8},{8,7},{9,10},{10,9},{11,... | collective-permute-start | bytes 3145736 | tf_op jit(solution)/shard_map/ppermute | solution.py:396
  15.2 0.1 collective-permute-start.1
  15.3 1.9 %collective-permute-start.2 = (bf16[2,64,1024]{2,1,0:T(8,128)(2,1)}, bf16[2,64,1024]{2,1,0:T(8,128)(2,1)S(1)}, u32[]{:S(2)}, u32[]{:S(2)}) collective-permute-start(bf16[2,64,1024]{2,1,0:T(8,128)(2,1)} %get-tuple-element.21), channel_id=1, source_target_pairs={{0,2},{2,4},{3,1},{4,6},{5,3},{6,8},{7,5},{8,10},{9,7},{10,12},{11... | collective-permute-start | bytes 786440 | tf_op jit(solution)/shard_map/ppermute | solution.py:397
  17.2 13.5 %collective-permute-done.2.far_ref = bf16[2,64,1024]{2,1,0:T(8,128)(2,1)S(1)} collective-permute-done((bf16[2,64,1024]{2,1,0:T(8,128)(2,1)}, bf16[2,64,1024]{2,1,0:T(8,128)(2,1)S(1)}, u32[]{:S(2)}, u32[]{:S(2)}) %collective-permute-start.2) | collective-permute-done | bytes 262176 | tf_op jit(solution)/shard_map/ppermute | solution.py:397
  30.7 0.0 copy-start.1
  30.7 0.0 collective-permute-done.cross_ref
  30.7 0.7 copy-done.1
  31.4 0.0 copy-start
  31.4 1.0 copy-done
  32.4 3.6 %far.1 = bf16[2,128,1024]{2,1,0:T(8,128)(2,1)} custom-call(bf16[64,256]{1,0:T(8,128)(2,1)} %constant.15.clone.pool_ref, bf16[2,256,1024]{2,1,0:T(8,128)(2,1)} %copy-done, bf16[2,64,1024]{2,1,0:T(8,128)(2,1)} %copy-done.1), custom_call_target="tpu_custom_call" | custom-call | tf_op jit(solution)/shard_map/far/pallas_call | solution.py:399
  36.0 0.0 collective-permute-start.3
  36.0 0.0 collective-permute-done.1.inner_ref
  36.0 0.0 copy-start.2
  36.0 2.1 %collective-permute-done.3.swap_ref = bf16[2,128,1024]{2,1,0:T(8,128)(2,1)S(1)} collective-permute-done((bf16[2,128,1024]{2,1,0:T(8,128)(2,1)}, bf16[2,128,1024]{2,1,0:T(8,128)(2,1)S(1)}, u32[]{:S(2)}, u32[]{:S(2)}) %collective-permute-start.3) | collective-permute-done | bytes 524320 | tf_op jit(solution)/shard_map/ppermute | solution.py:408
  38.1 0.0 copy-done.2
  38.1 0.0 copy-start.5
  38.1 0.8 copy-done.5
  38.9 31.7 %core.1 = (bf16[512,1024]{1,0:T(8,128)(2,1)}, f32[512,1024]{1,0:T(8,128)}, f32[512,1024]{1,0:T(8,128)}, f32[512,1024]{1,0:T(8,128)}, bf16[2,256,1024]{2,1,0:T(8,...) custom-call(bf16[128,128]{1,0:T(8,128)(2,1)} %constant.14.clone.pool_ref, ...), custom_call_target="tpu_custom_call" | custom-call | tf_op jit(solution)/shard_map/core/pallas_call | solution.py:410
  70.6 0.2 collective-permute-start.4
  70.8 0.4 collective-permute-start.6
  71.2 1.6 %collective-permute-done.4.got_ref = bf16[2,128,1024]{2,1,0:T(8,128)(2,1)S(1)} collective-permute-done((bf16[2,128,1024]{2,1,0:T(8,128)(2,1)}, bf16[2,128,1024]{2,1,0:T(8,128)(2,1)S(1)}, u32[]{:S(2)}, u32[]{:S(2)}) %collective-permute-start.4) | collective-permute-done | bytes 524320 | tf_op jit(solution)/shard_map/ppermute | solution.py:471
  72.8 0.0 copy-start.6
  72.8 0.8 copy-done.6
  73.6 4.0 %fold.1 = (bf16[2,256,1024]{2,1,0:T(8,128)(2,1)}, bf16[2,64,1024]{2,1,0:T(8,128)(2,1)}) custom-call(bf16[256,64]{1,0:T(8,128)(2,1)} %constant.19.clone.pool_ref, bf16[2,256,1024]{2,1,0:T(8,128)(2,1)} %get-tuple-element.24.cross_ref, bf16[2,64,1024]{2,1,0:T(8,128)(2,1)} %get-tuple-element.25.far_ref, bf16[2,128,1024]{2,1,0:T(8,128)(2,1)} %copy-done.6), custom_call_target="tpu_custom_call" | custom-call | tf_op jit(solution)/shard_map/fold/pallas_call | solution.py:472
  77.6 7.1 %collective-permute-start.5 = (bf16[2,256,1024]{2,1,0:T(8,128)(2,1)}, bf16[2,256,1024]{2,1,0:T(8,128)(2,1)S(1)}, u32[]{:S(2)}, u32[]{:S(2)}) collective-permute-start(bf16[2,256,1024]{2,1,0:T(8,128)(2,1)} %get-tuple-element.27), channel_id=1, source_target_pairs={{1,2},{2,1},{3,4},{4,3},{5,6},{6,5},{7,8},{8,7},{9,10},{10,9},{11,... | collective-permute-start | bytes 3145736 | tf_op jit(solution)/shard_map/ppermute | solution.py:481
  84.8 1.9 %collective-permute-start.7 = (bf16[2,64,1024]{2,1,0:T(8,128)(2,1)}, bf16[2,64,1024]{2,1,0:T(8,128)(2,1)S(1)}, u32[]{:S(2)}, u32[]{:S(2)}) collective-permute-start(bf16[2,64,1024]{2,1,0:T(8,128)(2,1)} %get-tuple-element.29), channel_id=1, source_target_pairs={{1,3},{2,0},{3,5},{4,2},{5,7},{6,4},{7,9},{8,6},{9,11},{10,8},{11,... | collective-permute-start | bytes 786440 | tf_op jit(solution)/shard_map/ppermute | solution.py:482
  86.7 13.5 %collective-permute-done.7.far_ref = bf16[2,64,1024]{2,1,0:T(8,128)(2,1)S(1)} collective-permute-done((bf16[2,64,1024]{2,1,0:T(8,128)(2,1)}, bf16[2,64,1024]{2,1,0:T(8,128)(2,1)S(1)}, u32[]{:S(2)}, u32[]{:S(2)}) %collective-permute-start.7) | collective-permute-done | bytes 262176 | tf_op jit(solution)/shard_map/ppermute | solution.py:482
  100.2 0.0 copy-start.7
  100.2 0.0 collective-permute-done.6.inner_ref
  100.2 0.0 copy-start.3
  100.2 0.0 collective-permute-done.5.cross_ref
  100.2 0.0 copy-start.4
  100.2 0.7 copy-done.7
  100.9 0.4 copy-done.3
  101.2 0.4 copy-done.4
  101.6 6.8 %final.1 = (f32[512,1024]{1,0:T(8,128)}, f32[512,1024]{1,0:T(8,128)}) custom-call(bf16[512,576]{1,0:T(8,128)(2,1)} %constant.20.clone.spread_ref, bf16[2,256,1024]{2,1,0:T(8,128)(2,1)} %copy-done.4, bf16[2,256,1024]{2,1,0:T(8,128)(2,1)} %copy-done.3, bf16[2,64,1024]{2,1,0:T(8,128)(2,1)} %copy-done.7, ...), custom_call_target="tpu_custom_call", output_to_operand_aliasing={{0}: (4, {}), {1}: (5, {})} | custom-call | tf_op jit(solution)/shard_map/final/pallas_call | solution.py:484
Async XLA Ops:
  5.3 25.4 %collective-permute-start = (bf16[2,256,1024]{2,1,0:T(8,128)(2,1)}, bf16[2,256,1024]{2,1,0:T(8,128)(2,1)S(1)}, u32[]{:S(2)}, u32[]{:S(2)}) collective-permute-start(bf16[2,256,1024]{2,1,0:T(8,128)(2,1)} %get-tuple-element.19), channel_id=1, source_target_pairs={{1,2},{2,1},{3,4},{4,3},{5,6},{6,5},{7,8},{8,7},{9,10},{10,9},{11,... | collective-permute-start | bytes 3145736 | tf_op jit(solution)/shard_map/ppermute | solution.py:396
  15.2 20.8 %collective-permute-start.1 = (bf16[2,256,1024]{2,1,0:T(8,128)(2,1)}, bf16[2,256,1024]{2,1,0:T(8,128)(2,1)S(1)}, u32[]{:S(2)}, u32[]{:S(2)}) collective-permute-start(bf16[2,256,1024]{2,1,0:T(8,128)(2,1)} %get-tuple-element.20), channel_id=1, source_target_pairs={{0,1},{1,0},{2,3},{3,2},{4,5},{5,4},{6,7},{7,6},{8,9},{9,8},{10,11... | collective-permute-start | bytes 3145736 | tf_op jit(solution)/shard_map/ppermute | solution.py:398
  15.3 15.4 %collective-permute-start.2 = (bf16[2,64,1024]{2,1,0:T(8,128)(2,1)}, bf16[2,64,1024]{2,1,0:T(8,128)(2,1)S(1)}, u32[]{:S(2)}, u32[]{:S(2)}) collective-permute-start(bf16[2,64,1024]{2,1,0:T(8,128)(2,1)} %get-tuple-element.21), channel_id=1, source_target_pairs={{0,2},{2,4},{3,1},{4,6},{5,3},{6,8},{7,5},{8,10},{9,7},{10,12},{11... | collective-permute-start | bytes 786440 | tf_op jit(solution)/shard_map/ppermute | solution.py:397
  30.7 0.7 copy-start.1
  31.4 1.0 copy-start
  36.0 2.1 %collective-permute-start.3 = (bf16[2,128,1024]{2,1,0:T(8,128)(2,1)}, bf16[2,128,1024]{2,1,0:T(8,128)(2,1)S(1)}, u32[]{:S(2)}, u32[]{:S(2)}) collective-permute-start(bf16[2,128,1024]{2,1,0:T(8,128)(2,1)} %far.1), channel_id=1, source_target_pairs={{0,1},{1,0},{2,3},{3,2},{4,5},{5,4},{6,7},{7,6},{8,9},{9,8},{10,11... | collective-permute-start | bytes 1572872 | tf_op jit(solution)/shard_map/ppermute | solution.py:408
  36.0 2.1 %copy-start.2 = (bf16[2,256,1024]{2,1,0:T(8,128)(2,1)}, bf16[2,256,1024]{2,1,0:T(8,128)(2,1)S(1)}, u32[]{:S(2)}) copy-start(bf16[2,256,1024]{2,1,0:T(8,128)(2,1)S(1)} %collective-permute-done.1.inner_ref) | copy-start | bytes 3145732
  38.1 0.8 copy-start.5
  70.6 2.2 %collective-permute-start.4 = (bf16[2,128,1024]{2,1,0:T(8,128)(2,1)}, bf16[2,128,1024]{2,1,0:T(8,128)(2,1)S(1)}, u32[]{:S(2)}, u32[]{:S(2)}) collective-permute-start(bf16[2,128,1024]{2,1,0:T(8,128)(2,1)} %get-tuple-element.26), channel_id=1, source_target_pairs={{0,1},{1,0},{2,3},{3,2},{4,5},{5,4},{6,7},{7,6},{8,9},{9,8},{10,11... | collective-permute-start | bytes 1572872 | tf_op jit(solution)/shard_map/ppermute | solution.py:471
  70.8 29.4 %collective-permute-start.6 = (bf16[2,256,1024]{2,1,0:T(8,128)(2,1)}, bf16[2,256,1024]{2,1,0:T(8,128)(2,1)S(1)}, u32[]{:S(2)}, u32[]{:S(2)}) collective-permute-start(bf16[2,256,1024]{2,1,0:T(8,128)(2,1)} %get-tuple-element.28), channel_id=1, source_target_pairs={{0,1},{1,0},{2,3},{3,2},{4,5},{5,4},{6,7},{7,6},{8,9},{9,8},{10,11... | collective-permute-start | bytes 3145736 | tf_op jit(solution)/shard_map/ppermute | solution.py:483
  72.8 0.8 copy-start.6
  77.6 22.6 %collective-permute-start.5 = (bf16[2,256,1024]{2,1,0:T(8,128)(2,1)}, bf16[2,256,1024]{2,1,0:T(8,128)(2,1)S(1)}, u32[]{:S(2)}, u32[]{:S(2)}) collective-permute-start(bf16[2,256,1024]{2,1,0:T(8,128)(2,1)} %get-tuple-element.27), channel_id=1, source_target_pairs={{1,2},{2,1},{3,4},{4,3},{5,6},{6,5},{7,8},{8,7},{9,10},{10,9},{11,... | collective-permute-start | bytes 3145736 | tf_op jit(solution)/shard_map/ppermute | solution.py:481
  84.8 15.4 %collective-permute-start.7 = (bf16[2,64,1024]{2,1,0:T(8,128)(2,1)}, bf16[2,64,1024]{2,1,0:T(8,128)(2,1)S(1)}, u32[]{:S(2)}, u32[]{:S(2)}) collective-permute-start(bf16[2,64,1024]{2,1,0:T(8,128)(2,1)} %get-tuple-element.29), channel_id=1, source_target_pairs={{1,3},{2,0},{3,5},{4,2},{5,7},{6,4},{7,9},{8,6},{9,11},{10,8},{11,... | collective-permute-start | bytes 786440 | tf_op jit(solution)/shard_map/ppermute | solution.py:482
  100.2 0.7 copy-start.7
  100.2 1.1 copy-start.3
  100.2 1.4 %copy-start.4 = (bf16[2,256,1024]{2,1,0:T(8,128)(2,1)}, bf16[2,256,1024]{2,1,0:T(8,128)(2,1)S(1)}, u32[]{:S(2)}) copy-start(bf16[2,256,1024]{2,1,0:T(8,128)(2,1)S(1)} %collective-permute-done.5.cross_ref) | copy-start | bytes 3145732

commit v2 on v1

v2 whole, which is shorter than its diff:
```python
import functools
import math

import jax
import jax.numpy as jnp
import numpy as np
from jax import lax
from jax.experimental import pallas as pl
from jax.experimental.pallas import tpu as pltpu
from jax.sharding import PartitionSpec as P

HD = 128
NB = 128
PAIR = 2 * NB
EDGE = 2 * NB
SCALE = 1.0 / math.sqrt(HD)
SCALE_LOG2 = SCALE * math.log2(math.e)
PENALTY = 1e30
BF = jnp.bfloat16
F32 = jnp.float32


def pool_matrix(rows, source_rows, pieces):
    matrix = np.zeros((rows, source_rows), np.float32)
    for first, count, source, factor in pieces:
        for row in range(count):
            start = source + row * factor
            matrix[first + row, start : start + factor] = 1.0 / factor
    return matrix


BLOCK_POOL = pool_matrix(64, 128, [(0, 64, 0, 2)])
NEAR_POOL = pool_matrix(128, 256, [(0, 64, 0, 2), (64, 32, 0, 4), (96, 32, 128, 2)])
FAR_POOL = pool_matrix(64, 256, [(0, 16, 0, 8), (16, 16, 128, 4), (32, 32, 192, 2)])
SPREAD = pool_matrix(
    576,
    512,
    [
        (0, 128, 0, 1),
        (128, 64, 128, 2),
        (192, 64, 256, 4),
        (256, 128, 384, 1),
        (384, 64, 256, 2),
        (448, 64, 0, 4),
        (512, 64, 0, 8),
    ],
).T
BLOCK_SPREAD = np.concatenate([BLOCK_POOL.T, BLOCK_POOL.T], axis=1)


def mm(a, b):
    return jnp.dot(a, b, preferred_element_type=F32)


def mm_nt(a, b):
    return lax.dot_general(a, b, (((1,), (1,)), ((), ())), preferred_element_type=F32)


def is_even():
    return lax.rem(lax.axis_index("ctx"), 2) == 0


def block(even, number):
    return pl.ds(pl.multiple_of(jnp.where(even, number, 3 - number) * NB, NB), NB)


def pool_kernel(k_ref, v_ref, cross_ref, inner_ref, far_ref):
    even = is_even()
    row = lax.broadcasted_iota(jnp.int32, (NB, NB), 0)
    col = lax.broadcasted_iota(jnp.int32, (NB, NB), 1)
    matrix = jnp.where(row == (col >> 1), 0.5, 0.0)
    matrix = jnp.where(row == (col >> 2) + 64, 0.25, matrix)
    matrix = jnp.where(row == (col >> 3) + 96, 0.125, matrix).astype(BF)
    for which, ref in enumerate((k_ref, v_ref)):
        pooled = [mm(matrix, ref[block(even, b), :]).astype(BF) for b in range(4)]
        cross_ref[which, :128] = ref[block(even, 0), :]
        cross_ref[which, 128:192] = pooled[1][:64]
        cross_ref[which, 192:224] = pooled[2][64:96]
        cross_ref[which, 224:] = pooled[3][64:96]
        inner_ref[which, :128] = ref[block(even, 3), :]
        inner_ref[which, 128:192] = pooled[2][:64]
        inner_ref[which, 192:224] = pooled[0][64:96]
        inner_ref[which, 224:] = pooled[1][64:96]
        for b in range(4):
            far_ref[which, b * 16 : (b + 1) * 16] = pooled[b][96:112]


def far_kernel(pool_ref, cross_ref, far_ref, out_ref):
    for which in range(2):
        out_ref[which, :64] = far_ref[which]
        out_ref[which, 64:] = mm(pool_ref[...], cross_ref[which]).astype(BF)


def fold_kernel(pool_ref, cross_ref, far_ref, got_ref, cross_out, far_out):
    for which in range(2):
        spread = mm(pool_ref[...], got_ref[which, 64:])
        cross_out[which] = (cross_ref[which].astype(F32) + spread).astype(BF)
        far_out[which] = (far_ref[which].astype(F32) + got_ref[which, :64].astype(F32)).astype(BF)


def final_kernel(spread_ref, cross_ref, inner_ref, far_ref, kg_ref, vg_ref, kg_out, vg_out):
    even = is_even()
    for which, (ref, out) in enumerate(((kg_ref, kg_out), (vg_ref, vg_out))):
        rows = jnp.concatenate([cross_ref[which], inner_ref[which], far_ref[which]], axis=0)
        spread = mm(spread_ref[...], rows)
        for b in range(4):
            at = block(even, b)
            out[at, :] = ref[at, :].astype(F32) + spread[b * NB : (b + 1) * NB]


NEAR_ROWS = (640, 832)
NEAR_CHUNKS = (
    ((0, 384, 0, "own"), (384, 512, 1, "own"), (512, 640, 2, "inner")),
    (
        (0, 384, 0, "own"),
        (384, 512, 0, "inner"),
        (512, 576, 1, "inner"),
        (576, 640, 1, "own"),
        (640, 704, 1, "inner"),
        (704, 768, 1, "own"),
        (768, 832, 2, "inner"),
    ),
)
NEAR_ADMIT = (
    (((0, 256), (384, 512), (512, 640)), ((0, 384), (448, 512), (512, 640))),
    (((0, 384), (512, 704), (768, 832)), ((128, 512), (576, 768), (768, 832))),
)
NEAR_ZEROS = (
    (((256, 384),), ((384, 448),)),
    (((384, 512), (704, 768)), ((0, 128), (512, 576))),
)
CROSS_ROWS = 640
CROSS_SPAN = ((0, 512), (256, 576))
CROSS_CHUNKS = (
    (
        (0, 128, 0, "cross"),
        (128, 192, 1, "cross"),
        (192, 256, 1, "cross"),
        (256, 320, 2, "cross"),
        (320, 384, 3, "far0"),
        (384, 448, 3, "far1"),
        (448, 512, 3, "far2"),
    ),
    (
        (256, 320, 2, "cross"),
        (320, 384, 3, "far0"),
        (384, 448, 3, "far1"),
        (448, 512, 3, "far2"),
        (512, 576, 2, "cross"),
    ),
)
CROSS_ADMIT = ((((0, 128), (192, 512)), ((128, 512),)), (((256, 576),), ((256, 576),)))
CROSS_ZEROS = ((((128, 192),), ((0, 128),)), ((), ()))


def overlap(chunk, ranges):
    for low, high in ranges:
        first, end = max(chunk[0], low), min(chunk[1], high)
        if first < end:
            return first, end
    return None


def fold_rows(x, op):
    return op(x.reshape(x.shape[0] // 8, 8, x.shape[1]), axis=0)


def lanes_of(blk):
    return slice(blk * NB, (blk + 1) * NB)


def penalties_of(devices):
    d = lax.axis_index("ctx")
    step = jnp.where(is_even(), 1, -1)

    def penalty(other):
        return jnp.where((other >= 0) & (other < devices), 0.0, PENALTY).astype(F32)

    return {
        "own": 0.0,
        "cross": penalty(d - step),
        "inner": penalty(d + step),
        "far0": penalty(d - 2 * step),
        "far1": penalty(d + 3 * step),
        "far2": penalty(d + 2 * step),
    }


def scores(chunks, admit, penalties, rows, q, s_ref):
    best = [None, None]
    for chunk in chunks:
        low, high, level, side = chunk
        s = mm_nt(rows[low:high], q)
        s_ref[low:high] = s
        for blk in range(2):
            part = overlap(chunk, admit[blk])
            if part is None:
                continue
            piece = s[part[0] - low : part[1] - low, lanes_of(blk)]
            top = fold_rows(piece, jnp.max) * SCALE_LOG2 + (level - penalties[side])
            best[blk] = top if best[blk] is None else jnp.maximum(best[blk], top)
    return jnp.concatenate([jnp.max(b, axis=0, keepdims=True) for b in best], axis=1)


def exponentials(chunks, admit, penalties, best, s_ref, p_ref, base):
    totals = []
    for blk in range(2):
        lanes = lanes_of(blk)
        total = jnp.zeros((8, NB), F32)
        for chunk in chunks:
            low, high, level, side = chunk
            part = overlap(chunk, admit[blk])
            if part is None:
                continue
            shift = best[:, lanes] - (level - penalties[side])
            prob = jnp.exp2(s_ref[part[0] : part[1], lanes] * SCALE_LOG2 - shift)
            total = total + fold_rows(prob, jnp.sum)
            p_ref[part[0] - base : part[1] - base, lanes] = prob.astype(BF)
        totals.append(jnp.sum(total, axis=0, keepdims=True))
    return jnp.concatenate(totals, axis=1)


def score_grads(chunks, admit, rows, g_t, inverse, delta, exp_ref, p_ref, ds_ref, base):
    for chunk in chunks:
        low, high, level, side = chunk
        dp = mm(rows[low:high], g_t)
        for blk in range(2):
            lanes = lanes_of(blk)
            part = overlap(chunk, admit[blk])
            if part is None:
                continue
            here = slice(part[0] - base, part[1] - base)
            piece = dp[part[0] - low : part[1] - low, lanes]
            prob = exp_ref[here, lanes].astype(F32) * inverse[:, lanes]
            p_ref[here, lanes] = prob.astype(BF)
            ds_ref[here, lanes] = (prob * (piece - delta[:, lanes])).astype(BF)


def put_zeros(zeros, base, *refs):
    for ref in refs:
        for blk in range(2):
            for low, high in zeros[blk]:
                ref[low - base : high - base, lanes_of(blk)] = jnp.zeros((high - low, NB), BF)


def lay_near(even, which, own, inner_ref, pool_ref, near_ref, a, b):
    inner = inner_ref[which]
    near = mm(near_ref[...], inner).astype(BF)
    tokens = [own[block(even, i), :] for i in range(4)]
    halves = [mm(pool_ref[...], t).astype(BF) for t in tokens]
    a[:128] = tokens[0]
    a[128:256] = tokens[1]
    a[256:384] = tokens[2]
    a[384:448] = halves[2]
    a[448:512] = halves[3]
    a[512:576] = near[64:]
    a[576:640] = inner[192:]
    b[:128] = tokens[1]
    b[128:256] = tokens[2]
    b[256:384] = tokens[3]
    b[384:512] = inner[:128]
    b[512:576] = near[:64]
    b[576:640] = halves[0]
    b[640:704] = inner[128:192]
    b[704:768] = halves[1]
    b[768:832] = inner[192:]


STEP = 2
WIDE = STEP * HD
UNITS = tuple((head, pair) for head in range(STEP) for pair in range(2))


def two(even, ref, pair, head):
    lanes = lanes_of(head)
    return jnp.concatenate(
        [ref[block(even, 2 * pair), lanes], ref[block(even, 2 * pair + 1), lanes]], axis=0
    )


def put_two(even, ref, pair, head, rows):
    ref[block(even, 2 * pair), lanes_of(head)] = rows[:NB]
    ref[block(even, 2 * pair + 1), lanes_of(head)] = rows[NB:]


def staggered(*stages):
    for time in range(len(UNITS) + len(stages) - 1):
        for lag, stage in enumerate(stages):
            if 0 <= time - lag < len(UNITS):
                stage(*UNITS[time - lag])


def columns(pair):
    return slice(pair * PAIR, (pair + 1) * PAIR)


def first_kernel(
    devices,
    pool_ref,
    near_ref,
    q_ref,
    k_ref,
    v_ref,
    inner_ref,
    pa_ref,
    pb_ref,
    out_ref,
    stat_ref,
    ka_ref,
    kb_ref,
    va_ref,
    vb_ref,
    s_ref,
):
    even = is_even()
    penalties = penalties_of(devices)
    lay_near(even, 0, k_ref, inner_ref, pool_ref, near_ref, ka_ref, kb_ref)
    lay_near(even, 1, v_ref, inner_ref, pool_ref, near_ref, va_ref, vb_ref)
    keys, values, exps = (ka_ref, kb_ref), (va_ref, vb_ref), (pa_ref, pb_ref)
    best = {}

    def score(head, pair):
        best[head, pair] = scores(
            NEAR_CHUNKS[pair],
            NEAR_ADMIT[pair],
            penalties,
            keys[pair].at[:, lanes_of(head)],
            two(even, q_ref, pair, head),
            s_ref.at[head, pair],
        )

    def exponential(head, pair):
        p = exps[pair].at[head]
        put_zeros(NEAR_ZEROS[pair], 0, p)
        total = exponentials(
            NEAR_CHUNKS[pair],
            NEAR_ADMIT[pair],
            penalties,
            best[head, pair],
            s_ref.at[head, pair],
            p,
            0,
        )
        stat_ref[head, 0:1, columns(pair)] = best[head, pair]
        stat_ref[head, 1:2, columns(pair)] = total

    def attend(head, pair):
        cols = values[pair][:, lanes_of(head)].T
        out_ref[head, :, columns(pair)] = mm(cols, exps[pair][head])

    staggered(score, exponential, attend)


def cross_kernel(
    devices,
    near_ref,
    near_t_ref,
    q_ref,
    g_ref,
    cross_ref,
    far_ref,
    swap_ref,
    sum_ref,
    stat_ref,
    att_ref,
    dq_ref,
    stat_out,
    crossg_ref,
    farg_ref,
    swapg_ref,
    k_ref,
    v_ref,
    s_ref,
    p_ref,
    ds_ref,
):
    even = is_even()
    penalties = penalties_of(devices)

    @pl.when(pl.program_id(0) == 0)
    def _():
        for head, pair in UNITS:
            base = CROSS_SPAN[pair][0]
            put_zeros(CROSS_ZEROS[pair], base, p_ref.at[head, pair], ds_ref.at[head, pair])

    for which, rows in enumerate((k_ref, v_ref)):
        cross = cross_ref[which]
        near = mm(near_ref[...], cross).astype(BF)
        rows[:128] = cross[:128]
        rows[128:192] = near[:64]
        rows[192:256] = cross[128:192]
        rows[256:320] = cross[192:]
        rows[320:384] = far_ref[which]
        rows[384:512] = swap_ref[which]
        rows[512:576] = near[64:]
        rows[576:] = jnp.zeros((64, WIDE), BF)
    state = {}
    grads = {}

    def score(head, pair):
        best = scores(
            CROSS_CHUNKS[pair],
            CROSS_ADMIT[pair],
            penalties,
            k_ref.at[:, lanes_of(head)],
            two(even, q_ref, pair, head),
            s_ref.at[head, pair],
        )
        state[head, pair] = jnp.maximum(best, stat_ref[head, 0:1, columns(pair)])

    def exponential(head, pair):
        best = state[head, pair]
        total = exponentials(
            CROSS_CHUNKS[pair],
            CROSS_ADMIT[pair],
            penalties,
            best,
            s_ref.at[head, pair],
            p_ref.at[head, pair],
            CROSS_SPAN[pair][0],
        )
        factor = jnp.exp2(stat_ref[head, 0:1, columns(pair)] - best)
        inverse = 1.0 / (total + stat_ref[head, 1:2, columns(pair)] * factor)
        state[head, pair] = factor, inverse

    def attend(head, pair):
        base, end = CROSS_SPAN[pair]
        factor, inverse = state[head, pair]
        cols = v_ref[base:end, lanes_of(head)].T
        new = mm(cols, p_ref[head, pair, : end - base])
        out_t = (sum_ref[head, :, columns(pair)] * factor + new) * inverse
        put_two(even, att_ref, pair, head, out_t.T.astype(BF))
        g_t = two(even, g_ref, pair, head).T
        delta = jnp.sum(out_t * g_t.astype(F32), axis=0, keepdims=True)
        stat_out[head, 0:1, columns(pair)] = inverse * factor
        stat_out[head, 1:2, columns(pair)] = delta
        state[head, pair] = inverse, delta, g_t

    def differentiate(head, pair):
        inverse, delta, g_t = state[head, pair]
        p = p_ref.at[head, pair]
        score_grads(
            CROSS_CHUNKS[pair],
            CROSS_ADMIT[pair],
            v_ref.at[:, lanes_of(head)],
            g_t,
            inverse,
            delta,
            p,
            p,
            ds_ref.at[head, pair],
            CROSS_SPAN[pair][0],
        )

    def multiply(head, pair):
        base, end = CROSS_SPAN[pair]
        ds = ds_ref[head, pair, : end - base]
        cols = k_ref[base:end, lanes_of(head)].T
        dq_ref[head, :, columns(pair)] = mm(cols, ds)
        grads[head, pair] = (
            mm(ds, two(even, q_ref, pair, head)) * SCALE,
            mm(p_ref[head, pair, : end - base], two(even, g_ref, pair, head)),
        )

    staggered(score, exponential, attend, differentiate, multiply)
    for head in range(STEP):
        lanes = lanes_of(head)
        for which in range(2):
            a = grads[head, 0][which]
            b = grads[head, 1][which]
            near = jnp.concatenate([a[128:192], b[256:320]], axis=0).astype(BF)
            edge = jnp.concatenate([a[:128], a[192:256], a[256:320] + b[:64]], axis=0)
            crossg_ref[which, :, lanes] = (edge + mm(near_t_ref[...], near)).astype(BF)
            far = (a[320:512] + b[64:256]).astype(BF)
            farg_ref[which, :, lanes] = far[:64]
            swapg_ref[which, :, lanes] = far[64:]


def last_kernel(
    pool_ref,
    near_ref,
    near_t_ref,
    spread_ref,
    q_ref,
    k_ref,
    v_ref,
    g_ref,
    inner_ref,
    pa_ref,
    pb_ref,
    stat_ref,
    dqt_ref,
    dq_ref,
    kg_ref,
    vg_ref,
    innerg_ref,
    ka_ref,
    kb_ref,
    va_ref,
    vb_ref,
    wa_ref,
    wb_ref,
    dsa_ref,
    dsb_ref,
):
    even = is_even()

    @pl.when(pl.program_id(0) == 0)
    def _():
        for head in range(STEP):
            put_zeros(NEAR_ZEROS[0], 0, wa_ref.at[head], dsa_ref.at[head])
            put_zeros(NEAR_ZEROS[1], 0, wb_ref.at[head], dsb_ref.at[head])

    lay_near(even, 0, k_ref, inner_ref, pool_ref, near_ref, ka_ref, kb_ref)
    lay_near(even, 1, v_ref, inner_ref, pool_ref, near_ref, va_ref, vb_ref)
    keys, values, exps = (ka_ref, kb_ref), (va_ref, vb_ref), (pa_ref, pb_ref)
    weights, logits = (wa_ref, wb_ref), (dsa_ref, dsb_ref)
    grads = {}

    def differentiate(head, pair):
        score_grads(
            NEAR_CHUNKS[pair],
            NEAR_ADMIT[pair],
            values[pair].at[:, lanes_of(head)],
            two(even, g_ref, pair, head).T,
            stat_ref[head, 0:1, columns(pair)],
            stat_ref[head, 1:2, columns(pair)],
            exps[pair].at[head],
            weights[pair].at[head],
            logits[pair].at[head],
            0,
        )

    def multiply(head, pair):
        ds = logits[pair][head]
        cols = keys[pair][:, lanes_of(head)].T
        dq_t = (dqt_ref[head, :, columns(pair)] + mm(cols, ds)) * SCALE
        put_two(even, dq_ref, pair, head, dq_t.T)
        grads[head, pair] = (
            mm(ds, two(even, q_ref, pair, head)) * SCALE,
            mm(weights[pair][head], two(even, g_ref, pair, head)),
        )

    def collect(head, pair):
        if pair == 0:
            return
        lanes = lanes_of(head)
        for which, out in enumerate((kg_ref, vg_ref)):
            a = grads[head, 0][which]
            b = grads[head, 1][which]
            tokens = (a[:128], a[128:256] + b[:128], a[256:384] + b[128:256], b[256:384])
            halves = (b[576:640], b[704:768], a[384:448], a[448:512])
            for i in range(4):
                high = halves[i].astype(BF)
                low = (halves[i] - high.astype(F32)).astype(BF)
                spread = mm(spread_ref[...], jnp.concatenate([high, low], axis=0))
                out[block(even, i), lanes] = (tokens[i] + spread).astype(BF)
            near = jnp.concatenate([b[512:576], a[512:576]], axis=0).astype(BF)
            edge = jnp.concatenate([b[384:512], b[640:704], a[576:640] + b[768:832]], axis=0)
            innerg_ref[which, :, lanes] = (edge + mm(near_t_ref[...], near)).astype(BF)

    staggered(differentiate, multiply, collect)


CORE_VMEM = 32 * 2**20
SIDE_VMEM = 16 * 2**20


def params(limit=SIDE_VMEM):
    return pltpu.CompilerParams(vmem_limit_bytes=limit)


def cost(flops, moved):
    return pl.CostEstimate(flops=int(flops), bytes_accessed=int(moved), transcendentals=0)


def whole(shape):
    return pl.BlockSpec(shape, lambda i: (0,) * len(shape))


def part(rows, width, first=0):
    return pl.BlockSpec((rows, width), lambda i: (0, first + i))


def duo(rows, width, first=0):
    return pl.BlockSpec((2, rows, width), lambda i: (0, 0, first + i))


def per_head(rows, width, first=0):
    return pl.BlockSpec((STEP, rows, width), lambda i: (first + i, 0, 0))


def constant(matrix):
    return jnp.asarray(matrix, BF)


def shaped(*shape, dtype=BF):
    return jax.ShapeDtypeStruct(shape, dtype)


def swap_pairs(n):
    return [(i, i ^ 1) for i in range(n)]


def in_range(pairs, n):
    return [(i, j) for i, j in pairs if 0 <= j < n]


def cross_pairs(n):
    return in_range([(i, i + 1 if i % 2 else i - 1) for i in range(n)], n)


def far_pairs(n):
    return in_range([(i, i - 2 if i % 2 else i + 2) for i in range(n)], n)


def back_pairs(n):
    return in_range([(i, i + 2 if i % 2 else i - 2) for i in range(n)], n)


def call_pool(keys, values):
    tok, lanes = keys.shape
    width = 256
    return pl.pallas_call(
        pool_kernel,
        grid=(lanes // width,),
        in_specs=[part(tok, width), part(tok, width)],
        out_specs=[duo(EDGE, width), duo(EDGE, width), duo(64, width)],
        out_shape=[shaped(2, EDGE, lanes), shaped(2, EDGE, lanes), shaped(2, 64, lanes)],
        compiler_params=params(60 * 2**20),
        cost_estimate=cost(1e9, 5 * tok * lanes * 2),
        name="pool",
    )(keys, values)


def call_far(cross, far):
    lanes = cross.shape[2]
    width = lanes
    return pl.pallas_call(
        far_kernel,
        grid=(lanes // width,),
        in_specs=[whole((64, 256)), duo(EDGE, width), duo(64, width)],
        out_specs=duo(128, width),
        out_shape=shaped(2, 128, lanes),
        compiler_params=params(),
        cost_estimate=cost(1e9, 2 * 448 * lanes * 2),
        name="far",
    )(constant(FAR_POOL), cross, far)


def call_first(n, queries, keys, values, inner):
    tok, lanes = queries.shape
    heads = lanes // HD
    fixed = [constant(m) for m in (BLOCK_POOL, NEAR_POOL)]
    return pl.pallas_call(
        functools.partial(first_kernel, n),
        grid=(heads // STEP,),
        in_specs=[whole(m.shape) for m in fixed] + [part(tok, WIDE)] * 3 + [duo(EDGE, WIDE)],
        out_specs=[
            per_head(NEAR_ROWS[0], PAIR),
            per_head(NEAR_ROWS[1], PAIR),
            per_head(HD, tok),
            per_head(8, tok),
        ],
        out_shape=[
            shaped(heads, NEAR_ROWS[0], PAIR),
            shaped(heads, NEAR_ROWS[1], PAIR),
            shaped(heads, HD, tok, dtype=F32),
            shaped(heads, 8, tok, dtype=F32),
        ],
        scratch_shapes=[pltpu.VMEM((rows, WIDE), BF) for rows in NEAR_ROWS * 2]
        + [pltpu.VMEM((STEP, 2, NEAR_ROWS[1], PAIR), F32)],
        compiler_params=params(CORE_VMEM),
        cost_estimate=cost(heads * 1.5e9, 20 * tok * lanes),
        name="first",
    )(*fixed, queries, keys, values, inner)


def call_cross(n, queries, out_grad, cross, far, swap, sums, stats):
    tok, lanes = queries.shape
    heads = lanes // HD
    fixed = [constant(m) for m in (NEAR_POOL, NEAR_POOL.T)]
    return pl.pallas_call(
        functools.partial(cross_kernel, n),
        grid=(heads // STEP,),
        in_specs=[whole(m.shape) for m in fixed]
        + [part(tok, WIDE)] * 2
        + [duo(EDGE, WIDE), duo(64, WIDE), duo(128, WIDE), per_head(HD, tok), per_head(8, tok)],
        out_specs=[
            part(tok, WIDE),
            per_head(HD, tok),
            per_head(8, tok),
            duo(EDGE, WIDE),
            duo(64, WIDE),
            duo(128, WIDE),
        ],
        out_shape=[
            shaped(tok, lanes),
            shaped(heads, HD, tok, dtype=F32),
            shaped(heads, 8, tok, dtype=F32),
            shaped(2, EDGE, lanes),
            shaped(2, 64, lanes),
            shaped(2, 128, lanes),
        ],
        scratch_shapes=[
            pltpu.VMEM((CROSS_ROWS, WIDE), BF),
            pltpu.VMEM((CROSS_ROWS, WIDE), BF),
            pltpu.VMEM((STEP, 2, CROSS_ROWS, PAIR), F32),
            pltpu.VMEM((STEP, 2, 512, PAIR), BF),
            pltpu.VMEM((STEP, 2, 512, PAIR), BF),
        ],
        compiler_params=params(CORE_VMEM),
        cost_estimate=cost(heads * 1.5e9, 20 * tok * lanes),
        name="cross",
    )(*fixed, queries, out_grad, cross, far, swap, sums, stats)


def call_last(arrays, inner, pa, pb, stats, dqt, group, earlier):
    start, heads = group
    first = start // STEP
    tok, feat = arrays[0].shape
    lanes = heads * HD
    taken = [] if earlier is None else [earlier]
    fixed = [constant(m) for m in (BLOCK_POOL, NEAR_POOL, NEAR_POOL.T, BLOCK_SPREAD)]

    def kernel(*refs):
        last_kernel(*refs[:13], *refs[13 + len(taken) :])

    return pl.pallas_call(
        kernel,
        grid=(heads // STEP,),
        in_specs=[whole(m.shape) for m in fixed]
        + [part(tok, WIDE, first)] * 4
        + [
            duo(EDGE, WIDE, first),
            per_head(NEAR_ROWS[0], PAIR, first),
            per_head(NEAR_ROWS[1], PAIR, first),
            per_head(8, tok, first),
            per_head(HD, tok, first),
        ]
        + [pl.BlockSpec(memory_space=pl.ANY)] * len(taken),
        out_specs=[part(tok, WIDE, first), part(tok, WIDE), part(tok, WIDE), duo(EDGE, WIDE)],
        out_shape=[
            shaped(tok, feat, dtype=F32),
            shaped(tok, lanes),
            shaped(tok, lanes),
            shaped(2, EDGE, lanes),
        ],
        scratch_shapes=[pltpu.VMEM((rows, WIDE), BF) for rows in NEAR_ROWS * 2]
        + [pltpu.VMEM((STEP, rows, PAIR), BF) for rows in NEAR_ROWS * 2],
        input_output_aliases={13 + i: i for i in range(len(taken))},
        compiler_params=params(CORE_VMEM),
        cost_estimate=cost(heads * 1.5e9, 20 * tok * lanes),
        name="last",
    )(*fixed, *arrays, inner, pa, pb, stats, dqt, *taken)


def call_fold(cross, far, got):
    lanes = cross.shape[2]
    width = lanes
    return pl.pallas_call(
        fold_kernel,
        grid=(lanes // width,),
        in_specs=[whole((256, 64)), duo(EDGE, width), duo(64, width), duo(128, width)],
        out_specs=[duo(EDGE, width), duo(64, width)],
        out_shape=[shaped(2, EDGE, lanes), shaped(2, 64, lanes)],
        compiler_params=params(),
        cost_estimate=cost(1e9, 2 * 768 * lanes * 2),
        name="fold",
    )(constant(FAR_POOL.T), cross, far, got)


def call_final(cross, inner, far, kg, vg, feat, group, earlier):
    first, heads = group
    tok, lanes = kg.shape
    width = 256
    offset = first * HD // width
    taken = [] if earlier is None else list(earlier)

    def kernel(*refs):
        final_kernel(*refs[:6], *refs[6 + len(taken) :])

    return pl.pallas_call(
        kernel,
        grid=(lanes // width,),
        in_specs=[
            whole((512, 576)),
            duo(EDGE, width, offset),
            duo(EDGE, width),
            duo(64, width, offset),
        ]
        + [part(tok, width)] * 2
        + [pl.BlockSpec(memory_space=pl.ANY)] * len(taken),
        out_specs=[part(tok, width, offset)] * 2,
        out_shape=[shaped(tok, feat, dtype=F32)] * 2,
        input_output_aliases={6 + i: i for i in range(len(taken))},
        compiler_params=params(),
        cost_estimate=cost(2e9, 16 * tok * lanes),
        name="final",
    )(constant(SPREAD), cross, inner, far, kg, vg, *taken)


GROUPS = ((0, 4), (4, 4))


def body(queries, keys, values, out_grad):
    feat = queries.shape[1]
    n = lax.axis_size("ctx")
    send = functools.partial(lax.ppermute, axis_name="ctx")
    cross, inner, far = call_pool(keys, values)
    cross = send(cross, perm=cross_pairs(n))
    far = send(far, perm=far_pairs(n))
    inner = send(inner, perm=swap_pairs(n))
    pa, pb, sums, stats = call_first(n, queries, keys, values, inner)
    cross, far, stats = lax.optimization_barrier((cross, far, stats))
    swap = send(call_far(cross, far), perm=swap_pairs(n))
    att, dqt, stats, cross_g, far_g, swap_g = call_cross(
        n, queries, out_grad, cross, far, swap, sums, stats
    )
    cross_g, far_g = call_fold(cross_g, far_g, send(swap_g, perm=swap_pairs(n)))
    cross_g, far_g, stats = lax.optimization_barrier((cross_g, far_g, stats))
    cross_g = send(cross_g, perm=cross_pairs(n))
    far_g = send(far_g, perm=back_pairs(n))
    arrays = (queries, keys, values, out_grad)
    dq = None
    parts = []
    for number, group in enumerate(GROUPS):
        if number == 1:
            far_g, stats = lax.optimization_barrier((far_g, stats))
        dq, kg, vg, inner_g = call_last(arrays, inner, pa, pb, stats, dqt, group, dq)
        parts.append((send(inner_g, perm=swap_pairs(n)), kg, vg))
    grads = None
    for group, (inner_g, kg, vg) in zip(GROUPS, parts):
        grads = call_final(cross_g, inner_g, far_g, kg, vg, feat, group, grads)
    return att, dq, *grads


def solution(mesh):
    spec = P("ctx", None)
    return jax.shard_map(
        body,
        mesh=mesh,
        in_specs=(spec, spec, spec, spec),
        out_specs=(spec, spec, spec, spec),
        check_vma=False,
    )
```

time: 110 us -> 79.5 us (0.72); the launches traced: 108 us -> 79.2 us
  waiting for transfers between devices: 30.7 us -> 14.2 us
  Pallas kernels: 50.8 us -> 39.4 us
  local copies, waits for them, and re-layouts: 4.66 us -> 0.06 us
  starting transfers between devices: 21.6 us -> 24.7 us
    ppermute x8 -> x9, waiting for transfers between devices: 30.7 us -> 14.2 us  [the longest x1 6.24 us: body(): cross = send(cross, perm=cross_pairs(n))]
    pallas_call x5 -> x9, Pallas kernels: 50.8 us -> 39.4 us  [the longest x2 12.3 us: call_last(): pl.pallas_call(kernel, grid=(heads // STEP,), in_specs=[whole(m.shape) fo...]
    unnamed x16 -> x22, local copies, waits for them, and re-layouts: 4.66 us -> 0.06 us
    ppermute x8 -> x9, starting transfers between devices: 21.6 us -> 24.7 us  [the longest x1 9.4 us: body(): cross = send(cross, perm=cross_pairs(n))]
  transfers between devices with their start and end apart: 8 -> 9, of which waited for: 4 -> 4; matrix products, arithmetic and copies ran while one was open for 0% -> 0% of each run, Pallas kernels for 7% -> 27%
where the time goes in v2:
time: 79.5 us; the launch traced here: 79.2 us
  Pallas kernels  39.4 us (50%)
  starting transfers between devices  24.7 us (31%)
  waiting for transfers between devices  14.2 us (18%)
  between operations  0.83 us (1%)
    pallas_call x2, Pallas kernels, call_last(): pl.pallas_call(kernel, grid=(heads // STEP,), in_specs=[whole(m.shape) fo...  12.3 us
    pallas_call x1, Pallas kernels, call_cross(): pl.pallas_call(functools.partial(cross_kernel, n), grid=(heads // STEP,),...  10.5 us
    ppermute x1, starting transfers between devices, body(): cross = send(cross, perm=cross_pairs(n))  9.4 us
    ppermute x1, starting transfers between devices, body(): far_g = send(far_g, perm=back_pairs(n))  7.13 us
    pallas_call x1, Pallas kernels, call_first(): pl.pallas_call(functools.partial(first_kernel, n), grid=(heads // STEP,),...  6.68 us
    ppermute x1, waiting for transfers between devices, body(): cross = send(cross, perm=cross_pairs(n))  6.24 us
    ppermute x1, waiting for transfers between devices, body(): cross_g = send(cross_g, perm=cross_pairs(n))  4.87 us
    pallas_call x2, Pallas kernels, call_final(): pl.pallas_call(kernel, grid=(lanes // width,), in_specs=[whole((512, 576)...  4.72 us
  transfers between devices with their start and end apart: 9, of which 4 were waited for; matrix products, arithmetic and copies ran while one was open for 0% of the time, Pallas kernels for 27%

profile of v2, /device:TPU:6, one launch (start us, length us, event | category | flops | bytes accessed | tf_op | source)
XLA Modules:
  0.0 79.2 jit_solution(2497230732069757543)
XLA Ops:
  0.6 0.0 copy-start.5
  0.6 0.0 copy-start.10
  0.7 0.0 copy-start.4
  0.7 0.0 copy-start.3
  0.7 0.0 copy-start.1
  0.7 4.4 %pool.1 = (bf16[2,256,1024]{2,1,0:T(8,128)(2,1)}, bf16[2,256,1024]{2,1,0:T(8,128)(2,1)}, bf16[2,64,1024]{2,1,0:T(8,128)(2,1)}) custom-call(bf16[512,1024]{1,0:T(8,128)(2,1)} %refs_5_.3, bf16[512,1024]{1,0:T(8,128)(2,1)} %refs_6_.3), custom_call_target="tpu_custom_call" | custom-call | flops 1000000000 | bytes 5242880 | tf_op jit(solution)/shard_map/pool/pallas_call | solution.py:624
  5.1 0.0 collective-permute-start.2
  5.1 3.8 %collective-permute-start.1 = (bf16[2,64,1024]{2,1,0:T(8,128)(2,1)}, bf16[2,64,1024]{2,1,0:T(8,128)(2,1)S(1)}, u32[]{:S(2)}, u32[]{:S(2)}) collective-permute-start(bf16[2,64,1024]{2,1,0:T(8,128)(2,1)} %get-tuple-element.40), channel_id=1, source_target_pairs={{0,2},{2,4},{3,1},{4,6},{5,3},{6,8},{7,5},{8,10},{9,7},{10,12},{11... | collective-permute-start | bytes 786440 | tf_op jit(solution)/shard_map/ppermute | solution.py:812
  8.9 0.0 copy-start.9
  9.0 9.4 %collective-permute-start = (bf16[2,256,1024]{2,1,0:T(8,128)(2,1)}, bf16[2,256,1024]{2,1,0:T(8,128)(2,1)S(1)}, u32[]{:S(2)}, u32[]{:S(2)}) collective-permute-start(bf16[2,256,1024]{2,1,0:T(8,128)(2,1)} %get-tuple-element.39), channel_id=1, source_target_pairs={{1,2},{2,1},{3,4},{4,3},{5,6},{6,5},{7,8},{8,7},{9,10},{10,9},{11,... | collective-permute-start | bytes 3145736 | tf_op jit(solution)/shard_map/ppermute | solution.py:811
  18.4 0.0 collective-permute-done.2.inner_ref.refs_8_
  18.4 0.0 copy-done.5
  18.4 0.0 copy-done.10
  18.4 0.0 copy-done.4
  18.4 0.0 copy-done.3
  18.4 0.0 copy-done.1
  18.4 6.7 %first.1 = (bf16[8,640,256]{2,1,0:T(8,128)(2,1)S(1)}, bf16[8,832,256]{2,1,0:T(8,128)(2,1)S(1)}, f32[8,128,512]{2,1,0:T(8,128)S(1)}, f32[8,8,512]{2,1,0:T(8,128)S(1)}) custom-call(bf16[64,128]{1,0:T(8,128)(2,1)S(1)} %copy-done.10, bf16[128,256]{1,0:T(8,128)(2,1)S(1)} %copy-done.5, bf16[512,1024]{1,0:T(8,128)(2,1)S(1)} %copy-done.1, ...), custom_call_target="tpu_custom_call" | custom-call | flops 12000000000 | bytes 10485760 | tf_op jit(solution)/shard_map/first/pallas_call | solution.py:655
  25.1 0.0 copy-start.2
  25.1 0.0 copy-start.6
  25.1 0.0 collective-permute-done.1.far_ref
  25.1 6.2 %collective-permute-done.cross_ref = bf16[2,256,1024]{2,1,0:T(8,128)(2,1)S(1)} collective-permute-done((bf16[2,256,1024]{2,1,0:T(8,128)(2,1)}, bf16[2,256,1024]{2,1,0:T(8,128)(2,1)S(1)}, u32[]{:S(2)}, u32[]{:S(2)}) %collective-permute-start) | collective-permute-done | bytes 1048608 | tf_op jit(solution)/shard_map/ppermute | solution.py:811
  31.4 0.0 copy-done.9
  31.4 0.3 far.1
  31.7 0.9 %collective-permute-start.3 = (bf16[2,128,1024]{2,1,0:T(8,128)(2,1)S(1)}, bf16[2,128,1024]{2,1,0:T(8,128)(2,1)S(1)}, u32[]{:S(2)}, u32[]{:S(2)}) collective-permute-start(bf16[2,128,1024]{2,1,0:T(8,128)(2,1)S(1)} %far.1), channel_id=1, source_target_pairs={{0,1},{1,0},{2,3},{3,2},{4,5},{5,4},{6,7},{7,6},{8,9},{9,8},{10,11... | collective-permute-start | bytes 1572872 | tf_op jit(solution)/shard_map/ppermute | solution.py:816
  32.6 1.5 %collective-permute-done.3.swap_ref = bf16[2,128,1024]{2,1,0:T(8,128)(2,1)S(1)} collective-permute-done((bf16[2,128,1024]{2,1,0:T(8,128)(2,1)S(1)}, bf16[2,128,1024]{2,1,0:T(8,128)(2,1)S(1)}, u32[]{:S(2)}, u32[]{:S(2)}) %collective-permute-start.3) | collective-permute-done | bytes 524320 | tf_op jit(solution)/shard_map/ppermute | solution.py:816
  34.1 0.0 copy-done.2
  34.1 0.0 copy-done.6
  34.1 0.0 copy-start.7
  34.1 10.5 %cross.1 = (bf16[512,1024]{1,0:T(8,128)(2,1)}, f32[8,128,512]{2,1,0:T(8,128)S(1)}, f32[8,8,512]{2,1,0:T(8,128)S(1)}, bf16[2,256,1024]{2,1,0:T(8,128)(2,1)S(1)}, ...) custom-call(bf16[128,256]{1,0:T(8,128)(2,1)S(1)} %copy-done.5, bf16[256,128]{1,0:T(8,128)(2,1)S(1)} %copy-done.6, ...), custom_call_target="tpu_custom_call" | custom-call | flops 12000000000 | bytes 10485760 | tf_op jit(solution)/shard_map/cross/pallas_call | solution.py:683
  44.6 0.0 copy-start.8
  44.6 0.4 collective-permute-start.4
  45.0 1.5 %collective-permute-done.4.got_ref = bf16[2,128,1024]{2,1,0:T(8,128)(2,1)S(1)} collective-permute-done((bf16[2,128,1024]{2,1,0:T(8,128)(2,1)S(1)}, bf16[2,128,1024]{2,1,0:T(8,128)(2,1)S(1)}, u32[]{:S(2)}, u32[]{:S(2)}) %collective-permute-start.4) | collective-permute-done | bytes 524320 | tf_op jit(solution)/shard_map/ppermute | solution.py:820
  46.6 0.0 copy-done.7
  46.6 0.4 fold.1
  47.0 7.1 %collective-permute-start.5 = (bf16[2,64,1024]{2,1,0:T(8,128)(2,1)S(1)}, bf16[2,64,1024]{2,1,0:T(8,128)(2,1)S(1)}, u32[]{:S(2)}, u32[]{:S(2)}) collective-permute-start(bf16[2,64,1024]{2,1,0:T(8,128)(2,1)S(1)} %get-tuple-element.56), channel_id=1, source_target_pairs={{1,3},{2,0},{3,5},{4,2},{5,7},{6,4},{7,9},{8,6},{9,11},{10,8},{11,... | collective-permute-start | bytes 786440 | tf_op jit(solution)/shard_map/ppermute | solution.py:823
  54.2 2.6 %collective-permute-start.6 = (bf16[2,256,1024]{2,1,0:T(8,128)(2,1)S(1)}, bf16[2,256,1024]{2,1,0:T(8,128)(2,1)S(1)}, u32[]{:S(2)}, u32[]{:S(2)}) collective-permute-start(bf16[2,256,1024]{2,1,0:T(8,128)(2,1)S(1)} %get-tuple-element.62), channel_id=1, source_target_pairs={{1,2},{2,1},{3,4},{4,3},{5,6},{6,5},{7,8},{8,7},{9,10},{10,9},{11,... | collective-permute-start | bytes 3145736 | tf_op jit(solution)/shard_map/ppermute | solution.py:822
  56.8 0.0 copy-done.8
  56.8 6.2 %last.2 = (f32[512,1024]{1,0:T(8,128)}, bf16[512,512]{1,0:T(8,128)(2,1)S(1)}, bf16[512,512]{1,0:T(8,128)(2,1)S(1)}, bf16[2,256,512]{2,1,0:T(8,128)(2,1)S(1)}) custom-call(bf16[64,128]{1,0:T(8,128)(2,1)S(1)} %copy-done.10, bf16[128,256]{1,0:T(8,128)(2,1)S(1)} %copy-done.5, bf16[256,128]{1,0:T(8,128)(2,1)S(1)} %copy-done.6, bf16[128,128]{1,0:T(8,128)(2,1)S(1)} %copy-done.8, ...), custom_call_target="tpu_custom_call" | custom-call | flops 6000000000 | bytes 5242880 | tf_op jit(solution)/shard_map/last/pallas_call | solution.py:729
  63.0 0.0 collective-permute-start.8
  63.0 0.0 collective-permute-done.5.refs_3_
  63.0 6.2 %last.3 = (f32[512,1024]{1,0:T(8,128)}, bf16[512,512]{1,0:T(8,128)(2,1)S(1)}, bf16[512,512]{1,0:T(8,128)(2,1)S(1)}, bf16[2,256,512]{2,1,0:T(8,128)(2,1)S(1)}) custom-call(bf16[64,128]{1,0:T(8,128)(2,1)S(1)} %copy-done.10, bf16[128,256]{1,0:T(8,128)(2,1)S(1)} %copy-done.5, bf16[256,128]{1,0:T(8,128)(2,1)S(1)} %copy-done.6, ...), custom_call_target="tpu_custom_call", output_to_operand_aliasing={{0}: (13, {})} | custom-call | flops 6000000000 | bytes 5242880 | tf_op jit(solution)/shard_map/last/pallas_call | solution.py:729
  69.2 0.5 collective-permute-start.7
  69.6 0.0 collective-permute-done.8.refs_2_
  69.6 4.9 %collective-permute-done.6.refs_1_ = bf16[2,256,1024]{2,1,0:T(8,128)(2,1)S(1)} collective-permute-done((bf16[2,256,1024]{2,1,0:T(8,128)(2,1)S(1)}, bf16[2,256,1024]{2,1,0:T(8,128)(2,1)S(1)}, u32[]{:S(2)}, u32[]{:S(2)}) %collective-permute-start.6) | collective-permute-done | bytes 1048608 | tf_op jit(solution)/shard_map/ppermute | solution.py:822
  74.5 0.0 copy-done
  74.5 2.4 %final.2 = (f32[512,1024]{1,0:T(8,128)}, f32[512,1024]{1,0:T(8,128)}) custom-call(bf16[512,576]{1,0:T(8,128)(2,1)S(1)} %copy-done, bf16[2,256,1024]{2,1,0:T(8,128)(2,1)S(1)} %collective-permute-done.6.refs_1_, bf16[2,256,512]{2,1,0:T(8,128)(2,1)S(1)} %collective-permute-done.8.refs_2_, bf16[2,64,1024]{2,1,0:T(8,128)(2,1)S(1)} %collective-permute-done.5.refs_3_, ...), custom_call_target="tpu_custom_call" | custom-call | flops 2000000000 | bytes 4194304 | tf_op jit(solution)/shard_map/final/pallas_call | solution.py:783
  76.9 0.0 collective-permute-done.7.refs_2_
  76.9 2.4 %final.3 = (f32[512,1024]{1,0:T(8,128)}, f32[512,1024]{1,0:T(8,128)}) custom-call(bf16[512,576]{1,0:T(8,128)(2,1)S(1)} %copy-done, bf16[2,256,1024]{2,1,0:T(8,128)(2,1)S(1)} %collective-permute-done.6.refs_1_, bf16[2,256,512]{2,1,0:T(8,128)(2,1)S(1)} %collective-permute-done.7.refs_2_, ...), custom_call_target="tpu_custom_call", output_to_operand_aliasing={{0}: (6, {}), {1}: (7, {})} | custom-call | flops 2000000000 | bytes 4194304 | tf_op jit(solution)/shard_map/final/pallas_call | solution.py:783
  (1 shorter events, 0.0 us)
Async XLA Ops:
  0.6 17.7 %copy-start.5 = (bf16[128,256]{1,0:T(8,128)(2,1)S(1)}, bf16[128,256]{1,0:T(8,128)(2,1)}, u32[]{:S(2)}) copy-start(bf16[128,256]{1,0:T(8,128)(2,1)} %constant.15.clone.near_ref.refs_1_) | copy-start | bytes 196612
  0.6 17.7 %copy-start.10 = (bf16[64,128]{1,0:T(8,128)(2,1)S(1)}, bf16[64,128]{1,0:T(8,128)(2,1)}, u32[]{:S(2)}) copy-start(bf16[64,128]{1,0:T(8,128)(2,1)} %constant.14.clone.pool_ref.refs_0_) | copy-start | bytes 49156
  0.7 17.7 %copy-start.4 = (bf16[512,1024]{1,0:T(8,128)(2,1)S(1)}, bf16[512,1024]{1,0:T(8,128)(2,1)}, u32[]{:S(2)}) copy-start(bf16[512,1024]{1,0:T(8,128)(2,1)} %refs_6_.3) | copy-start | bytes 3145732
  0.7 17.7 %copy-start.3 = (bf16[512,1024]{1,0:T(8,128)(2,1)S(1)}, bf16[512,1024]{1,0:T(8,128)(2,1)}, u32[]{:S(2)}) copy-start(bf16[512,1024]{1,0:T(8,128)(2,1)} %refs_5_.3) | copy-start | bytes 3145732
  0.7 17.7 %copy-start.1 = (bf16[512,1024]{1,0:T(8,128)(2,1)S(1)}, bf16[512,1024]{1,0:T(8,128)(2,1)}, u32[]{:S(2)}) copy-start(bf16[512,1024]{1,0:T(8,128)(2,1)} %refs_4_.3) | copy-start | bytes 3145732
  5.1 13.2 %collective-permute-start.2 = (bf16[2,256,1024]{2,1,0:T(8,128)(2,1)}, bf16[2,256,1024]{2,1,0:T(8,128)(2,1)S(1)}, u32[]{:S(2)}, u32[]{:S(2)}) collective-permute-start(bf16[2,256,1024]{2,1,0:T(8,128)(2,1)} %get-tuple-element.41), channel_id=1, source_target_pairs={{0,1},{1,0},{2,3},{3,2},{4,5},{5,4},{6,7},{7,6},{8,9},{9,8},{10,11... | collective-permute-start | bytes 3145736 | tf_op jit(solution)/shard_map/ppermute | solution.py:813
  5.1 20.0 %collective-permute-start.1 = (bf16[2,64,1024]{2,1,0:T(8,128)(2,1)}, bf16[2,64,1024]{2,1,0:T(8,128)(2,1)S(1)}, u32[]{:S(2)}, u32[]{:S(2)}) collective-permute-start(bf16[2,64,1024]{2,1,0:T(8,128)(2,1)} %get-tuple-element.40), channel_id=1, source_target_pairs={{0,2},{2,4},{3,1},{4,6},{5,3},{6,8},{7,5},{8,10},{9,7},{10,12},{11... | collective-permute-start | bytes 786440 | tf_op jit(solution)/shard_map/ppermute | solution.py:812
  8.9 22.4 %copy-start.9 = (bf16[64,256]{1,0:T(8,128)(2,1)S(1)}, bf16[64,256]{1,0:T(8,128)(2,1)}, u32[]{:S(2)}) copy-start(bf16[64,256]{1,0:T(8,128)(2,1)} %constant.16.clone.pool_ref) | copy-start | bytes 98308
  9.0 22.4 %collective-permute-start = (bf16[2,256,1024]{2,1,0:T(8,128)(2,1)}, bf16[2,256,1024]{2,1,0:T(8,128)(2,1)S(1)}, u32[]{:S(2)}, u32[]{:S(2)}) collective-permute-start(bf16[2,256,1024]{2,1,0:T(8,128)(2,1)} %get-tuple-element.39), channel_id=1, source_target_pairs={{1,2},{2,1},{3,4},{4,3},{5,6},{6,5},{7,8},{8,7},{9,10},{10,9},{11,... | collective-permute-start | bytes 3145736 | tf_op jit(solution)/shard_map/ppermute | solution.py:811
  25.1 9.0 %copy-start.2 = (bf16[512,1024]{1,0:T(8,128)(2,1)S(1)}, bf16[512,1024]{1,0:T(8,128)(2,1)}, u32[]{:S(2)}) copy-start(bf16[512,1024]{1,0:T(8,128)(2,1)} %refs_7_.3) | copy-start | bytes 3145732
  25.1 9.0 %copy-start.6 = (bf16[256,128]{1,0:T(8,128)(2,1)S(1)}, bf16[256,128]{1,0:T(8,128)(2,1)}, u32[]{:S(2)}) copy-start(bf16[256,128]{1,0:T(8,128)(2,1)} %constant.17.clone.near_t_ref.refs_2_) | copy-start | bytes 196612
  31.7 2.4 %collective-permute-start.3 = (bf16[2,128,1024]{2,1,0:T(8,128)(2,1)S(1)}, bf16[2,128,1024]{2,1,0:T(8,128)(2,1)S(1)}, u32[]{:S(2)}, u32[]{:S(2)}) collective-permute-start(bf16[2,128,1024]{2,1,0:T(8,128)(2,1)S(1)} %far.1), channel_id=1, source_target_pairs={{0,1},{1,0},{2,3},{3,2},{4,5},{5,4},{6,7},{7,6},{8,9},{9,8},{10,11... | collective-permute-start | bytes 1572872 | tf_op jit(solution)/shard_map/ppermute | solution.py:816
  34.1 12.5 %copy-start.7 = (bf16[256,64]{1,0:T(8,128)(2,1)S(1)}, bf16[256,64]{1,0:T(8,128)(2,1)}, u32[]{:S(2)}) copy-start(bf16[256,64]{1,0:T(8,128)(2,1)} %constant.18.clone.pool_ref) | copy-start | bytes 98308
  44.6 12.2 %copy-start.8 = (bf16[128,128]{1,0:T(8,128)(2,1)S(1)}, bf16[128,128]{1,0:T(8,128)(2,1)}, u32[]{:S(2)}) copy-start(bf16[128,128]{1,0:T(8,128)(2,1)} %constant.19.clone.refs_3_) | copy-start | bytes 98308
  44.6 1.9 %collective-permute-start.4 = (bf16[2,128,1024]{2,1,0:T(8,128)(2,1)S(1)}, bf16[2,128,1024]{2,1,0:T(8,128)(2,1)S(1)}, u32[]{:S(2)}, u32[]{:S(2)}) collective-permute-start(bf16[2,128,1024]{2,1,0:T(8,128)(2,1)S(1)} %get-tuple-element.52), channel_id=1, source_target_pairs={{0,1},{1,0},{2,3},{3,2},{4,5},{5,4},{6,7},{7,6},{8,9},{9,8},{10,11... | collective-permute-start | bytes 1572872 | tf_op jit(solution)/shard_map/ppermute | solution.py:820
  47.0 15.9 %collective-permute-start.5 = (bf16[2,64,1024]{2,1,0:T(8,128)(2,1)S(1)}, bf16[2,64,1024]{2,1,0:T(8,128)(2,1)S(1)}, u32[]{:S(2)}, u32[]{:S(2)}) collective-permute-start(bf16[2,64,1024]{2,1,0:T(8,128)(2,1)S(1)} %get-tuple-element.56), channel_id=1, source_target_pairs={{1,3},{2,0},{3,5},{4,2},{5,7},{6,4},{7,9},{8,6},{9,11},{10,8},{11,... | collective-permute-start | bytes 786440 | tf_op jit(solution)/shard_map/ppermute | solution.py:823
  54.2 20.3 %collective-permute-start.6 = (bf16[2,256,1024]{2,1,0:T(8,128)(2,1)S(1)}, bf16[2,256,1024]{2,1,0:T(8,128)(2,1)S(1)}, u32[]{:S(2)}, u32[]{:S(2)}) collective-permute-start(bf16[2,256,1024]{2,1,0:T(8,128)(2,1)S(1)} %get-tuple-element.62), channel_id=1, source_target_pairs={{1,2},{2,1},{3,4},{4,3},{5,6},{6,5},{7,8},{8,7},{9,10},{10,9},{11,... | collective-permute-start | bytes 3145736 | tf_op jit(solution)/shard_map/ppermute | solution.py:822
  63.0 6.7 %collective-permute-start.8 = (bf16[2,256,512]{2,1,0:T(8,128)(2,1)S(1)}, bf16[2,256,512]{2,1,0:T(8,128)(2,1)S(1)}, u32[]{:S(2)}, u32[]{:S(2)}) collective-permute-start(bf16[2,256,512]{2,1,0:T(8,128)(2,1)S(1)} %get-tuple-element.67), channel_id=1, source_target_pairs={{0,1},{1,0},{2,3},{3,2},{4,5},{5,4},{6,7},{7,6},{8,9},{9,8},{10,11... | collective-permute-start | bytes 1572872 | tf_op jit(solution)/shard_map/ppermute | solution.py:831
  63.0 11.5 %copy-start = (bf16[512,576]{1,0:T(8,128)(2,1)S(1)}, bf16[512,576]{1,0:T(8,128)(2,1)}, u32[]{:S(2)}) copy-start(bf16[512,576]{1,0:T(8,128)(2,1)} %constant.20.clone.refs_0_) | copy-start | bytes 1769476
  69.2 7.7 %collective-permute-start.7 = (bf16[2,256,512]{2,1,0:T(8,128)(2,1)S(1)}, bf16[2,256,512]{2,1,0:T(8,128)(2,1)S(1)}, u32[]{:S(2)}, u32[]{:S(2)}) collective-permute-start(bf16[2,256,512]{2,1,0:T(8,128)(2,1)S(1)} %get-tuple-element.63), channel_id=1, source_target_pairs={{0,1},{1,0},{2,3},{3,2},{4,5},{5,4},{6,7},{7,6},{8,9},{9,8},{10,11... | collective-permute-start | bytes 1572872 | tf_op jit(solution)/shard_map/ppermute | solution.py:831

commit v3 on v2

--- a/solution.py
+++ b/solution.py
@@ -32,19 +32,6 @@
 BLOCK_POOL = pool_matrix(64, 128, [(0, 64, 0, 2)])
 NEAR_POOL = pool_matrix(128, 256, [(0, 64, 0, 2), (64, 32, 0, 4), (96, 32, 128, 2)])
 FAR_POOL = pool_matrix(64, 256, [(0, 16, 0, 8), (16, 16, 128, 4), (32, 32, 192, 2)])
-SPREAD = pool_matrix(
-    576,
-    512,
-    [
-        (0, 128, 0, 1),
-        (128, 64, 128, 2),
-        (192, 64, 256, 4),
-        (256, 128, 384, 1),
-        (384, 64, 256, 2),
-        (448, 64, 0, 4),
-        (512, 64, 0, 8),
-    ],
-).T
 BLOCK_SPREAD = np.concatenate([BLOCK_POOL.T, BLOCK_POOL.T], axis=1)
 
 
@@ -64,25 +51,67 @@
     return pl.ds(pl.multiple_of(jnp.where(even, number, 3 - number) * NB, NB), NB)
 
 
-def pool_kernel(k_ref, v_ref, cross_ref, inner_ref, far_ref):
-    even = is_even()
+def means():
     row = lax.broadcasted_iota(jnp.int32, (NB, NB), 0)
     col = lax.broadcasted_iota(jnp.int32, (NB, NB), 1)
     matrix = jnp.where(row == (col >> 1), 0.5, 0.0)
     matrix = jnp.where(row == (col >> 2) + 64, 0.25, matrix)
-    matrix = jnp.where(row == (col >> 3) + 96, 0.125, matrix).astype(BF)
-    for which, ref in enumerate((k_ref, v_ref)):
-        pooled = [mm(matrix, ref[block(even, b), :]).astype(BF) for b in range(4)]
-        cross_ref[which, :128] = ref[block(even, 0), :]
-        cross_ref[which, 128:192] = pooled[1][:64]
-        cross_ref[which, 192:224] = pooled[2][64:96]
-        cross_ref[which, 224:] = pooled[3][64:96]
-        inner_ref[which, :128] = ref[block(even, 3), :]
-        inner_ref[which, 128:192] = pooled[2][:64]
-        inner_ref[which, 192:224] = pooled[0][64:96]
-        inner_ref[which, 224:] = pooled[1][64:96]
+    return jnp.where(row == (col >> 3) + 96, 0.125, matrix).astype(BF)
+
+
+def pool_kernel(
+    k_ref,
+    v_ref,
+    cross_out,
+    inner_out,
+    far_out,
+    rows_ref,
+    cross_ref,
+    inner_ref,
+    far_ref,
+    sems,
+    out_sems,
+):
+    even = is_even()
+
+    def copy(which, b):
+        ref = (k_ref, v_ref)[which]
+        return pltpu.make_async_copy(
+            ref.at[block(even, b), :], rows_ref.at[which, b], sems.at[which, b]
+        )
+
+    for which in range(2):
         for b in range(4):
-            far_ref[which, b * 16 : (b + 1) * 16] = pooled[b][96:112]
+            copy(which, b).start()
+    matrix = means()
+    copies = []
+    for which in range(2):
+        for b in range(4):
+            copy(which, b).wait()
+            rows = rows_ref[which, b]
+            pooled = mm(matrix, rows).astype(BF)
+            if b == 0:
+                cross_ref[which, :128] = rows
+                inner_ref[which, 192:224] = pooled[64:96]
+            if b == 1:
+                cross_ref[which, 128:192] = pooled[:64]
+                inner_ref[which, 224:] = pooled[64:96]
+            if b == 2:
+                inner_ref[which, 128:192] = pooled[:64]
+                cross_ref[which, 192:224] = pooled[64:96]
+            if b == 3:
+                inner_ref[which, :128] = rows
+                cross_ref[which, 224:] = pooled[64:96]
+            far_ref[which, b * 16 : (b + 1) * 16] = pooled[96:112]
+        places = ((cross_ref, cross_out), (far_ref, far_out), (inner_ref, inner_out))
+        for i, (source, target) in enumerate(places):
+            out = pltpu.make_async_copy(
+                source.at[which], target.at[which], out_sems.at[which, i]
+            )
+            out.start()
+            copies.append(out)
+    for out in copies:
+        out.wait()
 
 
 def far_kernel(pool_ref, cross_ref, far_ref, out_ref):
@@ -98,14 +127,28 @@
         far_out[which] = (far_ref[which].astype(F32) + got_ref[which, :64].astype(F32)).astype(BF)
 
 
-def final_kernel(spread_ref, cross_ref, inner_ref, far_ref, kg_ref, vg_ref, kg_out, vg_out):
+def final_kernel(cross_ref, inner_ref, far_ref, kg_ref, vg_ref, kg_out, vg_out):
     even = is_even()
+    row = lax.broadcasted_iota(jnp.int32, (NB, NB), 0)
+    col = lax.broadcasted_iota(jnp.int32, (NB, NB), 1)
+    matrix = jnp.where((row >> 1) == col, 0.5, 0.0)
+    matrix = jnp.where((row >> 2) + 64 == col, 0.25, matrix)
+    matrix = jnp.where((row >> 3) + 96 == col, 0.125, matrix).astype(BF)
     for which, (ref, out) in enumerate(((kg_ref, kg_out), (vg_ref, vg_out))):
-        rows = jnp.concatenate([cross_ref[which], inner_ref[which], far_ref[which]], axis=0)
-        spread = mm(spread_ref[...], rows)
+        cross = cross_ref.at[which]
+        inner = inner_ref.at[which]
+        none = jnp.zeros((64, out.shape[1]), BF)
+        firsts = (none, cross[128:192], inner[128:192], none)
+        seconds = (inner[192:224], inner[224:], cross[192:224], cross[224:])
         for b in range(4):
-            at = block(even, b)
-            out[at, :] = ref[at, :].astype(F32) + spread[b * NB : (b + 1) * NB]
+            far = far_ref[which, b * 16 : (b + 1) * 16]
+            pooled = jnp.concatenate([firsts[b], seconds[b], far, none[:16]], axis=0)
+            total = ref[block(even, b), :].astype(F32) + mm(matrix, pooled)
+            if b == 0:
+                total = total + cross[:128].astype(F32)
+            if b == 3:
+                total = total + inner[:128].astype(F32)
+            out[block(even, b), :] = total
 
 
 NEAR_ROWS = (640, 832)
@@ -220,10 +263,10 @@
     return jnp.concatenate(totals, axis=1)
 
 
-def score_grads(chunks, admit, rows, g_t, inverse, delta, exp_ref, p_ref, ds_ref, base):
+def score_grads(chunks, admit, product, inverse, delta, exp_ref, p_ref, ds_ref, base):
     for chunk in chunks:
         low, high, level, side = chunk
-        dp = mm(rows[low:high], g_t)
+        dp = product(low, high)
         for blk in range(2):
             lanes = lanes_of(blk)
             part = overlap(chunk, admit[blk])
@@ -267,8 +310,11 @@
 
 
 STEP = 2
-WIDE = STEP * HD
-UNITS = tuple((head, pair) for head in range(STEP) for pair in range(2))
+CROSS_STEP = 4
+
+
+def units(step):
+    return [(head, pair) for head in range(step) for pair in range(2)]
 
 
 def two(even, ref, pair, head):
@@ -283,11 +329,11 @@
     ref[block(even, 2 * pair + 1), lanes_of(head)] = rows[NB:]
 
 
-def staggered(*stages):
-    for time in range(len(UNITS) + len(stages) - 1):
+def staggered(work, *stages):
+    for time in range(len(work) + len(stages) - 1):
         for lag, stage in enumerate(stages):
-            if 0 <= time - lag < len(UNITS):
-                stage(*UNITS[time - lag])
+            if 0 <= time - lag < len(work):
+                stage(*work[time - lag])
 
 
 def columns(pair):
@@ -301,13 +347,16 @@
     q_ref,
     k_ref,
     v_ref,
+    g_ref,
     inner_ref,
     pa_ref,
     pb_ref,
+    dpa_ref,
+    dpb_ref,
+    ka_ref,
+    kb_ref,
     out_ref,
     stat_ref,
-    ka_ref,
-    kb_ref,
     va_ref,
     vb_ref,
     s_ref,
@@ -317,6 +366,7 @@
     lay_near(even, 0, k_ref, inner_ref, pool_ref, near_ref, ka_ref, kb_ref)
     lay_near(even, 1, v_ref, inner_ref, pool_ref, near_ref, va_ref, vb_ref)
     keys, values, exps = (ka_ref, kb_ref), (va_ref, vb_ref), (pa_ref, pb_ref)
+    products = (dpa_ref, dpb_ref)
     best = {}
 
     def score(head, pair):
@@ -344,11 +394,17 @@
         stat_ref[head, 0:1, columns(pair)] = best[head, pair]
         stat_ref[head, 1:2, columns(pair)] = total
 
+    def product(head, pair):
+        g_t = two(even, g_ref, pair, head).T
+        for low, high, _, _ in NEAR_CHUNKS[pair]:
+            dp = mm(values[pair][low:high, lanes_of(head)], g_t)
+            products[pair][head, low:high] = dp.astype(BF)
+
     def attend(head, pair):
         cols = values[pair][:, lanes_of(head)].T
         out_ref[head, :, columns(pair)] = mm(cols, exps[pair][head])
 
-    staggered(score, exponential, attend)
+    staggered(units(STEP), score, product, exponential, attend)
 
 
 def cross_kernel(
@@ -379,7 +435,7 @@
 
     @pl.when(pl.program_id(0) == 0)
     def _():
-        for head, pair in UNITS:
+        for head, pair in units(CROSS_STEP):
             base = CROSS_SPAN[pair][0]
             put_zeros(CROSS_ZEROS[pair], base, p_ref.at[head, pair], ds_ref.at[head, pair])
 
@@ -393,7 +449,7 @@
         rows[320:384] = far_ref[which]
         rows[384:512] = swap_ref[which]
         rows[512:576] = near[64:]
-        rows[576:] = jnp.zeros((64, WIDE), BF)
+        rows[576:] = jnp.zeros((64, rows.shape[1]), BF)
     state = {}
     grads = {}
 
@@ -442,8 +498,7 @@
         score_grads(
             CROSS_CHUNKS[pair],
             CROSS_ADMIT[pair],
-            v_ref.at[:, lanes_of(head)],
-            g_t,
+            lambda low, high: mm(v_ref[low:high, lanes_of(head)], g_t),
             inverse,
             delta,
             p,
@@ -462,8 +517,8 @@
             mm(p_ref[head, pair, : end - base], two(even, g_ref, pair, head)),
         )
 
-    staggered(score, exponential, attend, differentiate, multiply)
-    for head in range(STEP):
+    staggered(units(CROSS_STEP), score, exponential, attend, differentiate, multiply)
+    for head in range(CROSS_STEP):
         lanes = lanes_of(head)
         for which in range(2):
             a = grads[head, 0][which]
@@ -477,27 +532,22 @@
 
 
 def last_kernel(
-    pool_ref,
-    near_ref,
     near_t_ref,
     spread_ref,
     q_ref,
-    k_ref,
-    v_ref,
     g_ref,
-    inner_ref,
     pa_ref,
     pb_ref,
+    dpa_ref,
+    dpb_ref,
+    ka_ref,
+    kb_ref,
     stat_ref,
     dqt_ref,
     dq_ref,
     kg_ref,
     vg_ref,
     innerg_ref,
-    ka_ref,
-    kb_ref,
-    va_ref,
-    vb_ref,
     wa_ref,
     wb_ref,
     dsa_ref,
@@ -511,9 +561,7 @@
             put_zeros(NEAR_ZEROS[0], 0, wa_ref.at[head], dsa_ref.at[head])
             put_zeros(NEAR_ZEROS[1], 0, wb_ref.at[head], dsb_ref.at[head])
 
-    lay_near(even, 0, k_ref, inner_ref, pool_ref, near_ref, ka_ref, kb_ref)
-    lay_near(even, 1, v_ref, inner_ref, pool_ref, near_ref, va_ref, vb_ref)
-    keys, values, exps = (ka_ref, kb_ref), (va_ref, vb_ref), (pa_ref, pb_ref)
+    keys, exps, products = (ka_ref, kb_ref), (pa_ref, pb_ref), (dpa_ref, dpb_ref)
     weights, logits = (wa_ref, wb_ref), (dsa_ref, dsb_ref)
     grads = {}
 
@@ -521,8 +569,7 @@
         score_grads(
             NEAR_CHUNKS[pair],
             NEAR_ADMIT[pair],
-            values[pair].at[:, lanes_of(head)],
-            two(even, g_ref, pair, head).T,
+            lambda low, high: products[pair][head, low:high].astype(F32),
             stat_ref[head, 0:1, columns(pair)],
             stat_ref[head, 1:2, columns(pair)],
             exps[pair].at[head],
@@ -559,11 +606,10 @@
             edge = jnp.concatenate([b[384:512], b[640:704], a[576:640] + b[768:832]], axis=0)
             innerg_ref[which, :, lanes] = (edge + mm(near_t_ref[...], near)).astype(BF)
 
-    staggered(differentiate, multiply, collect)
-
-
-CORE_VMEM = 32 * 2**20
-SIDE_VMEM = 16 * 2**20
+    staggered(units(STEP), differentiate, multiply, collect)
+
+
+SIDE_VMEM = 8 * 2**20
 
 
 def params(limit=SIDE_VMEM):
@@ -586,8 +632,8 @@
     return pl.BlockSpec((2, rows, width), lambda i: (0, 0, first + i))
 
 
-def per_head(rows, width, first=0):
-    return pl.BlockSpec((STEP, rows, width), lambda i: (first + i, 0, 0))
+def per_head(rows, width, first=0, step=STEP):
+    return pl.BlockSpec((step, rows, width), lambda i: (first + i, 0, 0))
 
 
 def constant(matrix):
@@ -620,13 +666,20 @@
 
 def call_pool(keys, values):
     tok, lanes = keys.shape
-    width = 256
     return pl.pallas_call(
         pool_kernel,
-        grid=(lanes // width,),
-        in_specs=[part(tok, width), part(tok, width)],
-        out_specs=[duo(EDGE, width), duo(EDGE, width), duo(64, width)],
+        grid=(1,),
+        in_specs=[pl.BlockSpec(memory_space=pl.ANY)] * 2,
+        out_specs=[pl.BlockSpec(memory_space=pl.ANY)] * 3,
         out_shape=[shaped(2, EDGE, lanes), shaped(2, EDGE, lanes), shaped(2, 64, lanes)],
+        scratch_shapes=[
+            pltpu.VMEM((2, 4, NB, lanes), BF),
+            pltpu.VMEM((2, EDGE, lanes), BF),
+            pltpu.VMEM((2, EDGE, lanes), BF),
+            pltpu.VMEM((2, 64, lanes), BF),
+            pltpu.SemaphoreType.DMA((2, 4)),
+            pltpu.SemaphoreType.DMA((2, 3)),
+        ],
         compiler_params=params(60 * 2**20),
         cost_estimate=cost(1e9, 5 * tok * lanes * 2),
         name="pool",
@@ -648,51 +701,47 @@
     )(constant(FAR_POOL), cross, far)
 
 
-def call_first(n, queries, keys, values, inner):
-    tok, lanes = queries.shape
+def call_first(n, arrays, inner):
+    tok, lanes = arrays[0].shape
     heads = lanes // HD
+    wide = STEP * HD
     fixed = [constant(m) for m in (BLOCK_POOL, NEAR_POOL)]
     return pl.pallas_call(
         functools.partial(first_kernel, n),
         grid=(heads // STEP,),
-        in_specs=[whole(m.shape) for m in fixed] + [part(tok, WIDE)] * 3 + [duo(EDGE, WIDE)],
-        out_specs=[
-            per_head(NEAR_ROWS[0], PAIR),
-            per_head(NEAR_ROWS[1], PAIR),
-            per_head(HD, tok),
-            per_head(8, tok),
-        ],
-        out_shape=[
-            shaped(heads, NEAR_ROWS[0], PAIR),
-            shaped(heads, NEAR_ROWS[1], PAIR),
-            shaped(heads, HD, tok, dtype=F32),
-            shaped(heads, 8, tok, dtype=F32),
-        ],
-        scratch_shapes=[pltpu.VMEM((rows, WIDE), BF) for rows in NEAR_ROWS * 2]
+        in_specs=[whole(m.shape) for m in fixed] + [part(tok, wide)] * 4 + [duo(EDGE, wide)],
+        out_specs=[per_head(rows, PAIR) for rows in NEAR_ROWS * 2]
+        + [part(rows, wide) for rows in NEAR_ROWS]
+        + [per_head(HD, tok), per_head(8, tok)],
+        out_shape=[shaped(heads, rows, PAIR) for rows in NEAR_ROWS * 2]
+        + [shaped(rows, lanes) for rows in NEAR_ROWS]
+        + [shaped(heads, HD, tok, dtype=F32), shaped(heads, 8, tok, dtype=F32)],
+        scratch_shapes=[pltpu.VMEM((rows, wide), BF) for rows in NEAR_ROWS]
         + [pltpu.VMEM((STEP, 2, NEAR_ROWS[1], PAIR), F32)],
-        compiler_params=params(CORE_VMEM),
-        cost_estimate=cost(heads * 1.5e9, 20 * tok * lanes),
+        compiler_params=params(16 * 2**20),
+        cost_estimate=cost(heads * 3e8, 4 * tok * lanes),
         name="first",
-    )(*fixed, queries, keys, values, inner)
+    )(*fixed, *arrays, inner)
 
 
 def call_cross(n, queries, out_grad, cross, far, swap, sums, stats):
     tok, lanes = queries.shape
     heads = lanes // HD
+    wide = CROSS_STEP * HD
     fixed = [constant(m) for m in (NEAR_POOL, NEAR_POOL.T)]
     return pl.pallas_call(
         functools.partial(cross_kernel, n),
-        grid=(heads // STEP,),
+        grid=(heads // CROSS_STEP,),
         in_specs=[whole(m.shape) for m in fixed]
-        + [part(tok, WIDE)] * 2
-        + [duo(EDGE, WIDE), duo(64, WIDE), duo(128, WIDE), per_head(HD, tok), per_head(8, tok)],
+        + [part(tok, wide)] * 2
+        + [duo(EDGE, wide), duo(64, wide), duo(128, wide), per_head(HD, tok, step=CROSS_STEP), per_head(8, tok, step=CROSS_STEP)],
         out_specs=[
-            part(tok, WIDE),
-            per_head(HD, tok),
-            per_head(8, tok),
-            duo(EDGE, WIDE),
-            duo(64, WIDE),
-            duo(128, WIDE),
+            part(tok, wide),
+            per_head(HD, tok, step=CROSS_STEP),
+            per_head(8, tok, step=CROSS_STEP),
+            duo(EDGE, wide),
+            duo(64, wide),
+            duo(128, wide),
         ],
         out_shape=[
             shaped(tok, lanes),
@@ -703,56 +752,50 @@
             shaped(2, 128, lanes),
         ],
         scratch_shapes=[
-            pltpu.VMEM((CROSS_ROWS, WIDE), BF),
-            pltpu.VMEM((CROSS_ROWS, WIDE), BF),
-            pltpu.VMEM((STEP, 2, CROSS_ROWS, PAIR), F32),
-            pltpu.VMEM((STEP, 2, 512, PAIR), BF),
-            pltpu.VMEM((STEP, 2, 512, PAIR), BF),
+            pltpu.VMEM((CROSS_ROWS, wide), BF),
+            pltpu.VMEM((CROSS_ROWS, wide), BF),
+            pltpu.VMEM((CROSS_STEP, 2, CROSS_ROWS, PAIR), F32),
+            pltpu.VMEM((CROSS_STEP, 2, 512, PAIR), BF),
+            pltpu.VMEM((CROSS_STEP, 2, 512, PAIR), BF),
         ],
-        compiler_params=params(CORE_VMEM),
+        compiler_params=params(20 * 2**20),
         cost_estimate=cost(heads * 1.5e9, 20 * tok * lanes),
         name="cross",
     )(*fixed, queries, out_grad, cross, far, swap, sums, stats)
 
 
-def call_last(arrays, inner, pa, pb, stats, dqt, group, earlier):
+def call_last(queries, out_grad, near, stats, dqt, group, earlier):
     start, heads = group
-    first = start // STEP
-    tok, feat = arrays[0].shape
-    lanes = heads * HD
+    tok, feat = queries.shape
+    first, wide, lanes = start // STEP, STEP * HD, heads * HD
     taken = [] if earlier is None else [earlier]
-    fixed = [constant(m) for m in (BLOCK_POOL, NEAR_POOL, NEAR_POOL.T, BLOCK_SPREAD)]
+    fixed = [constant(m) for m in (NEAR_POOL.T, BLOCK_SPREAD)]
 
     def kernel(*refs):
-        last_kernel(*refs[:13], *refs[13 + len(taken) :])
+        last_kernel(*refs[:12], *refs[12 + len(taken) :])
 
     return pl.pallas_call(
         kernel,
         grid=(heads // STEP,),
         in_specs=[whole(m.shape) for m in fixed]
-        + [part(tok, WIDE, first)] * 4
-        + [
-            duo(EDGE, WIDE, first),
-            per_head(NEAR_ROWS[0], PAIR, first),
-            per_head(NEAR_ROWS[1], PAIR, first),
-            per_head(8, tok, first),
-            per_head(HD, tok, first),
-        ]
+        + [part(tok, wide, first)] * 2
+        + [per_head(rows, PAIR, first) for rows in NEAR_ROWS * 2]
+        + [part(rows, wide, first) for rows in NEAR_ROWS]
+        + [per_head(8, tok, first), per_head(HD, tok, first)]
         + [pl.BlockSpec(memory_space=pl.ANY)] * len(taken),
-        out_specs=[part(tok, WIDE, first), part(tok, WIDE), part(tok, WIDE), duo(EDGE, WIDE)],
+        out_specs=[part(tok, wide, first), part(tok, wide), part(tok, wide), duo(EDGE, wide)],
         out_shape=[
             shaped(tok, feat, dtype=F32),
             shaped(tok, lanes),
             shaped(tok, lanes),
             shaped(2, EDGE, lanes),
         ],
-        scratch_shapes=[pltpu.VMEM((rows, WIDE), BF) for rows in NEAR_ROWS * 2]
-        + [pltpu.VMEM((STEP, rows, PAIR), BF) for rows in NEAR_ROWS * 2],
-        input_output_aliases={13 + i: i for i in range(len(taken))},
-        compiler_params=params(CORE_VMEM),
+        scratch_shapes=[pltpu.VMEM((STEP, rows, PAIR), BF) for rows in NEAR_ROWS * 2],
+        input_output_aliases={12 + i: i for i in range(len(taken))},
+        compiler_params=params(14 * 2**20),
         cost_estimate=cost(heads * 1.5e9, 20 * tok * lanes),
         name="last",
-    )(*fixed, *arrays, inner, pa, pb, stats, dqt, *taken)
+    )(*fixed, queries, out_grad, *near, stats, dqt, *taken)
 
 
 def call_fold(cross, far, got):
@@ -773,18 +816,17 @@
 def call_final(cross, inner, far, kg, vg, feat, group, earlier):
     first, heads = group
     tok, lanes = kg.shape
-    width = 256
+    width = min(512, lanes)
     offset = first * HD // width
     taken = [] if earlier is None else list(earlier)
 
     def kernel(*refs):
-        final_kernel(*refs[:6], *refs[6 + len(taken) :])
+        final_kernel(*refs[:5], *refs[5 + len(taken) :])
 
     return pl.pallas_call(
         kernel,
         grid=(lanes // width,),
         in_specs=[
-            whole((512, 576)),
             duo(EDGE, width, offset),
             duo(EDGE, width),
             duo(64, width, offset),
@@ -793,11 +835,11 @@
         + [pl.BlockSpec(memory_space=pl.ANY)] * len(taken),
         out_specs=[part(tok, width, offset)] * 2,
         out_shape=[shaped(tok, feat, dtype=F32)] * 2,
-        input_output_aliases={6 + i: i for i in range(len(taken))},
+        input_output_aliases={5 + i: i for i in range(len(taken))},
         compiler_params=params(),
         cost_estimate=cost(2e9, 16 * tok * lanes),
         name="final",
-    )(constant(SPREAD), cross, inner, far, kg, vg, *taken)
+    )(cross, inner, far, kg, vg, *taken)
 
 
 GROUPS = ((0, 4), (4, 4))
@@ -808,10 +850,11 @@
     n = lax.axis_size("ctx")
     send = functools.partial(lax.ppermute, axis_name="ctx")
     cross, inner, far = call_pool(keys, values)
-    cross = send(cross, perm=cross_pairs(n))
     far = send(far, perm=far_pairs(n))
     inner = send(inner, perm=swap_pairs(n))
-    pa, pb, sums, stats = call_first(n, queries, keys, values, inner)
+    cross = send(cross, perm=cross_pairs(n))
+    arrays = (queries, keys, values, out_grad)
+    *near, sums, stats = call_first(n, arrays, inner)
     cross, far, stats = lax.optimization_barrier((cross, far, stats))
     swap = send(call_far(cross, far), perm=swap_pairs(n))
     att, dqt, stats, cross_g, far_g, swap_g = call_cross(
@@ -821,13 +864,12 @@
     cross_g, far_g, stats = lax.optimization_barrier((cross_g, far_g, stats))
     cross_g = send(cross_g, perm=cross_pairs(n))
     far_g = send(far_g, perm=back_pairs(n))
-    arrays = (queries, keys, values, out_grad)
     dq = None
     parts = []
     for number, group in enumerate(GROUPS):
         if number == 1:
             far_g, stats = lax.optimization_barrier((far_g, stats))
-        dq, kg, vg, inner_g = call_last(arrays, inner, pa, pb, stats, dqt, group, dq)
+        dq, kg, vg, inner_g = call_last(queries, out_grad, near, stats, dqt, group, dq)
         parts.append((send(inner_g, perm=swap_pairs(n)), kg, vg))
     grads = None
     for group, (inner_g, kg, vg) in zip(GROUPS, parts):

time: 79.5 us -> 76.6 us (0.964)
  Pallas kernels: 39.4 us -> 36.1 us
  starting transfers between devices: 24.7 us -> 23.3 us
  local copies, waits for them, and re-layouts: 0.06 us -> 1.27 us
    ppermute x1, waiting for transfers between devices: 6.24 us -> 0.01 us  [body(): cross = send(cross, perm=cross_pairs(n))]
    ppermute x1, waiting for transfers between devices: 0.01 us -> 3.39 us  [body(): far = send(far, perm=far_pairs(n))]
    pallas_call x4, Pallas kernels: 19.7 us -> 16.6 us  [the longest x1 9.34 us: call_cross(): pl.pallas_call(functools.partial(cross_kernel, n), grid=(heads // CROSS_S...]
    ppermute x1, waiting for transfers between devices: 4.87 us -> 7.83 us  [body(): cross_g = send(cross_g, perm=cross_pairs(n))]
    pallas_call x2, Pallas kernels: 12.3 us -> 9.89 us  [call_last(): pl.pallas_call(kernel, grid=(heads // STEP,), in_specs=[whole(m.shape) fo...]
    pallas_call x1, Pallas kernels: 6.68 us -> 8.85 us  [call_first(): pl.pallas_call(functools.partial(first_kernel, n), grid=(heads // STEP,),...]
    ppermute x1, starting transfers between devices: 3.82 us -> 1.92 us  [body(): far = send(far, perm=far_pairs(n))]
    unnamed x22, local copies, waits for them, and re-layouts: 0.06 us -> 1.27 us
where the time goes in v3:
time: 76.6 us; the launch traced here: 76.4 us
  Pallas kernels  36.1 us (47%)
  starting transfers between devices  23.3 us (30%)
  waiting for transfers between devices  14.9 us (19%)
  local copies, waits for them, and re-layouts  1.27 us (2%)
  between operations  0.84 us (1%)
    ppermute x1, starting transfers between devices, body(): cross = send(cross, perm=cross_pairs(n))  10.6 us
    pallas_call x2, Pallas kernels, call_last(): pl.pallas_call(kernel, grid=(heads // STEP,), in_specs=[whole(m.shape) fo...  9.89 us
    pallas_call x1, Pallas kernels, call_cross(): pl.pallas_call(functools.partial(cross_kernel, n), grid=(heads // CROSS_S...  9.34 us
    pallas_call x1, Pallas kernels, call_first(): pl.pallas_call(functools.partial(first_kernel, n), grid=(heads // STEP,),...  8.85 us
    ppermute x1, starting transfers between devices, body(): far_g = send(far_g, perm=back_pairs(n))  7.88 us
    ppermute x1, waiting for transfers between devices, body(): cross_g = send(cross_g, perm=cross_pairs(n))  7.83 us
    pallas_call x1, Pallas kernels, call_pool(): pl.pallas_call(pool_kernel, grid=(1,), in_specs=[pl.BlockSpec(memory_spac...  3.98 us
    ppermute x1, waiting for transfers between devices, body(): far = send(far, perm=far_pairs(n))  3.39 us
  transfers between devices with their start and end apart: 9, of which 4 were waited for; matrix products, arithmetic and copies ran while one was open for 0% of the time, Pallas kernels for 27%

profile of v3, /device:TPU:6, one launch (start us, length us, event | category | flops | bytes accessed | tf_op | source)
XLA Modules:
  0.0 76.4 jit_solution(7278652276149259754)
XLA Ops:
  0.6 0.0 copy-start.7
  0.6 0.0 copy-start.10
  0.7 0.0 copy-start.1
  0.7 0.0 copy-start
  0.7 0.0 copy-start.2
  0.7 4.0 %pool.1 = (bf16[2,256,1024]{2,1,0:T(8,128)(2,1)}, bf16[2,256,1024]{2,1,0:T(8,128)(2,1)}, bf16[2,64,1024]{2,1,0:T(8,128)(2,1)}) custom-call(bf16[512,1024]{1,0:T(8,128)(2,1)} %k_ref.3, bf16[512,1024]{1,0:T(8,128)(2,1)} %v_ref.3), custom_call_target="tpu_custom_call" | custom-call | flops 1000000000 | bytes 5242880 | tf_op jit(solution)/shard_map/pool/pallas_call | solution.py:669
  4.7 0.1 collective-permute-start.2
  4.8 10.6 %collective-permute-start = (bf16[2,256,1024]{2,1,0:T(8,128)(2,1)}, bf16[2,256,1024]{2,1,0:T(8,128)(2,1)S(1)}, u32[]{:S(2)}, u32[]{:S(2)}) collective-permute-start(bf16[2,256,1024]{2,1,0:T(8,128)(2,1)} %get-tuple-element.43), channel_id=1, source_target_pairs={{1,2},{2,1},{3,4},{4,3},{5,6},{6,5},{7,8},{8,7},{9,10},{10,9},{11,... | collective-permute-start | bytes 3145736 | tf_op jit(solution)/shard_map/ppermute | solution.py:855
  15.4 1.9 %collective-permute-start.1 = (bf16[2,64,1024]{2,1,0:T(8,128)(2,1)}, bf16[2,64,1024]{2,1,0:T(8,128)(2,1)S(1)}, u32[]{:S(2)}, u32[]{:S(2)}) collective-permute-start(bf16[2,64,1024]{2,1,0:T(8,128)(2,1)} %get-tuple-element.44), channel_id=1, source_target_pairs={{0,2},{2,4},{3,1},{4,6},{5,3},{6,8},{7,5},{8,10},{9,7},{10,12},{11... | collective-permute-start | bytes 786440 | tf_op jit(solution)/shard_map/ppermute | solution.py:853
  17.3 0.0 collective-permute-done.2.inner_ref
  17.3 0.0 copy-done.7
  17.3 0.0 copy-done.10
  17.3 0.0 copy-done.1
  17.3 0.0 copy-done
  17.3 0.0 copy-done.2
  17.3 0.0 copy-start.3
  17.4 1.2 %copy-done.3 = bf16[512,1024]{1,0:T(8,128)(2,1)S(1)} copy-done((bf16[512,1024]{1,0:T(8,128)(2,1)S(1)}, bf16[512,1024]{1,0:T(8,128)(2,1)}, u32[]{:S(2)}) %copy-start.3) | copy-done | bytes 1048600
  18.6 0.0 copy-start.9
  18.6 8.8 %first.1 = (bf16[8,640,256]{2,1,0:T(8,128)(2,1)S(1)}, bf16[8,832,256]{2,1,0:T(8,128)(2,1)S(1)}, bf16[8,640,256]{2,1,0:T(8,128)(2,1)S(1)}, bf16[8,832,256]{2,1,0:...) custom-call(bf16[64,128]{1,0:T(8,128)(2,1)S(1)} %copy-done.10, ...), custom_call_target="tpu_custom_call" | custom-call | flops 2400000000 | bytes 2097152 | tf_op jit(solution)/shard_map/first/pallas_call | solution.py:709
  27.4 0.0 copy-start.4
  27.4 0.0 copy-start.5
  27.5 3.4 %collective-permute-done.1.far_ref = bf16[2,64,1024]{2,1,0:T(8,128)(2,1)S(1)} collective-permute-done((bf16[2,64,1024]{2,1,0:T(8,128)(2,1)}, bf16[2,64,1024]{2,1,0:T(8,128)(2,1)S(1)}, u32[]{:S(2)}, u32[]{:S(2)}) %collective-permute-start.1) | collective-permute-done | bytes 262176 | tf_op jit(solution)/shard_map/ppermute | solution.py:853
  30.8 0.0 collective-permute-done.cross_ref
  30.8 0.0 copy-done.9
  30.8 0.3 far.1
  31.2 0.1 collective-permute-start.3
  31.3 1.9 %collective-permute-done.3.swap_ref = bf16[2,128,1024]{2,1,0:T(8,128)(2,1)S(1)} collective-permute-done((bf16[2,128,1024]{2,1,0:T(8,128)(2,1)S(1)}, bf16[2,128,1024]{2,1,0:T(8,128)(2,1)S(1)}, u32[]{:S(2)}, u32[]{:S(2)}) %collective-permute-start.3) | collective-permute-done | bytes 524320 | tf_op jit(solution)/shard_map/ppermute | solution.py:859
  33.2 0.0 copy-done.4
  33.2 0.0 copy-done.5
  33.2 0.0 copy-start.6
  33.2 9.3 %cross.1 = (bf16[512,1024]{1,0:T(8,128)(2,1)}, f32[8,128,512]{2,1,0:T(8,128)S(1)}, f32[8,8,512]{2,1,0:T(8,128)S(1)}, bf16[2,256,1024]{2,1,0:T(8,128)(2,1)S(1)}, ...) custom-call(bf16[128,256]{1,0:T(8,128)(2,1)S(1)} %copy-done.7, bf16[256,128]{1,0:T(8,128)(2,1)S(1)} %copy-done.5, ...), custom_call_target="tpu_custom_call" | custom-call | flops 12000000000 | bytes 10485760 | tf_op jit(solution)/shard_map/cross/pallas_call | solution.py:732
  42.5 0.1 collective-permute-start.4
  42.6 1.8 %collective-permute-done.4.got_ref = bf16[2,128,1024]{2,1,0:T(8,128)(2,1)S(1)} collective-permute-done((bf16[2,128,1024]{2,1,0:T(8,128)(2,1)S(1)}, bf16[2,128,1024]{2,1,0:T(8,128)(2,1)S(1)}, u32[]{:S(2)}, u32[]{:S(2)}) %collective-permute-start.4) | collective-permute-done | bytes 524320 | tf_op jit(solution)/shard_map/ppermute | solution.py:863
  44.4 0.0 copy-done.6
  44.4 0.4 fold.1
  44.9 7.9 %collective-permute-start.5 = (bf16[2,64,1024]{2,1,0:T(8,128)(2,1)S(1)}, bf16[2,64,1024]{2,1,0:T(8,128)(2,1)S(1)}, u32[]{:S(2)}, u32[]{:S(2)}) collective-permute-start(bf16[2,64,1024]{2,1,0:T(8,128)(2,1)S(1)} %get-tuple-element.64), channel_id=1, source_target_pairs={{1,3},{2,0},{3,5},{4,2},{5,7},{6,4},{7,9},{8,6},{9,11},{10,8},{11,... | collective-permute-start | bytes 786440 | tf_op jit(solution)/shard_map/ppermute | solution.py:866
  52.8 2.1 %collective-permute-start.6 = (bf16[2,256,1024]{2,1,0:T(8,128)(2,1)S(1)}, bf16[2,256,1024]{2,1,0:T(8,128)(2,1)S(1)}, u32[]{:S(2)}, u32[]{:S(2)}) collective-permute-start(bf16[2,256,1024]{2,1,0:T(8,128)(2,1)S(1)} %get-tuple-element.70), channel_id=1, source_target_pairs={{1,2},{2,1},{3,4},{4,3},{5,6},{6,5},{7,8},{8,7},{9,10},{10,9},{11,... | collective-permute-start | bytes 3145736 | tf_op jit(solution)/shard_map/ppermute | solution.py:865
  54.9 0.0 copy-done.8
  54.9 4.9 %last.2 = (f32[512,1024]{1,0:T(8,128)}, bf16[512,512]{1,0:T(8,128)(2,1)S(1)}, bf16[512,512]{1,0:T(8,128)(2,1)S(1)}, bf16[2,256,512]{2,1,0:T(8,128)(2,1)S(1)}) custom-call(bf16[256,128]{1,0:T(8,128)(2,1)S(1)} %copy-done.5, bf16[128,128]{1,0:T(8,128)(2,1)S(1)} %copy-done.8, bf16[512,1024]{1,0:T(8,128)(2,1)S(1)} %copy-done.2, bf16[512,1024]{1,0:T(8,128)(2,1)S(1)} %copy-done.4, ...), custom_call_target="tpu_custom_call" | custom-call | flops 6000000000 | bytes 5242880 | tf_op jit(solution)/shard_map/last/pallas_call | solution.py:777
  59.8 0.0 collective-permute-start.8
  59.8 0.0 collective-permute-done.5.refs_2_
  59.8 4.9 %last.3 = (f32[512,1024]{1,0:T(8,128)}, bf16[512,512]{1,0:T(8,128)(2,1)S(1)}, bf16[512,512]{1,0:T(8,128)(2,1)S(1)}, bf16[2,256,512]{2,1,0:T(8,128)(2,1)S(1)}) custom-call(bf16[256,128]{1,0:T(8,128)(2,1)S(1)} %copy-done.5, bf16[128,128]{1,0:T(8,128)(2,1)S(1)} %copy-done.8, bf16[512,1024]{1,0:T(8,128)(2,1)S(1)} %copy-done.2, ...), custom_call_target="tpu_custom_call", output_to_operand_aliasing={{0}: (12, {})} | custom-call | flops 6000000000 | bytes 5242880 | tf_op jit(solution)/shard_map/last/pallas_call | solution.py:777
  64.8 0.5 collective-permute-start.7
  65.3 0.0 collective-permute-done.8.refs_1_
  65.3 7.8 %collective-permute-done.6.refs_0_ = bf16[2,256,1024]{2,1,0:T(8,128)(2,1)S(1)} collective-permute-done((bf16[2,256,1024]{2,1,0:T(8,128)(2,1)S(1)}, bf16[2,256,1024]{2,1,0:T(8,128)(2,1)S(1)}, u32[]{:S(2)}, u32[]{:S(2)}) %collective-permute-start.6) | collective-permute-done | bytes 1048608 | tf_op jit(solution)/shard_map/ppermute | solution.py:865
  73.1 1.6 %final.2 = (f32[512,1024]{1,0:T(8,128)}, f32[512,1024]{1,0:T(8,128)}) custom-call(bf16[2,256,1024]{2,1,0:T(8,128)(2,1)S(1)} %collective-permute-done.6.refs_0_, bf16[2,256,512]{2,1,0:T(8,128)(2,1)S(1)} %collective-permute-done.8.refs_1_, bf16[2,64,1024]{2,1,0:T(8,128)(2,1)S(1)} %collective-permute-done.5.refs_2_, ...), custom_call_target="tpu_custom_call" | custom-call | flops 2000000000 | bytes 4194304 | tf_op jit(solution)/shard_map/final/pallas_call | solution.py:826
  74.7 0.0 collective-permute-done.7.refs_1_
  74.7 1.6 %final.3 = (f32[512,1024]{1,0:T(8,128)}, f32[512,1024]{1,0:T(8,128)}) custom-call(bf16[2,256,1024]{2,1,0:T(8,128)(2,1)S(1)} %collective-permute-done.6.refs_0_, bf16[2,256,512]{2,1,0:T(8,128)(2,1)S(1)} %collective-permute-done.7.refs_1_, bf16[2,64,1024]{2,1,0:T(8,128)(2,1)S(1)} %collective-permute-done.5.refs_2_, ...), custom_call_target="tpu_custom_call", output_to_operand_aliasing={{0}: (5, {}), {1}: (6, {})} | custom-call | flops 2000000000 | bytes 4194304 | tf_op jit(solution)/shard_map/final/pallas_call | solution.py:826
  (1 shorter events, 0.0 us)
Async XLA Ops:
  0.6 16.7 %copy-start.7 = (bf16[128,256]{1,0:T(8,128)(2,1)S(1)}, bf16[128,256]{1,0:T(8,128)(2,1)}, u32[]{:S(2)}) copy-start(bf16[128,256]{1,0:T(8,128)(2,1)} %constant.13.clone.near_ref) | copy-start | bytes 196612
  0.6 16.7 %copy-start.10 = (bf16[64,128]{1,0:T(8,128)(2,1)S(1)}, bf16[64,128]{1,0:T(8,128)(2,1)}, u32[]{:S(2)}) copy-start(bf16[64,128]{1,0:T(8,128)(2,1)} %constant.12.clone.pool_ref) | copy-start | bytes 49156
  0.7 16.7 %copy-start.1 = (bf16[512,1024]{1,0:T(8,128)(2,1)S(1)}, bf16[512,1024]{1,0:T(8,128)(2,1)}, u32[]{:S(2)}) copy-start(bf16[512,1024]{1,0:T(8,128)(2,1)} %v_ref.3) | copy-start | bytes 3145732
  0.7 16.7 %copy-start = (bf16[512,1024]{1,0:T(8,128)(2,1)S(1)}, bf16[512,1024]{1,0:T(8,128)(2,1)}, u32[]{:S(2)}) copy-start(bf16[512,1024]{1,0:T(8,128)(2,1)} %k_ref.3) | copy-start | bytes 3145732
  0.7 16.7 %copy-start.2 = (bf16[512,1024]{1,0:T(8,128)(2,1)S(1)}, bf16[512,1024]{1,0:T(8,128)(2,1)}, u32[]{:S(2)}) copy-start(bf16[512,1024]{1,0:T(8,128)(2,1)} %refs_2_.3) | copy-start | bytes 3145732
  4.7 12.6 %collective-permute-start.2 = (bf16[2,256,1024]{2,1,0:T(8,128)(2,1)}, bf16[2,256,1024]{2,1,0:T(8,128)(2,1)S(1)}, u32[]{:S(2)}, u32[]{:S(2)}) collective-permute-start(bf16[2,256,1024]{2,1,0:T(8,128)(2,1)} %get-tuple-element.45), channel_id=1, source_target_pairs={{0,1},{1,0},{2,3},{3,2},{4,5},{5,4},{6,7},{7,6},{8,9},{9,8},{10,11... | collective-permute-start | bytes 3145736 | tf_op jit(solution)/shard_map/ppermute | solution.py:854
  4.8 26.1 %collective-permute-start = (bf16[2,256,1024]{2,1,0:T(8,128)(2,1)}, bf16[2,256,1024]{2,1,0:T(8,128)(2,1)S(1)}, u32[]{:S(2)}, u32[]{:S(2)}) collective-permute-start(bf16[2,256,1024]{2,1,0:T(8,128)(2,1)} %get-tuple-element.43), channel_id=1, source_target_pairs={{1,2},{2,1},{3,4},{4,3},{5,6},{6,5},{7,8},{8,7},{9,10},{10,9},{11,... | collective-permute-start | bytes 3145736 | tf_op jit(solution)/shard_map/ppermute | solution.py:855
  15.4 15.5 %collective-permute-start.1 = (bf16[2,64,1024]{2,1,0:T(8,128)(2,1)}, bf16[2,64,1024]{2,1,0:T(8,128)(2,1)S(1)}, u32[]{:S(2)}, u32[]{:S(2)}) collective-permute-start(bf16[2,64,1024]{2,1,0:T(8,128)(2,1)} %get-tuple-element.44), channel_id=1, source_target_pairs={{0,2},{2,4},{3,1},{4,6},{5,3},{6,8},{7,5},{8,10},{9,7},{10,12},{11... | collective-permute-start | bytes 786440 | tf_op jit(solution)/shard_map/ppermute | solution.py:853
  17.3 1.2 %copy-start.3 = (bf16[512,1024]{1,0:T(8,128)(2,1)S(1)}, bf16[512,1024]{1,0:T(8,128)(2,1)}, u32[]{:S(2)}) copy-start(bf16[512,1024]{1,0:T(8,128)(2,1)} %refs_3_.3) | copy-start | bytes 3145732
  18.6 12.3 %copy-start.9 = (bf16[64,256]{1,0:T(8,128)(2,1)S(1)}, bf16[64,256]{1,0:T(8,128)(2,1)}, u32[]{:S(2)}) copy-start(bf16[64,256]{1,0:T(8,128)(2,1)} %constant.14.clone.pool_ref) | copy-start | bytes 98308
  27.4 5.7 %copy-start.4 = (bf16[512,1024]{1,0:T(8,128)(2,1)S(1)}, bf16[512,1024]{1,0:T(8,128)(2,1)}, u32[]{:S(2)}) copy-start(bf16[512,1024]{1,0:T(8,128)(2,1)} %refs_3_.3) | copy-start | bytes 3145732
  27.4 5.7 %copy-start.5 = (bf16[256,128]{1,0:T(8,128)(2,1)S(1)}, bf16[256,128]{1,0:T(8,128)(2,1)}, u32[]{:S(2)}) copy-start(bf16[256,128]{1,0:T(8,128)(2,1)} %constant.15.clone.near_t_ref.refs_0_) | copy-start | bytes 196612
  31.2 2.0 %collective-permute-start.3 = (bf16[2,128,1024]{2,1,0:T(8,128)(2,1)S(1)}, bf16[2,128,1024]{2,1,0:T(8,128)(2,1)S(1)}, u32[]{:S(2)}, u32[]{:S(2)}) collective-permute-start(bf16[2,128,1024]{2,1,0:T(8,128)(2,1)S(1)} %far.1), channel_id=1, source_target_pairs={{0,1},{1,0},{2,3},{3,2},{4,5},{5,4},{6,7},{7,6},{8,9},{9,8},{10,11... | collective-permute-start | bytes 1572872 | tf_op jit(solution)/shard_map/ppermute | solution.py:859
  33.2 11.3 %copy-start.6 = (bf16[256,64]{1,0:T(8,128)(2,1)S(1)}, bf16[256,64]{1,0:T(8,128)(2,1)}, u32[]{:S(2)}) copy-start(bf16[256,64]{1,0:T(8,128)(2,1)} %constant.16.clone.pool_ref) | copy-start | bytes 98308
  42.5 12.4 %copy-start.8 = (bf16[128,128]{1,0:T(8,128)(2,1)S(1)}, bf16[128,128]{1,0:T(8,128)(2,1)}, u32[]{:S(2)}) copy-start(bf16[128,128]{1,0:T(8,128)(2,1)} %constant.17.clone.refs_1_) | copy-start | bytes 98308
  42.5 1.9 %collective-permute-start.4 = (bf16[2,128,1024]{2,1,0:T(8,128)(2,1)S(1)}, bf16[2,128,1024]{2,1,0:T(8,128)(2,1)S(1)}, u32[]{:S(2)}, u32[]{:S(2)}) collective-permute-start(bf16[2,128,1024]{2,1,0:T(8,128)(2,1)S(1)} %get-tuple-element.60), channel_id=1, source_target_pairs={{0,1},{1,0},{2,3},{3,2},{4,5},{5,4},{6,7},{7,6},{8,9},{9,8},{10,11... | collective-permute-start | bytes 1572872 | tf_op jit(solution)/shard_map/ppermute | solution.py:863
  44.9 15.0 %collective-permute-start.5 = (bf16[2,64,1024]{2,1,0:T(8,128)(2,1)S(1)}, bf16[2,64,1024]{2,1,0:T(8,128)(2,1)S(1)}, u32[]{:S(2)}, u32[]{:S(2)}) collective-permute-start(bf16[2,64,1024]{2,1,0:T(8,128)(2,1)S(1)} %get-tuple-element.64), channel_id=1, source_target_pairs={{1,3},{2,0},{3,5},{4,2},{5,7},{6,4},{7,9},{8,6},{9,11},{10,8},{11,... | collective-permute-start | bytes 786440 | tf_op jit(solution)/shard_map/ppermute | solution.py:866
  52.8 20.3 %collective-permute-start.6 = (bf16[2,256,1024]{2,1,0:T(8,128)(2,1)S(1)}, bf16[2,256,1024]{2,1,0:T(8,128)(2,1)S(1)}, u32[]{:S(2)}, u32[]{:S(2)}) collective-permute-start(bf16[2,256,1024]{2,1,0:T(8,128)(2,1)S(1)} %get-tuple-element.70), channel_id=1, source_target_pairs={{1,2},{2,1},{3,4},{4,3},{5,6},{6,5},{7,8},{8,7},{9,10},{10,9},{11,... | collective-permute-start | bytes 3145736 | tf_op jit(solution)/shard_map/ppermute | solution.py:865
  59.8 5.4 %collective-permute-start.8 = (bf16[2,256,512]{2,1,0:T(8,128)(2,1)S(1)}, bf16[2,256,512]{2,1,0:T(8,128)(2,1)S(1)}, u32[]{:S(2)}, u32[]{:S(2)}) collective-permute-start(bf16[2,256,512]{2,1,0:T(8,128)(2,1)S(1)} %get-tuple-element.75), channel_id=1, source_target_pairs={{0,1},{1,0},{2,3},{3,2},{4,5},{5,4},{6,7},{7,6},{8,9},{9,8},{10,11... | collective-permute-start | bytes 1572872 | tf_op jit(solution)/shard_map/ppermute | solution.py:873
  64.8 10.0 %collective-permute-start.7 = (bf16[2,256,512]{2,1,0:T(8,128)(2,1)S(1)}, bf16[2,256,512]{2,1,0:T(8,128)(2,1)S(1)}, u32[]{:S(2)}, u32[]{:S(2)}) collective-permute-start(bf16[2,256,512]{2,1,0:T(8,128)(2,1)S(1)} %get-tuple-element.71), channel_id=1, source_target_pairs={{0,1},{1,0},{2,3},{3,2},{4,5},{5,4},{6,7},{7,6},{8,9},{9,8},{10,11... | collective-permute-start | bytes 1572872 | tf_op jit(solution)/shard_map/ppermute | solution.py:873

commit v4 on v3

--- a/solution.py
+++ b/solution.py
@@ -71,6 +71,7 @@
     far_ref,
     sems,
     out_sems,
+    raw_sems,
 ):
     even = is_even()
 
@@ -91,19 +92,26 @@
             rows = rows_ref[which, b]
             pooled = mm(matrix, rows).astype(BF)
             if b == 0:
-                cross_ref[which, :128] = rows
-                inner_ref[which, 192:224] = pooled[64:96]
+                inner_ref[which, 64:96] = pooled[64:96]
             if b == 1:
-                cross_ref[which, 128:192] = pooled[:64]
-                inner_ref[which, 224:] = pooled[64:96]
+                cross_ref[which, :64] = pooled[:64]
+                inner_ref[which, 96:] = pooled[64:96]
             if b == 2:
-                inner_ref[which, 128:192] = pooled[:64]
-                cross_ref[which, 192:224] = pooled[64:96]
+                inner_ref[which, :64] = pooled[:64]
+                cross_ref[which, 64:96] = pooled[64:96]
             if b == 3:
-                inner_ref[which, :128] = rows
-                cross_ref[which, 224:] = pooled[64:96]
+                cross_ref[which, 96:] = pooled[64:96]
             far_ref[which, b * 16 : (b + 1) * 16] = pooled[96:112]
-        places = ((cross_ref, cross_out), (far_ref, far_out), (inner_ref, inner_out))
+            if b in (0, 3):
+                target = (cross_out if b == 0 else inner_out).at[which, :NB]
+                out = pltpu.make_async_copy(rows_ref.at[which, b], target, raw_sems.at[which, b % 2])
+                out.start()
+                copies.append(out)
+        places = (
+            (cross_ref, cross_out.at[:, NB:]),
+            (far_ref, far_out),
+            (inner_ref, inner_out.at[:, NB:]),
+        )
         for i, (source, target) in enumerate(places):
             out = pltpu.make_async_copy(
                 source.at[which], target.at[which], out_sems.at[which, i]
@@ -127,8 +135,11 @@
         far_out[which] = (far_ref[which].astype(F32) + got_ref[which, :64].astype(F32)).astype(BF)
 
 
-def final_kernel(cross_ref, inner_ref, far_ref, kg_ref, vg_ref, kg_out, vg_out):
+def final_kernel(
+    offset, cross_ref, inner_ref, far_ref, kg_ref, vg_ref, kg_out, vg_out, rows_ref, sems
+):
     even = is_even()
+    copies = []
     row = lax.broadcasted_iota(jnp.int32, (NB, NB), 0)
     col = lax.broadcasted_iota(jnp.int32, (NB, NB), 1)
     matrix = jnp.where((row >> 1) == col, 0.5, 0.0)
@@ -137,7 +148,7 @@
     for which, (ref, out) in enumerate(((kg_ref, kg_out), (vg_ref, vg_out))):
         cross = cross_ref.at[which]
         inner = inner_ref.at[which]
-        none = jnp.zeros((64, out.shape[1]), BF)
+        none = jnp.zeros((64, ref.shape[1]), BF)
         firsts = (none, cross[128:192], inner[128:192], none)
         seconds = (inner[192:224], inner[224:], cross[192:224], cross[224:])
         for b in range(4):
@@ -148,7 +159,16 @@
                 total = total + cross[:128].astype(F32)
             if b == 3:
                 total = total + inner[:128].astype(F32)
-            out[block(even, b), :] = total
+            rows_ref[which, b] = total
+            copy = pltpu.make_async_copy(
+                rows_ref.at[which, b],
+                out.at[block(even, b), pl.ds(offset, ref.shape[1])],
+                sems.at[which, b],
+            )
+            copy.start()
+            copies.append(copy)
+    for copy in copies:
+        copy.wait()
 
 
 NEAR_ROWS = (640, 832)
@@ -674,11 +694,12 @@
         out_shape=[shaped(2, EDGE, lanes), shaped(2, EDGE, lanes), shaped(2, 64, lanes)],
         scratch_shapes=[
             pltpu.VMEM((2, 4, NB, lanes), BF),
-            pltpu.VMEM((2, EDGE, lanes), BF),
-            pltpu.VMEM((2, EDGE, lanes), BF),
+            pltpu.VMEM((2, NB, lanes), BF),
+            pltpu.VMEM((2, NB, lanes), BF),
             pltpu.VMEM((2, 64, lanes), BF),
             pltpu.SemaphoreType.DMA((2, 4)),
             pltpu.SemaphoreType.DMA((2, 3)),
+            pltpu.SemaphoreType.DMA((2, 2)),
         ],
         compiler_params=params(60 * 2**20),
         cost_estimate=cost(1e9, 5 * tok * lanes * 2),
@@ -816,25 +837,27 @@
 def call_final(cross, inner, far, kg, vg, feat, group, earlier):
     first, heads = group
     tok, lanes = kg.shape
-    width = min(512, lanes)
-    offset = first * HD // width
     taken = [] if earlier is None else list(earlier)
 
     def kernel(*refs):
-        final_kernel(*refs[:5], *refs[5 + len(taken) :])
+        final_kernel(first * HD, *refs[:5], *refs[5 + len(taken) :])
 
     return pl.pallas_call(
         kernel,
-        grid=(lanes // width,),
+        grid=(1,),
         in_specs=[
-            duo(EDGE, width, offset),
-            duo(EDGE, width),
-            duo(64, width, offset),
+            duo(EDGE, lanes, first // heads),
+            duo(EDGE, lanes),
+            duo(64, lanes, first // heads),
         ]
-        + [part(tok, width)] * 2
+        + [part(tok, lanes)] * 2
         + [pl.BlockSpec(memory_space=pl.ANY)] * len(taken),
-        out_specs=[part(tok, width, offset)] * 2,
+        out_specs=[pl.BlockSpec(memory_space=pl.ANY)] * 2,
         out_shape=[shaped(tok, feat, dtype=F32)] * 2,
+        scratch_shapes=[
+            pltpu.VMEM((2, 4, NB, lanes), F32),
+            pltpu.SemaphoreType.DMA((2, 4)),
+        ],
         input_output_aliases={5 + i: i for i in range(len(taken))},
         compiler_params=params(),
         cost_estimate=cost(2e9, 16 * tok * lanes),

time: 76.6 us -> 76.5 us (level)
  no operation moved by 1% of the time
where the time goes in v4:
time: 76.5 us; the launch traced here: 76.2 us
  Pallas kernels  35.8 us (47%)
  starting transfers between devices  23.3 us (30%)
  waiting for transfers between devices  14.9 us (19%)
  local copies, waits for them, and re-layouts  1.27 us (2%)
  between operations  1.02 us (1%)
    ppermute x1, starting transfers between devices, body(): cross = send(cross, perm=cross_pairs(n))  10.6 us
    pallas_call x2, Pallas kernels, call_last(): pl.pallas_call(kernel, grid=(heads // STEP,), in_specs=[whole(m.shape) fo...  9.89 us
    pallas_call x1, Pallas kernels, call_cross(): pl.pallas_call(functools.partial(cross_kernel, n), grid=(heads // CROSS_S...  9.34 us
    pallas_call x1, Pallas kernels, call_first(): pl.pallas_call(functools.partial(first_kernel, n), grid=(heads // STEP,),...  8.85 us
    ppermute x1, starting transfers between devices, body(): far_g = send(far_g, perm=back_pairs(n))  7.88 us
    ppermute x1, waiting for transfers between devices, body(): cross_g = send(cross_g, perm=cross_pairs(n))  7.82 us
    pallas_call x1, Pallas kernels, call_pool(): pl.pallas_call(pool_kernel, grid=(1,), in_specs=[pl.BlockSpec(memory_spac...  3.85 us
    ppermute x1, waiting for transfers between devices, body(): far = send(far, perm=far_pairs(n))  3.39 us
  transfers between devices with their start and end apart: 9, of which 4 were waited for; matrix products, arithmetic and copies ran while one was open for 0% of the time, Pallas kernels for 27%

profile of v4, /device:TPU:6, one launch (start us, length us, event | category | flops | bytes accessed | tf_op | source)
XLA Modules:
  0.0 76.2 jit_solution(17020462412691942071)
XLA Ops:
  0.6 0.0 copy-start.7
  0.6 0.0 copy-start.10
  0.7 0.0 copy-start.1
  0.7 0.0 copy-start
  0.7 0.0 copy-start.2
  0.7 3.8 %pool.1 = (bf16[2,256,1024]{2,1,0:T(8,128)(2,1)}, bf16[2,256,1024]{2,1,0:T(8,128)(2,1)}, bf16[2,64,1024]{2,1,0:T(8,128)(2,1)}) custom-call(bf16[512,1024]{1,0:T(8,128)(2,1)} %k_ref.3, bf16[512,1024]{1,0:T(8,128)(2,1)} %v_ref.3), custom_call_target="tpu_custom_call" | custom-call | flops 1000000000 | bytes 5242880 | tf_op jit(solution)/shard_map/pool/pallas_call | solution.py:689
  4.5 0.1 collective-permute-start.2
  4.6 10.6 %collective-permute-start = (bf16[2,256,1024]{2,1,0:T(8,128)(2,1)}, bf16[2,256,1024]{2,1,0:T(8,128)(2,1)S(1)}, u32[]{:S(2)}, u32[]{:S(2)}) collective-permute-start(bf16[2,256,1024]{2,1,0:T(8,128)(2,1)} %get-tuple-element.43), channel_id=1, source_target_pairs={{1,2},{2,1},{3,4},{4,3},{5,6},{6,5},{7,8},{8,7},{9,10},{10,9},{11,... | collective-permute-start | bytes 3145736 | tf_op jit(solution)/shard_map/ppermute | solution.py:878
  15.2 1.9 %collective-permute-start.1 = (bf16[2,64,1024]{2,1,0:T(8,128)(2,1)}, bf16[2,64,1024]{2,1,0:T(8,128)(2,1)S(1)}, u32[]{:S(2)}, u32[]{:S(2)}) collective-permute-start(bf16[2,64,1024]{2,1,0:T(8,128)(2,1)} %get-tuple-element.44), channel_id=1, source_target_pairs={{0,2},{2,4},{3,1},{4,6},{5,3},{6,8},{7,5},{8,10},{9,7},{10,12},{11... | collective-permute-start | bytes 786440 | tf_op jit(solution)/shard_map/ppermute | solution.py:876
  17.1 0.0 collective-permute-done.2.inner_ref
  17.1 0.0 copy-done.7
  17.2 0.0 copy-done.10
  17.2 0.0 copy-done.1
  17.2 0.0 copy-done
  17.2 0.0 copy-done.2
  17.2 0.0 copy-start.3
  17.2 1.2 %copy-done.3 = bf16[512,1024]{1,0:T(8,128)(2,1)S(1)} copy-done((bf16[512,1024]{1,0:T(8,128)(2,1)S(1)}, bf16[512,1024]{1,0:T(8,128)(2,1)}, u32[]{:S(2)}) %copy-start.3) | copy-done | bytes 1048600
  18.4 0.0 copy-start.9
  18.4 8.8 %first.1 = (bf16[8,640,256]{2,1,0:T(8,128)(2,1)S(1)}, bf16[8,832,256]{2,1,0:T(8,128)(2,1)S(1)}, bf16[8,640,256]{2,1,0:T(8,128)(2,1)S(1)}, bf16[8,832,256]{2,1,0:...) custom-call(bf16[64,128]{1,0:T(8,128)(2,1)S(1)} %copy-done.10, ...), custom_call_target="tpu_custom_call" | custom-call | flops 2400000000 | bytes 2097152 | tf_op jit(solution)/shard_map/first/pallas_call | solution.py:730
  27.3 0.0 copy-start.4
  27.3 0.0 copy-start.5
  27.3 3.4 %collective-permute-done.1.far_ref = bf16[2,64,1024]{2,1,0:T(8,128)(2,1)S(1)} collective-permute-done((bf16[2,64,1024]{2,1,0:T(8,128)(2,1)}, bf16[2,64,1024]{2,1,0:T(8,128)(2,1)S(1)}, u32[]{:S(2)}, u32[]{:S(2)}) %collective-permute-start.1) | collective-permute-done | bytes 262176 | tf_op jit(solution)/shard_map/ppermute | solution.py:876
  30.7 0.0 collective-permute-done.cross_ref
  30.7 0.0 copy-done.9
  30.7 0.3 far.1
  31.0 0.1 collective-permute-start.3
  31.1 1.9 %collective-permute-done.3.swap_ref = bf16[2,128,1024]{2,1,0:T(8,128)(2,1)S(1)} collective-permute-done((bf16[2,128,1024]{2,1,0:T(8,128)(2,1)S(1)}, bf16[2,128,1024]{2,1,0:T(8,128)(2,1)S(1)}, u32[]{:S(2)}, u32[]{:S(2)}) %collective-permute-start.3) | collective-permute-done | bytes 524320 | tf_op jit(solution)/shard_map/ppermute | solution.py:882
  33.0 0.0 copy-done.4
  33.0 0.0 copy-done.5
  33.0 0.0 copy-start.6
  33.0 9.3 %cross.1 = (bf16[512,1024]{1,0:T(8,128)(2,1)}, f32[8,128,512]{2,1,0:T(8,128)S(1)}, f32[8,8,512]{2,1,0:T(8,128)S(1)}, bf16[2,256,1024]{2,1,0:T(8,128)(2,1)S(1)}, ...) custom-call(bf16[128,256]{1,0:T(8,128)(2,1)S(1)} %copy-done.7, bf16[256,128]{1,0:T(8,128)(2,1)S(1)} %copy-done.5, ...), custom_call_target="tpu_custom_call" | custom-call | flops 12000000000 | bytes 10485760 | tf_op jit(solution)/shard_map/cross/pallas_call | solution.py:753
  42.4 0.1 collective-permute-start.4
  42.5 1.8 %collective-permute-done.4.got_ref = bf16[2,128,1024]{2,1,0:T(8,128)(2,1)S(1)} collective-permute-done((bf16[2,128,1024]{2,1,0:T(8,128)(2,1)S(1)}, bf16[2,128,1024]{2,1,0:T(8,128)(2,1)S(1)}, u32[]{:S(2)}, u32[]{:S(2)}) %collective-permute-start.4) | collective-permute-done | bytes 524320 | tf_op jit(solution)/shard_map/ppermute | solution.py:886
  44.3 0.0 copy-done.6
  44.3 0.4 fold.1
  44.7 7.9 %collective-permute-start.5 = (bf16[2,64,1024]{2,1,0:T(8,128)(2,1)S(1)}, bf16[2,64,1024]{2,1,0:T(8,128)(2,1)S(1)}, u32[]{:S(2)}, u32[]{:S(2)}) collective-permute-start(bf16[2,64,1024]{2,1,0:T(8,128)(2,1)S(1)} %get-tuple-element.64), channel_id=1, source_target_pairs={{1,3},{2,0},{3,5},{4,2},{5,7},{6,4},{7,9},{8,6},{9,11},{10,8},{11,... | collective-permute-start | bytes 786440 | tf_op jit(solution)/shard_map/ppermute | solution.py:889
  52.6 2.1 %collective-permute-start.6 = (bf16[2,256,1024]{2,1,0:T(8,128)(2,1)S(1)}, bf16[2,256,1024]{2,1,0:T(8,128)(2,1)S(1)}, u32[]{:S(2)}, u32[]{:S(2)}) collective-permute-start(bf16[2,256,1024]{2,1,0:T(8,128)(2,1)S(1)} %get-tuple-element.70), channel_id=1, source_target_pairs={{1,2},{2,1},{3,4},{4,3},{5,6},{6,5},{7,8},{8,7},{9,10},{10,9},{11,... | collective-permute-start | bytes 3145736 | tf_op jit(solution)/shard_map/ppermute | solution.py:888
  54.7 0.0 copy-done.8
  54.7 5.0 %last.2 = (f32[512,1024]{1,0:T(8,128)}, bf16[512,512]{1,0:T(8,128)(2,1)S(1)}, bf16[512,512]{1,0:T(8,128)(2,1)S(1)}, bf16[2,256,512]{2,1,0:T(8,128)(2,1)S(1)}) custom-call(bf16[256,128]{1,0:T(8,128)(2,1)S(1)} %copy-done.5, bf16[128,128]{1,0:T(8,128)(2,1)S(1)} %copy-done.8, bf16[512,1024]{1,0:T(8,128)(2,1)S(1)} %copy-done.2, bf16[512,1024]{1,0:T(8,128)(2,1)S(1)} %copy-done.4, ...), custom_call_target="tpu_custom_call" | custom-call | flops 6000000000 | bytes 5242880 | tf_op jit(solution)/shard_map/last/pallas_call | solution.py:798
  59.7 0.0 collective-permute-start.8
  59.7 0.0 collective-permute-done.5.refs_2_
  59.7 4.9 %last.3 = (f32[512,1024]{1,0:T(8,128)}, bf16[512,512]{1,0:T(8,128)(2,1)S(1)}, bf16[512,512]{1,0:T(8,128)(2,1)S(1)}, bf16[2,256,512]{2,1,0:T(8,128)(2,1)S(1)}) custom-call(bf16[256,128]{1,0:T(8,128)(2,1)S(1)} %copy-done.5, bf16[128,128]{1,0:T(8,128)(2,1)S(1)} %copy-done.8, bf16[512,1024]{1,0:T(8,128)(2,1)S(1)} %copy-done.2, ...), custom_call_target="tpu_custom_call", output_to_operand_aliasing={{0}: (12, {})} | custom-call | flops 6000000000 | bytes 5242880 | tf_op jit(solution)/shard_map/last/pallas_call | solution.py:798
  64.6 0.5 collective-permute-start.7
  65.1 0.0 collective-permute-done.8.refs_1_
  65.1 7.8 %collective-permute-done.6.refs_0_ = bf16[2,256,1024]{2,1,0:T(8,128)(2,1)S(1)} collective-permute-done((bf16[2,256,1024]{2,1,0:T(8,128)(2,1)S(1)}, bf16[2,256,1024]{2,1,0:T(8,128)(2,1)S(1)}, u32[]{:S(2)}, u32[]{:S(2)}) %collective-permute-start.6) | collective-permute-done | bytes 1048608 | tf_op jit(solution)/shard_map/ppermute | solution.py:888
  72.9 1.6 %final.2 = (f32[512,1024]{1,0:T(8,128)}, f32[512,1024]{1,0:T(8,128)}) custom-call(bf16[2,256,1024]{2,1,0:T(8,128)(2,1)S(1)} %collective-permute-done.6.refs_0_, bf16[2,256,512]{2,1,0:T(8,128)(2,1)S(1)} %collective-permute-done.8.refs_1_, bf16[2,64,1024]{2,1,0:T(8,128)(2,1)S(1)} %collective-permute-done.5.refs_2_, ...), custom_call_target="tpu_custom_call" | custom-call | flops 2000000000 | bytes 4194304 | tf_op jit(solution)/shard_map/final/pallas_call | solution.py:845
  74.5 0.0 collective-permute-done.7.refs_1_
  74.5 1.6 %final.3 = (f32[512,1024]{1,0:T(8,128)}, f32[512,1024]{1,0:T(8,128)}) custom-call(bf16[2,256,1024]{2,1,0:T(8,128)(2,1)S(1)} %collective-permute-done.6.refs_0_, bf16[2,256,512]{2,1,0:T(8,128)(2,1)S(1)} %collective-permute-done.7.refs_1_, bf16[2,64,1024]{2,1,0:T(8,128)(2,1)S(1)} %collective-permute-done.5.refs_2_, ...), custom_call_target="tpu_custom_call", output_to_operand_aliasing={{0}: (5, {}), {1}: (6, {})} | custom-call | flops 2000000000 | bytes 4194304 | tf_op jit(solution)/shard_map/final/pallas_call | solution.py:845
  (1 shorter events, 0.0 us)
Async XLA Ops:
  0.6 16.5 %copy-start.7 = (bf16[128,256]{1,0:T(8,128)(2,1)S(1)}, bf16[128,256]{1,0:T(8,128)(2,1)}, u32[]{:S(2)}) copy-start(bf16[128,256]{1,0:T(8,128)(2,1)} %constant.13.clone.near_ref) | copy-start | bytes 196612
  0.6 16.5 %copy-start.10 = (bf16[64,128]{1,0:T(8,128)(2,1)S(1)}, bf16[64,128]{1,0:T(8,128)(2,1)}, u32[]{:S(2)}) copy-start(bf16[64,128]{1,0:T(8,128)(2,1)} %constant.12.clone.pool_ref) | copy-start | bytes 49156
  0.7 16.5 %copy-start.1 = (bf16[512,1024]{1,0:T(8,128)(2,1)S(1)}, bf16[512,1024]{1,0:T(8,128)(2,1)}, u32[]{:S(2)}) copy-start(bf16[512,1024]{1,0:T(8,128)(2,1)} %v_ref.3) | copy-start | bytes 3145732
  0.7 16.5 %copy-start = (bf16[512,1024]{1,0:T(8,128)(2,1)S(1)}, bf16[512,1024]{1,0:T(8,128)(2,1)}, u32[]{:S(2)}) copy-start(bf16[512,1024]{1,0:T(8,128)(2,1)} %k_ref.3) | copy-start | bytes 3145732
  0.7 16.5 %copy-start.2 = (bf16[512,1024]{1,0:T(8,128)(2,1)S(1)}, bf16[512,1024]{1,0:T(8,128)(2,1)}, u32[]{:S(2)}) copy-start(bf16[512,1024]{1,0:T(8,128)(2,1)} %refs_2_.3) | copy-start | bytes 3145732
  4.5 12.6 %collective-permute-start.2 = (bf16[2,256,1024]{2,1,0:T(8,128)(2,1)}, bf16[2,256,1024]{2,1,0:T(8,128)(2,1)S(1)}, u32[]{:S(2)}, u32[]{:S(2)}) collective-permute-start(bf16[2,256,1024]{2,1,0:T(8,128)(2,1)} %get-tuple-element.45), channel_id=1, source_target_pairs={{0,1},{1,0},{2,3},{3,2},{4,5},{5,4},{6,7},{7,6},{8,9},{9,8},{10,11... | collective-permute-start | bytes 3145736 | tf_op jit(solution)/shard_map/ppermute | solution.py:877
  4.6 26.1 %collective-permute-start = (bf16[2,256,1024]{2,1,0:T(8,128)(2,1)}, bf16[2,256,1024]{2,1,0:T(8,128)(2,1)S(1)}, u32[]{:S(2)}, u32[]{:S(2)}) collective-permute-start(bf16[2,256,1024]{2,1,0:T(8,128)(2,1)} %get-tuple-element.43), channel_id=1, source_target_pairs={{1,2},{2,1},{3,4},{4,3},{5,6},{6,5},{7,8},{8,7},{9,10},{10,9},{11,... | collective-permute-start | bytes 3145736 | tf_op jit(solution)/shard_map/ppermute | solution.py:878
  15.2 15.5 %collective-permute-start.1 = (bf16[2,64,1024]{2,1,0:T(8,128)(2,1)}, bf16[2,64,1024]{2,1,0:T(8,128)(2,1)S(1)}, u32[]{:S(2)}, u32[]{:S(2)}) collective-permute-start(bf16[2,64,1024]{2,1,0:T(8,128)(2,1)} %get-tuple-element.44), channel_id=1, source_target_pairs={{0,2},{2,4},{3,1},{4,6},{5,3},{6,8},{7,5},{8,10},{9,7},{10,12},{11... | collective-permute-start | bytes 786440 | tf_op jit(solution)/shard_map/ppermute | solution.py:876
  17.2 1.2 %copy-start.3 = (bf16[512,1024]{1,0:T(8,128)(2,1)S(1)}, bf16[512,1024]{1,0:T(8,128)(2,1)}, u32[]{:S(2)}) copy-start(bf16[512,1024]{1,0:T(8,128)(2,1)} %refs_3_.3) | copy-start | bytes 3145732
  18.4 12.3 %copy-start.9 = (bf16[64,256]{1,0:T(8,128)(2,1)S(1)}, bf16[64,256]{1,0:T(8,128)(2,1)}, u32[]{:S(2)}) copy-start(bf16[64,256]{1,0:T(8,128)(2,1)} %constant.14.clone.pool_ref) | copy-start | bytes 98308
  27.3 5.7 %copy-start.4 = (bf16[512,1024]{1,0:T(8,128)(2,1)S(1)}, bf16[512,1024]{1,0:T(8,128)(2,1)}, u32[]{:S(2)}) copy-start(bf16[512,1024]{1,0:T(8,128)(2,1)} %refs_3_.3) | copy-start | bytes 3145732
  27.3 5.7 %copy-start.5 = (bf16[256,128]{1,0:T(8,128)(2,1)S(1)}, bf16[256,128]{1,0:T(8,128)(2,1)}, u32[]{:S(2)}) copy-start(bf16[256,128]{1,0:T(8,128)(2,1)} %constant.15.clone.near_t_ref.refs_0_) | copy-start | bytes 196612
  31.0 2.0 %collective-permute-start.3 = (bf16[2,128,1024]{2,1,0:T(8,128)(2,1)S(1)}, bf16[2,128,1024]{2,1,0:T(8,128)(2,1)S(1)}, u32[]{:S(2)}, u32[]{:S(2)}) collective-permute-start(bf16[2,128,1024]{2,1,0:T(8,128)(2,1)S(1)} %far.1), channel_id=1, source_target_pairs={{0,1},{1,0},{2,3},{3,2},{4,5},{5,4},{6,7},{7,6},{8,9},{9,8},{10,11... | collective-permute-start | bytes 1572872 | tf_op jit(solution)/shard_map/ppermute | solution.py:882
  33.0 11.3 %copy-start.6 = (bf16[256,64]{1,0:T(8,128)(2,1)S(1)}, bf16[256,64]{1,0:T(8,128)(2,1)}, u32[]{:S(2)}) copy-start(bf16[256,64]{1,0:T(8,128)(2,1)} %constant.16.clone.pool_ref) | copy-start | bytes 98308
  42.3 12.4 %copy-start.8 = (bf16[128,128]{1,0:T(8,128)(2,1)S(1)}, bf16[128,128]{1,0:T(8,128)(2,1)}, u32[]{:S(2)}) copy-start(bf16[128,128]{1,0:T(8,128)(2,1)} %constant.17.clone.refs_1_) | copy-start | bytes 98308
  42.4 1.9 %collective-permute-start.4 = (bf16[2,128,1024]{2,1,0:T(8,128)(2,1)S(1)}, bf16[2,128,1024]{2,1,0:T(8,128)(2,1)S(1)}, u32[]{:S(2)}, u32[]{:S(2)}) collective-permute-start(bf16[2,128,1024]{2,1,0:T(8,128)(2,1)S(1)} %get-tuple-element.60), channel_id=1, source_target_pairs={{0,1},{1,0},{2,3},{3,2},{4,5},{5,4},{6,7},{7,6},{8,9},{9,8},{10,11... | collective-permute-start | bytes 1572872 | tf_op jit(solution)/shard_map/ppermute | solution.py:886
  44.7 15.0 %collective-permute-start.5 = (bf16[2,64,1024]{2,1,0:T(8,128)(2,1)S(1)}, bf16[2,64,1024]{2,1,0:T(8,128)(2,1)S(1)}, u32[]{:S(2)}, u32[]{:S(2)}) collective-permute-start(bf16[2,64,1024]{2,1,0:T(8,128)(2,1)S(1)} %get-tuple-element.64), channel_id=1, source_target_pairs={{1,3},{2,0},{3,5},{4,2},{5,7},{6,4},{7,9},{8,6},{9,11},{10,8},{11,... | collective-permute-start | bytes 786440 | tf_op jit(solution)/shard_map/ppermute | solution.py:889
  52.6 20.3 %collective-permute-start.6 = (bf16[2,256,1024]{2,1,0:T(8,128)(2,1)S(1)}, bf16[2,256,1024]{2,1,0:T(8,128)(2,1)S(1)}, u32[]{:S(2)}, u32[]{:S(2)}) collective-permute-start(bf16[2,256,1024]{2,1,0:T(8,128)(2,1)S(1)} %get-tuple-element.70), channel_id=1, source_target_pairs={{1,2},{2,1},{3,4},{4,3},{5,6},{6,5},{7,8},{8,7},{9,10},{10,9},{11,... | collective-permute-start | bytes 3145736 | tf_op jit(solution)/shard_map/ppermute | solution.py:888
  59.7 5.4 %collective-permute-start.8 = (bf16[2,256,512]{2,1,0:T(8,128)(2,1)S(1)}, bf16[2,256,512]{2,1,0:T(8,128)(2,1)S(1)}, u32[]{:S(2)}, u32[]{:S(2)}) collective-permute-start(bf16[2,256,512]{2,1,0:T(8,128)(2,1)S(1)} %get-tuple-element.75), channel_id=1, source_target_pairs={{0,1},{1,0},{2,3},{3,2},{4,5},{5,4},{6,7},{7,6},{8,9},{9,8},{10,11... | collective-permute-start | bytes 1572872 | tf_op jit(solution)/shard_map/ppermute | solution.py:896
  64.6 9.9 %collective-permute-start.7 = (bf16[2,256,512]{2,1,0:T(8,128)(2,1)S(1)}, bf16[2,256,512]{2,1,0:T(8,128)(2,1)S(1)}, u32[]{:S(2)}, u32[]{:S(2)}) collective-permute-start(bf16[2,256,512]{2,1,0:T(8,128)(2,1)S(1)} %get-tuple-element.71), channel_id=1, source_target_pairs={{0,1},{1,0},{2,3},{3,2},{4,5},{5,4},{6,7},{7,6},{8,9},{9,8},{10,11... | collective-permute-start | bytes 1572872 | tf_op jit(solution)/shard_map/ppermute | solution.py:896
